TPU v7x, 32 devices: a whole 2x2x4 slice. The times are simulated.
32 devices in a mesh: fsdp: 4 (over y, core), ctx: 4 (over z), tp: 2 (over x).
Axes of the slice: x: 2, y: 2, z: 4, core: 2. Of those that a mesh axis runs over, the one named last changes fastest.
Arguments:
- tokens: bfloat16 [8, 2048, 960], P('fsdp', ('ctx', 'tp')), may hold values from -6 to 6
- cotangent: bfloat16 [8, 2048, 960], P('fsdp', ('ctx', 'tp')), may hold values from -6 to 6
- input_gain: bfloat16 [960], P('fsdp'), may hold values from 0.099609375 to 1.8984375
- w_query: bfloat16 [960, 960], P('fsdp'), may hold values from -0.1875 to 0.1875
- w_keyval: bfloat16 [960, 640], P('fsdp'), may hold values from -0.1875 to 0.1875
- w_output: bfloat16 [960, 960], P('fsdp'), may hold values from -2 to 2
- middle_gain: bfloat16 [960], P('fsdp'), may hold values from 0.099609375 to 1.8984375
- w_gate: bfloat16 [960, 2560], P('fsdp', 'tp'), may hold values from -0.1875 to 0.1875
- w_up: bfloat16 [960, 2560], P('fsdp', 'tp'), may hold values from -0.1875 to 0.1875
- w_down: bfloat16 [960, 2560], P('fsdp', 'tp'), may hold values from -0.25 to 0.25
Outputs:
- result: bfloat16 [8, 2048, 960], P('fsdp', ('ctx', 'tp'))
- grad_tokens: float32 [8, 2048, 960], P('fsdp', ('ctx', 'tp'))
- grad_input_gain: float32 [960], P('fsdp')
- grad_w_query: float32 [960, 960], P('fsdp')
- grad_w_keyval: float32 [960, 640], P('fsdp')
- grad_w_output: float32 [960, 960], P('fsdp')
- grad_middle_gain: float32 [960], P('fsdp')
- grad_w_gate: float32 [960, 2560], P('fsdp', 'tp')
- grad_w_up: float32 [960, 2560], P('fsdp', 'tp')
- grad_w_down: float32 [960, 2560], P('fsdp', 'tp')
All inputs are finite; a program needn't handle non-finite values.
Results may differ from a plain program's by a relative error of at most 0.02.
Values may be sent and summed in bfloat16 or wider, within the bound.
A program may use at most 128 MiB of HBM per device.

v0:
```python
import jax
import jax.numpy as jnp
from jax import lax
from jax.experimental import pallas as pl
from jax.experimental.pallas import tpu as pltpu
from jax.sharding import PartitionSpec as P

QUERY_HEADS = 15
KEYVAL_HEADS = 5
GROUP = QUERY_HEADS // KEYVAL_HEADS
HEAD_WIDTH = 64
HALF = HEAD_WIDTH // 2
KEY_WIDTH = 320
QUERY_WIDTH = QUERY_HEADS * HEAD_WIDTH
SCALE = HEAD_WIDTH ** (-0.5)

EPS = 1e-05
THETA = 10000.0
VMEM_LIMIT = 40 * 1024 * 1024


def dot(left, right, left_dim, right_dim):
    return lax.dot_general(
        left, right, (((left_dim,), (right_dim,)), ((), ())), preferred_element_type=jnp.float32
    )


def rope_tables(token_positions, first_place):
    position = (first_place + lax.iota(jnp.int32, token_positions)).astype(jnp.float32)
    frequency = THETA ** (-(2.0 * lax.iota(jnp.int32, HALF).astype(jnp.float32)) / HEAD_WIDTH)
    angles = frequency[:, None] * position[None, :]
    return (jnp.cos(angles), jnp.sin(angles))


def apply_rotary(rows, cosine, sine):
    shaped = rows.reshape(-1, 2, HALF, rows.shape[-1])
    leading = shaped[:, 0]
    trailing = shaped[:, 1]
    return jnp.stack(
        [leading * cosine - trailing * sine, trailing * cosine + leading * sine], 1
    ).reshape(rows.shape)


def normalize(value_rows):
    inverse_rms = lax.rsqrt(jnp.mean(value_rows * value_rows, -1, keepdims=True) + EPS)
    return (value_rows * inverse_rms, inverse_rms)


def norm_back(back_unit, unit_rows, inverse_rms):
    return inverse_rms * (
        back_unit - unit_rows * jnp.mean(back_unit * unit_rows, -1, keepdims=True)
    )


def causal(scores):
    key_place = lax.broadcasted_iota(jnp.int32, scores.shape, 0)
    query_place = lax.broadcasted_iota(jnp.int32, scores.shape, 1)
    return jnp.where(key_place <= query_place, scores, -jnp.inf)


def forward_kernel(query_ref, key_ref, value_ref, mixed_ref, lse_ref):
    place = lax.axis_index("ctx")
    queries = [query_ref[g] * jnp.bfloat16(SCALE) for g in range(GROUP)]

    def scores_of(keys_turned, g, masked):
        scores = dot(keys_turned, queries[g], 1, 0)
        return causal(scores) if masked else scores

    def first():
        keys_turned = key_ref[0, 0, 0].T
        values = value_ref[0, 0, 0]
        carried = []
        for g in range(GROUP):
            scores = scores_of(keys_turned, g, True)
            top = jnp.max(scores, 0, keepdims=True)
            lifted = jnp.exp(scores - top)
            total = jnp.sum(lifted, 0, keepdims=True)
            carried += [top, total, dot(values, lifted.astype(jnp.bfloat16), 1, 0)]
        return tuple(carried)

    def step(block, carried):
        keys_turned = key_ref[block, 0, 0].T
        values = value_ref[block, 0, 0]
        later = []
        for g in range(GROUP):
            top, total, mixed = carried[3 * g : 3 * g + 3]
            scores = scores_of(keys_turned, g, False)
            new_top = jnp.maximum(top, jnp.max(scores, 0, keepdims=True))
            lifted = jnp.exp(scores - new_top)
            shrink = jnp.exp(top - new_top)
            later += [
                new_top,
                total * shrink + jnp.sum(lifted, 0, keepdims=True),
                mixed * shrink + dot(values, lifted.astype(jnp.bfloat16), 1, 0),
            ]
        return tuple(later)

    carried = lax.fori_loop(1, place + 1, step, first())
    for g in range(GROUP):
        top, total, mixed = carried[3 * g : 3 * g + 3]
        mixed_ref[g] = (mixed / total).astype(jnp.bfloat16)
        lse_ref[g] = top + jnp.log(total)


def attend_forward(query, keyval):
    blocks, token_positions = keyval.shape[0], keyval.shape[-1]
    head_block = (GROUP, HEAD_WIDTH, token_positions)
    key_block = (blocks, 1, 1, HEAD_WIDTH, token_positions)
    area = QUERY_HEADS * token_positions * token_positions * blocks
    return pl.pallas_call(
        forward_kernel,
        grid=(KEYVAL_HEADS,),
        in_specs=[
            pl.BlockSpec(head_block, lambda j: (j, 0, 0)),
            pl.BlockSpec(key_block, lambda j: (0, 0, j, 0, 0)),
            pl.BlockSpec(key_block, lambda j: (0, 1, j, 0, 0)),
        ],
        out_specs=[
            pl.BlockSpec(head_block, lambda j: (j, 0, 0)),
            pl.BlockSpec((GROUP, 1, token_positions), lambda j: (j, 0, 0)),
        ],
        out_shape=[
            jax.ShapeDtypeStruct(query.shape, jnp.bfloat16),
            jax.ShapeDtypeStruct((QUERY_HEADS, 1, token_positions), jnp.float32),
        ],
        compiler_params=pltpu.CompilerParams(vmem_limit_bytes=VMEM_LIMIT),
        cost_estimate=pl.CostEstimate(
            flops=16 * HEAD_WIDTH * area, bytes_accessed=6 * query.size, transcendentals=area
        ),
        name="attend_forward",
    )(query, keyval, keyval)


def backward_kernel(
    query_ref, key_ref, value_ref, back_ref, mixed_ref, lse_ref, cosine_ref, sine_ref,
    back_query_ref, back_keyval_ref,
):
    place = lax.axis_index("ctx")
    blocks = key_ref.shape[0]
    queries = [query_ref[g] * jnp.bfloat16(SCALE) for g in range(GROUP)]
    backs = [back_ref[g] for g in range(GROUP)]
    tops = [lse_ref[g] for g in range(GROUP)]
    sums = [
        jnp.sum(backs[g].astype(jnp.float32) * mixed_ref[g].astype(jnp.float32), 0, keepdims=True)
        for g in range(GROUP)
    ]

    def step(block, carried, masked=False):
        keys = key_ref[block, 0, 0]
        keys_turned = keys.T
        values_turned = value_ref[block, 0, 0].T
        back_key = jnp.zeros(keys.shape, jnp.float32)
        back_value = jnp.zeros(keys.shape, jnp.float32)
        later = []
        for g in range(GROUP):
            scores = dot(keys_turned, queries[g], 1, 0)
            if masked:
                scores = causal(scores)
            weights = jnp.exp(scores - tops[g])
            back_weights = dot(values_turned, backs[g], 1, 0)
            back_scores = (weights * (back_weights - sums[g])).astype(jnp.bfloat16)
            later.append(carried[g] + dot(keys, back_scores, 1, 0))
            back_key += dot(queries[g], back_scores, 1, 1)
            back_value += dot(backs[g], weights.astype(jnp.bfloat16), 1, 1)
        back_keyval_ref[block, 0, 0] = back_key.astype(jnp.bfloat16)
        back_keyval_ref[block, 1, 0] = back_value.astype(jnp.bfloat16)
        return tuple(later)

    start = tuple(jnp.zeros(query_ref.shape[1:], jnp.float32) for g in range(GROUP))
    carried = lax.fori_loop(1, place + 1, step, step(0, start, True))

    def clear(block, unused):
        zero = jnp.zeros(key_ref.shape[3:], jnp.bfloat16)
        back_keyval_ref[block, 0, 0] = zero
        back_keyval_ref[block, 1, 0] = zero
        return unused

    lax.fori_loop(place + 1, blocks, clear, 0)
    cosine = cosine_ref[...]
    sine = sine_ref[...]
    for g in range(GROUP):
        leading = carried[g][:HALF] * SCALE
        trailing = carried[g][HALF:] * SCALE
        back_query_ref[g, :HALF] = (leading * cosine + trailing * sine).astype(jnp.bfloat16)
        back_query_ref[g, HALF:] = (trailing * cosine - leading * sine).astype(jnp.bfloat16)


def attend_backward(query, keyval, back_mixed, mixed, lse, cosine, sine, first, count):
    blocks, token_positions = keyval.shape[0], keyval.shape[-1]
    head_block = (GROUP, HEAD_WIDTH, token_positions)
    key_block = (blocks, 1, 1, HEAD_WIDTH, token_positions)
    area = count * GROUP * token_positions * token_positions * blocks
    heads = pl.BlockSpec(head_block, lambda j: (j + first, 0, 0))
    table = pl.BlockSpec((HALF, token_positions), lambda j: (0, 0))
    return pl.pallas_call(
        backward_kernel,
        grid=(count,),
        in_specs=[
            heads,
            pl.BlockSpec(key_block, lambda j: (0, 0, j + first, 0, 0)),
            pl.BlockSpec(key_block, lambda j: (0, 1, j + first, 0, 0)),
            heads,
            heads,
            pl.BlockSpec((GROUP, 1, token_positions), lambda j: (j + first, 0, 0)),
            table,
            table,
        ],
        out_specs=[
            pl.BlockSpec(head_block, lambda j: (j, 0, 0)),
            pl.BlockSpec((blocks, 2, 1, HEAD_WIDTH, token_positions), lambda j: (0, 0, j, 0, 0)),
        ],
        out_shape=[
            jax.ShapeDtypeStruct((count * GROUP, HEAD_WIDTH, token_positions), jnp.bfloat16),
            jax.ShapeDtypeStruct(
                (blocks, 2, count, HEAD_WIDTH, token_positions), jnp.bfloat16
            ),
        ],
        compiler_params=pltpu.CompilerParams(vmem_limit_bytes=VMEM_LIMIT),
        cost_estimate=pl.CostEstimate(
            flops=40 * HEAD_WIDTH * area, bytes_accessed=10 * query.size, transcendentals=area
        ),
        name="attend_backward",
    )(query, keyval, keyval, back_mixed, mixed, lse, cosine, sine)


def move_along(value, distance):
    blocks = lax.axis_size("ctx")
    pairs = [(i, i + distance) for i in range(blocks) if 0 <= i + distance < blocks]
    return lax.ppermute(value, "ctx", pairs)


def trade(value, axis, step):
    pairs = [(i, i ^ step) for i in range(lax.axis_size(axis))]
    return lax.ppermute(value, axis, pairs)


def add_low(left, right):
    return (left.astype(jnp.float32) + right.astype(jnp.float32)).astype(jnp.bfloat16)


def scatter_sum(value, axis):
    size = lax.axis_size(axis)
    index = lax.axis_index(axis)
    rows = value.shape[0] // size
    step = 1
    while step < size:
        count = value.shape[0] // (2 * rows)
        split = value.reshape(count, 2, rows, value.shape[-1])
        second = (index // step) % 2 == 1
        kept = jnp.where(second, split[:, 1], split[:, 0])
        sent = jnp.where(second, split[:, 0], split[:, 1])
        value = add_low(kept, trade(sent, axis, step)).reshape(count * rows, value.shape[-1])
        step *= 2
    return value


def whole_sum(value, others):
    half_rows = value.shape[0] // 2
    second = lax.axis_index("ctx") % 2 == 1
    upper, lower = value[:half_rows], value[half_rows:]
    received = trade(jnp.where(second, upper, lower), "ctx", 1)
    total = add_low(jnp.where(second, lower, upper), received)
    for axis, first_step in others:
        step = first_step
        while step < lax.axis_size(axis):
            total = add_low(total, trade(total, axis, step))
            step *= 2
    received = trade(total, "ctx", 1)
    return jnp.concatenate(
        [jnp.where(second, received, total), jnp.where(second, total, received)], 0
    ).astype(jnp.float32)


def on_device(
    tokens, cotangent, input_gain, w_query, w_keyval, w_output, middle_gain, w_gate, w_up, w_down
):
    half = lax.axis_index("tp")
    low_half = half == 0
    pair = [(0, 1), (1, 0)]

    def to_partner(value_rows):
        return lax.ppermute(value_rows, "tp", pair)

    def in_order(mine, received):
        return jnp.concatenate(
            [jnp.where(low_half, mine, received), jnp.where(low_half, received, mine)], 0
        )

    def take(value_rows, index):
        return lax.dynamic_index_in_dim(value_rows, index, 0, keepdims=False)

    tokens_own = in_order(take(tokens, half), to_partner(take(tokens, 1 - half)))
    full_gain_one, full_gain_two = (
        lax.all_gather(input_gain, "fsdp", axis=0, tiled=True),
        lax.all_gather(middle_gain, "fsdp", axis=0, tiled=True),
    )
    full_in = lax.all_gather(jnp.concatenate([w_query, w_keyval], 1), "fsdp", axis=0, tiled=True)
    full_output = lax.all_gather(w_output, "fsdp", axis=0, tiled=True)
    full_gate = lax.all_gather(w_gate, "fsdp", axis=0, tiled=True)
    full_up = lax.all_gather(w_up, "fsdp", axis=0, tiled=True)
    full_down = lax.all_gather(w_down, "fsdp", axis=0, tiled=True)
    cotangent_received = to_partner(cotangent)
    cotangent_own = in_order(take(cotangent, half), take(cotangent_received, half))
    cotangent_other = in_order(take(cotangent, 1 - half), take(cotangent_received, 1 - half))

    token_positions = tokens_own.shape[0]
    cosine, sine = rope_tables(token_positions, lax.axis_index("ctx") * token_positions)
    gain_one = full_gain_one.astype(jnp.float32)
    inputs = tokens_own.astype(jnp.float32)
    unit_one, inverse_one = normalize(inputs)
    normed_one = (unit_one * gain_one).astype(jnp.bfloat16)
    keyval_raw = dot(full_in[:, QUERY_WIDTH:], normed_one, 0, 1)
    keyval_low = jnp.concatenate(
        [apply_rotary(keyval_raw[:KEY_WIDTH], cosine, sine), keyval_raw[KEY_WIDTH:]], 0
    ).astype(jnp.bfloat16)
    blocks = lax.axis_size("ctx")
    keyval = jnp.stack([keyval_low] + [move_along(keyval_low, s) for s in range(1, blocks)], 0)
    keyval = keyval.reshape(blocks, 2, KEYVAL_HEADS, HEAD_WIDTH, token_positions)
    query_raw = dot(full_in[:, :QUERY_WIDTH], normed_one, 0, 1)
    query_low = (
        apply_rotary(query_raw, cosine, sine)
        .astype(jnp.bfloat16)
        .reshape(QUERY_HEADS, HEAD_WIDTH, token_positions)
    )
    mixed_heads, lse = attend_forward(query_low, keyval)
    mixed_low = mixed_heads.reshape(QUERY_WIDTH, token_positions)
    middle = inputs + dot(mixed_low, full_output, 0, 0)

    gain_two = full_gain_two.astype(jnp.float32)
    unit_two, inverse_two = normalize(middle)
    normed_two = (unit_two * gain_two).astype(jnp.bfloat16)
    normed_other = to_partner(normed_two)

    def feed(rows, back_rows):
        gate_proj = dot(rows, full_gate, 1, 0)
        up_proj = dot(rows, full_up, 1, 0)
        sigmoid_gate = jax.nn.sigmoid(gate_proj)
        swish_gate = gate_proj * sigmoid_gate
        hidden = (swish_gate * up_proj).astype(jnp.bfloat16)
        back_hidden = dot(back_rows, full_down, 1, 0)
        back_gate = (
            back_hidden * up_proj * sigmoid_gate * (1.0 + gate_proj * (1.0 - sigmoid_gate))
        ).astype(jnp.bfloat16)
        back_up = (back_hidden * swish_gate).astype(jnp.bfloat16)
        return (hidden, back_gate, back_up)

    def feed_input_back(back_gate, back_up):
        return dot(back_gate, full_gate, 1, 1) + dot(back_up, full_up, 1, 1)

    hidden_own, back_gate_own, back_up_own = feed(normed_two, cotangent_own)
    hidden_other, back_gate_other, back_up_other = feed(normed_other, cotangent_other)
    back_two_received = to_partner(
        feed_input_back(back_gate_other, back_up_other).astype(jnp.bfloat16)
    )
    back_two = feed_input_back(back_gate_own, back_up_own) + back_two_received.astype(jnp.float32)
    feed_received = to_partner(dot(hidden_other, full_down, 1, 1).astype(jnp.bfloat16))
    result_own = (
        middle + dot(hidden_own, full_down, 1, 1) + feed_received.astype(jnp.float32)
    ).astype(jnp.bfloat16)

    def feed_gradient(left_own, right_own, left_other, right_other):
        gradient = dot(left_own, right_own, 0, 0) + dot(left_other, right_other, 0, 0)
        shared = scatter_sum(gradient.astype(jnp.bfloat16), "fsdp")
        return whole_sum(shared, (("ctx", 2),))

    share_down = feed_gradient(cotangent_own, hidden_own, cotangent_other, hidden_other)
    share_gate = feed_gradient(normed_two, back_gate_own, normed_other, back_gate_other)
    share_up = feed_gradient(normed_two, back_up_own, normed_other, back_up_other)

    grad_gain_two = jnp.sum(back_two * unit_two, axis=0)
    back_middle = cotangent_own.astype(jnp.float32) + norm_back(
        back_two * gain_two, unit_two, inverse_two
    )
    back_attention = back_middle.astype(jnp.bfloat16)
    back_mixed = dot(full_output, back_attention, 1, 1).astype(jnp.bfloat16)
    back_mixed = back_mixed.reshape(query_low.shape)
    grad_output = dot(mixed_low, back_attention, 1, 0).astype(jnp.bfloat16)
    share_output = whole_sum(scatter_sum(grad_output, "fsdp"), (("tp", 1), ("ctx", 2)))

    back_query = []
    back_key = []
    back_value = []
    for first, count in ((0, 3), (3, 2)):
        part_query, part_keyval = attend_backward(
            query_low, keyval, back_mixed, mixed_heads, lse, cosine, sine, first, count
        )
        part_keyval = part_keyval.reshape(blocks, 2 * count * HEAD_WIDTH, token_positions)
        owned = part_keyval[0].astype(jnp.float32)
        for s in range(1, blocks):
            owned += move_along(part_keyval[s], -s).astype(jnp.float32)
        back_query.append(part_query.reshape(-1, token_positions))
        back_key.append(
            apply_rotary(owned[: count * HEAD_WIDTH], cosine, -sine).astype(jnp.bfloat16)
        )
        back_value.append(owned[count * HEAD_WIDTH :].astype(jnp.bfloat16))
    back_in = jnp.concatenate(back_query + back_key + back_value, 0)
    grad_in = dot(normed_one, back_in, 0, 1)
    back_one = dot(back_in, full_in, 0, 1)
    grad_gain_one = jnp.sum(back_one * unit_one, axis=0)
    back_inputs = back_middle + norm_back(back_one * gain_one, unit_one, inverse_one)

    def to_positions(value_rows):
        split = value_rows.reshape(2, token_positions // 2, value_rows.shape[-1])
        received = to_partner(take(split, 1 - half))
        return in_order(take(split, half)[None], received[None])

    result = to_positions(result_own)
    grad_tokens = to_positions(back_inputs.astype(jnp.bfloat16)).astype(jnp.float32)
    gradients = jnp.concatenate([grad_in, grad_gain_one[:, None], grad_gain_two[:, None]], 1)
    share_in = lax.psum(
        lax.psum_scatter(
            gradients.astype(jnp.bfloat16), "fsdp", scatter_dimension=0, tiled=True
        ),
        ("ctx", "tp"),
    ).astype(jnp.float32)
    width = full_in.shape[1]
    return (
        result,
        grad_tokens,
        share_in[:, width],
        share_in[:, :QUERY_WIDTH],
        share_in[:, QUERY_WIDTH:width],
        share_output,
        share_in[:, width + 1],
        share_gate,
        share_up,
        share_down,
    )


def solution(mesh):
    rows = P("fsdp", ("ctx", "tp"), None)
    specs = (
        P("fsdp"), P("fsdp", None), P("fsdp", None), P("fsdp", None),
        P("fsdp"), P("fsdp", "tp"), P("fsdp", "tp"), P("fsdp", "tp"),
    )
    return jax.shard_map(
        on_device,
        mesh=mesh,
        in_specs=(rows, rows) + specs,
        out_specs=(rows, rows) + specs,
        check_vma=False,
    )
```

profile of v0, /device:TPU:0, one launch (start us, length us, event | category | flops | bytes accessed | tf_op | source)
XLA Modules:
  0.0 522.0 jit_solution(15918234388384990716)
XLA Ops:
  16.7 6.9 %all-reduce.2 = (bf16[960]{0:T(1024)(128)(2,1)S(1)}, bf16[960]{0:T(1024)(128)(2,1)S(1)}) all-reduce(bf16[960]{0:T(1024)(128)(2,1)S(1)} %dynamic-update-slice, bf16[960]{0:T(1024)(128)(2,1)S(1)} %dynamic-update-slice.1), channel_id=1, replica_groups=mesh['fsdp'=4,'ctx'=4,'tp'=2] {'fsdp'}, use_global_device_ids=true, to_apply=%add | all-reduce | flops 1920 | bytes 7680
  28.3 18.8 %collective-permute-done.7 = bf16[2,256,960]{1,2,0:T(8,128)(2,1)} collective-permute-done((bf16[2,256,960]{1,2,0:T(8,128)(2,1)S(1)}, bf16[2,256,960]{1,2,0:T(8,128)(2,1)}, u32[]{:S(2)}, u32[]{:S(2)}) %collective-permute-start.7) | collective-permute-done | bytes 983072 | tf_op jit(solution)/shard_map/ppermute | solution.py:282
  53.0 5.9 %collective-permute-start.3 = (bf16[640,512]{1,0:T(8,128)(2,1)S(1)}, bf16[640,512]{1,0:T(8,128)(2,1)S(1)}, u32[]{:S(2)}, u32[]{:S(2)}) collective-permute-start(bf16[640,512]{1,0:T(8,128)(2,1)S(1)} %pad_maximum_fusion.8), channel_id=1, source_target_pairs={{0,6},{1,7},{8,14},{9,15},{16,22},{17,23},{24,30},{25,31}} | collective-permute-start | bytes 1966088 | tf_op jit(solution)/shard_map/ppermute | solution.py:229
  64.6 9.5 %collective-permute-done.3 = bf16[640,512]{1,0:T(8,128)(2,1)S(1)} collective-permute-done((bf16[640,512]{1,0:T(8,128)(2,1)S(1)}, bf16[640,512]{1,0:T(8,128)(2,1)S(1)}, u32[]{:S(2)}, u32[]{:S(2)}) %collective-permute-start.3) | collective-permute-done | bytes 655392 | tf_op jit(solution)/shard_map/ppermute | solution.py:229
  74.1 14.0 %collective-permute-done.2 = bf16[640,512]{1,0:T(8,128)(2,1)S(1)} collective-permute-done((bf16[640,512]{1,0:T(8,128)(2,1)S(1)}, bf16[640,512]{1,0:T(8,128)(2,1)S(1)}, u32[]{:S(2)}, u32[]{:S(2)}) %collective-permute-start.2) | collective-permute-done | bytes 655392 | tf_op jit(solution)/shard_map/ppermute | solution.py:229
  88.1 12.0 %collective-permute-done.1 = bf16[640,512]{1,0:T(8,128)(2,1)S(1)} collective-permute-done((bf16[640,512]{1,0:T(8,128)(2,1)S(1)}, bf16[640,512]{1,0:T(8,128)(2,1)S(1)}, u32[]{:S(2)}, u32[]{:S(2)}) %collective-permute-start.1) | collective-permute-done | bytes 655392 | tf_op jit(solution)/shard_map/ppermute | solution.py:229
  100.5 7.4 %attend_forward.1 = (bf16[15,64,512]{2,1,0:T(8,128)(2,1)S(1)}, f32[15,1,512]{2,1,0:T(1,128)S(1)}) custom-call(bf16[15,64,512]{2,1,0:T(8,128)(2,1)S(1)} %bitcast.222, bf16[4,2,5,64,512]{4,3,2,1,0:T(8,128)(2,1)S(1)} %pad_maximum_fusion.key_ref.value_ref, bf16[4,2,5,64,512]{4,3,2,1,0:T(8,128)(2,1)S(1)} %pad_maximum_fusion.key_ref.value_ref), custom_call_target="tpu_custom_call" | custom-call | flops 16106127360 | bytes 2949120 | tf_op jit(solution)/shard_map/attend_forward/pallas_call | solution.py:110
  126.2 17.3 %all-gather.14.cloned.1.call-done = bf16[960,1280]{1,0:T(8,128)(2,1)} async-done(((bf16[240,1280]{1,0:T(8,128)(2,1)}), bf16[960,1280]{1,0:T(8,128)(2,1)}) %all-gather.14.cloned.1.call-update) | async-done | bytes 2457616 | tf_op jit(solution)/shard_map/all_gather | solution.py:301
  143.6 5.9 %multiply_convert_fusion.2 = (bf16[512,1280]{1,0:T(8,128)(2,1)S(1)}, bf16[512,1280]{1,0:T(8,128)(2,1)S(1)}, bf16[512,1280]{1,0:T(8,128)(2,1)S(1)}) fusion(f32[512,1280]{1,0:T(8,128)} %fusion.55, f32[512,1280]{1,0:T(8,128)} %fusion.56, bf16[960,1280]{1,0:T(8,128)(2,1)} %all-gather.14.cloned.1.call-done, bf16[256,960]{0,1:T(8,128)(2,1)} %get-tuple-element.39, ...), kind=kOutput, calls=%fused_computation.14 | convolution fusion | flops 1270087680 | bytes 12615680 | tf_op jit(solution)/shard_map/dot_general | solution.py:23
  188.3 8.0 %collective-permute-done.8 = bf16[512,960]{0,1:T(8,128)(2,1)S(1)} collective-permute-done((bf16[512,960]{0,1:T(8,128)(2,1)S(1)}, bf16[512,960]{0,1:T(8,128)(2,1)S(1)}, u32[]{:S(2)}, u32[]{:S(2)}) %collective-permute-start.8) | collective-permute-done | bytes 983072 | tf_op jit(solution)/shard_map/ppermute | solution.py:282
  202.0 8.4 %attend_backward.2 = (bf16[9,64,512]{2,1,0:T(8,128)(2,1)S(1)}, bf16[4,2,3,64,512]{4,3,2,1,0:T(8,128)(2,1)S(1)}) custom-call(bf16[15,64,512]{2,1,0:T(8,128)(2,1)S(1)} %bitcast.223, bf16[4,2,5,64,512]{4,3,2,1,0:T(8,128)(2,1)S(1)} %pad_maximum_fusion.key_ref.value_ref, bf16[4,2,5,64,512]{4,3,2,1,0:T(8,128)(2,1)S(1)} %pad_maximum_fusion.key_ref.value_ref, ...), custom_call_target="tpu_custom_call" | custom-call | flops 24159191040 | bytes 4915200 | tf_op jit(solution)/shard_map/attend_backward/pallas_call | solution.py:195
  244.9 49.7 %collective-permute-done.14 = bf16[256,512]{1,0:T(8,128)(2,1)S(1)} collective-permute-done((bf16[256,512]{1,0:T(8,128)(2,1)}, bf16[256,512]{1,0:T(8,128)(2,1)S(1)}, u32[]{:S(2)}, u32[]{:S(2)}) %collective-permute-start.14) | collective-permute-done | bytes 262176 | tf_op jit(solution)/shard_map/ppermute | solution.py:229
  295.9 13.7 %collective-permute-done.13 = bf16[256,512]{1,0:T(8,128)(2,1)S(1)} collective-permute-done((bf16[256,512]{1,0:T(8,128)(2,1)S(1)}, bf16[256,512]{1,0:T(8,128)(2,1)S(1)}, u32[]{:S(2)}, u32[]{:S(2)}) %collective-permute-start.13) | collective-permute-done | bytes 262176 | tf_op jit(solution)/shard_map/ppermute | solution.py:229
  333.0 6.0 %concatenate.61 = bf16[960,1602]{1,0:T(8,128)(2,1)} concatenate(bf16[960,1600]{1,0:T(8,128)(2,1)} %convolution_convert_fusion, bf16[960,1]{1,0:T(8,128)(2,1)S(1)} %broadcast_in_dim.14, bf16[960,1]{1,0:T(8,128)(2,1)S(1)} %broadcast_in_dim.15), dimensions={1} | concatenate | bytes 6151680 | tf_op jit(solution)/shard_map/concatenate | solution.py:409
  342.0 7.9 %collective-permute-start.24 = (bf16[120,1280]{1,0:T(8,128)(2,1)S(1)}, bf16[120,1280]{1,0:T(8,128)(2,1)S(1)}, u32[]{:S(2)}, u32[]{:S(2)}) collective-permute-start(bf16[120,1280]{1,0:T(8,128)(2,1)S(1)} %select_bitcast_fusion.14), channel_id=1, source_target_pairs={{0,2},{2,0},{4,6},{6,4},{1,3},{3,1},{5,7},{7,5},{8,10},{10,8},{12,... | collective-permute-start | bytes 921608 | tf_op jit(solution)/shard_map/ppermute | solution.py:234
  370.4 16.1 %collective-permute-done.17 = bf16[1,240,960]{2,1,0:T(8,128)(2,1)S(1)} collective-permute-done((bf16[1,240,960]{2,1,0:T(8,128)(2,1)S(1)}, bf16[1,240,960]{2,1,0:T(8,128)(2,1)S(1)}, u32[]{:S(2)}, u32[]{:S(2)}) %collective-permute-start.17) | collective-permute-done | bytes 460832 | tf_op jit(solution)/shard_map/ppermute | solution.py:234
  386.8 7.3 %collective-permute-done.25 = bf16[120,1280]{1,0:T(8,128)(2,1)S(1)} collective-permute-done((bf16[120,1280]{1,0:T(8,128)(2,1)S(1)}, bf16[120,1280]{1,0:T(8,128)(2,1)S(1)}, u32[]{:S(2)}, u32[]{:S(2)}) %collective-permute-start.25) | collective-permute-done | bytes 307232 | tf_op jit(solution)/shard_map/ppermute | solution.py:234
  394.3 6.4 %collective-permute-done.30 = bf16[120,1280]{1,0:T(8,128)(2,1)S(1)} collective-permute-done((bf16[120,1280]{1,0:T(8,128)(2,1)S(1)}, bf16[120,1280]{1,0:T(8,128)(2,1)S(1)}, u32[]{:S(2)}, u32[]{:S(2)}) %collective-permute-start.30) | collective-permute-done | bytes 307232 | tf_op jit(solution)/shard_map/ppermute | solution.py:234
  412.2 5.9 %collective-permute-done.26 = bf16[120,1280]{1,0:T(8,128)(2,1)S(1)} collective-permute-done((bf16[120,1280]{1,0:T(8,128)(2,1)S(1)}, bf16[120,1280]{1,0:T(8,128)(2,1)S(1)}, u32[]{:S(2)}, u32[]{:S(2)}) %collective-permute-start.26) | collective-permute-done | bytes 307232 | tf_op jit(solution)/shard_map/ppermute | solution.py:234
  418.2 6.5 %collective-permute-done.31 = bf16[120,1280]{1,0:T(8,128)(2,1)S(1)} collective-permute-done((bf16[120,1280]{1,0:T(8,128)(2,1)S(1)}, bf16[120,1280]{1,0:T(8,128)(2,1)S(1)}, u32[]{:S(2)}, u32[]{:S(2)}) %collective-permute-start.31) | collective-permute-done | bytes 307232 | tf_op jit(solution)/shard_map/ppermute | solution.py:234
  424.7 6.1 %collective-permute-done.36 = bf16[120,1280]{1,0:T(8,128)(2,1)S(1)} collective-permute-done((bf16[120,1280]{1,0:T(8,128)(2,1)S(1)}, bf16[120,1280]{1,0:T(8,128)(2,1)S(1)}, u32[]{:S(2)}, u32[]{:S(2)}) %collective-permute-start.36) | collective-permute-done | bytes 307232 | tf_op jit(solution)/shard_map/ppermute | solution.py:234
  433.3 19.9 %collective-permute-done.20 = bf16[120,960]{1,0:T(8,128)(2,1)S(1)} collective-permute-done((bf16[120,960]{1,0:T(8,128)(2,1)S(1)}, bf16[120,960]{1,0:T(8,128)(2,1)S(1)}, u32[]{:S(2)}, u32[]{:S(2)}) %collective-permute-start.20) | collective-permute-done | bytes 230432 | tf_op jit(solution)/shard_map/ppermute | solution.py:234
  454.5 6.4 %collective-permute-done.21 = bf16[120,960]{1,0:T(8,128)(2,1)S(1)} collective-permute-done((bf16[120,960]{1,0:T(8,128)(2,1)S(1)}, bf16[120,960]{1,0:T(8,128)(2,1)S(1)}, u32[]{:S(2)}, u32[]{:S(2)}) %collective-permute-start.21) | collective-permute-done | bytes 230432 | tf_op jit(solution)/shard_map/ppermute | solution.py:234
  462.0 48.8 %all-reduce.5.cloned.1.call-done = bf16[240,1602]{1,0:T(8,128)(2,1)} async-done(((bf16[240,1602]{1,0:T(8,128)(2,1)}), bf16[240,1602]{1,0:T(8,128)(2,1)}) %all-reduce.5.cloned.1.call-update) | async-done | bytes 768976 | tf_op jit(solution)/shard_map/psum | solution.py:410
  (311 shorter events, 190.8 us)
Async XLA Ops:
  7.2 42.4 %all-gather.6.cloned.1.call-start = ((), (), s32[]{:S(2)}) async-start(), calls=%async_computation.1 | async-start | bytes 3993600 | tf_op jit(solution)/shard_map/all_gather | solution.py:297
  9.5 99.3 %all-gather.8.cloned.1.call-start = ((), (), s32[]{:S(2)}) async-start(), calls=%async_computation.2 | async-start | bytes 2457600 | tf_op jit(solution)/shard_map/all_gather | solution.py:298
  10.3 105.7 %all-gather.10.cloned.1.call-start = ((), (), s32[]{:S(2)}) async-start(), calls=%async_computation.3 | async-start | bytes 3072000 | tf_op jit(solution)/shard_map/all_gather | solution.py:299
  11.0 110.1 %all-gather.12.cloned.1.call-start = ((), (), s32[]{:S(2)}) async-start(), calls=%async_computation.4 | async-start | bytes 3072000 | tf_op jit(solution)/shard_map/all_gather | solution.py:300
  11.6 132.0 %all-gather.14.cloned.1.call-start = ((), (), s32[]{:S(2)}) async-start(), calls=%async_computation.5 | async-start | bytes 3072000 | tf_op jit(solution)/shard_map/all_gather | solution.py:301
  14.7 32.4 %collective-permute-start.7 = (bf16[2,256,960]{1,2,0:T(8,128)(2,1)S(1)}, bf16[2,256,960]{1,2,0:T(8,128)(2,1)}, u32[]{:S(2)}, u32[]{:S(2)}) collective-permute-start(bf16[2,256,960]{1,2,0:T(8,128)(2,1)S(1)} %copy-done.38), channel_id=1, source_target_pairs={{0,1},{1,0},{2,3},{3,2},{4,5},{5,4},{6,7},{7,6},{8,9},{9,8},{10,11... | collective-permute-start | bytes 2949128 | tf_op jit(solution)/shard_map/ppermute | solution.py:282
  14.8 418.4 %reduce-scatter.2.cloned.1.call-start = ((), (), s32[]{:S(2)}) async-start(), calls=%async_computation.6 | async-start | bytes 3993600 | tf_op jit(solution)/shard_map/reduce_scatter | solution.py:411
  60.2 39.9 %collective-permute-start.1 = (bf16[640,512]{1,0:T(8,128)(2,1)S(1)}, bf16[640,512]{1,0:T(8,128)(2,1)S(1)}, u32[]{:S(2)}, u32[]{:S(2)}) collective-permute-start(bf16[640,512]{1,0:T(8,128)(2,1)S(1)} %pad_maximum_fusion.8), channel_id=1, source_target_pairs={{0,2},{2,4},{4,6},{1,3},{3,5},{5,7},{8,10},{10,12},{12,14},{9,11},... | collective-permute-start | bytes 1966088 | tf_op jit(solution)/shard_map/ppermute | solution.py:229
  114.5 43.9 %collective-permute-start.4 = (bf16[512,960]{0,1:T(8,128)(2,1)}, bf16[512,960]{0,1:T(8,128)(2,1)}, u32[]{:S(2)}, u32[]{:S(2)}) collective-permute-start(bf16[512,960]{0,1:T(8,128)(2,1)} %multiply_convert_fusion.6), channel_id=1, source_target_pairs={{0,1},{1,0},{2,3},{3,2},{4,5},{5,4},{6,7},{7,6},{8,9},{9,8},{10,11... | collective-permute-start | bytes 2949128 | tf_op jit(solution)/shard_map/ppermute | solution.py:282
  175.6 46.0 %collective-permute-start.5 = (bf16[512,960]{0,1:T(8,128)(2,1)}, bf16[512,960]{0,1:T(8,128)(2,1)}, u32[]{:S(2)}, u32[]{:S(2)}) collective-permute-start(bf16[512,960]{0,1:T(8,128)(2,1)} %convolution_convert_fusion.3), channel_id=1, source_target_pairs={{0,1},{1,0},{2,3},{3,2},{4,5},{5,4},{6,7},{7,6},{8,9},{9,8},{10,11... | collective-permute-start | bytes 2949128 | tf_op jit(solution)/shard_map/ppermute | solution.py:282
  180.7 51.1 %collective-permute-start.22 = (bf16[2,240,1280]{2,1,0:T(8,128)(2,1)}, bf16[2,240,1280]{2,1,0:T(8,128)(2,1)}, u32[]{:S(2)}, u32[]{:S(2)}) collective-permute-start(bf16[2,240,1280]{2,1,0:T(8,128)(2,1)} %select_bitcast_fusion.2), channel_id=1, source_target_pairs={{0,8},{8,0},{16,24},{24,16},{1,9},{9,1},{17,25},{25,17},{2,10},{10... | collective-permute-start | bytes 3686408 | tf_op jit(solution)/shard_map/ppermute | solution.py:234
  185.2 50.9 %collective-permute-start.27 = (bf16[2,240,1280]{2,1,0:T(8,128)(2,1)}, bf16[2,240,1280]{2,1,0:T(8,128)(2,1)}, u32[]{:S(2)}, u32[]{:S(2)}) collective-permute-start(bf16[2,240,1280]{2,1,0:T(8,128)(2,1)} %select_bitcast_fusion.1), channel_id=1, source_target_pairs={{0,8},{8,0},{16,24},{24,16},{1,9},{9,1},{17,25},{25,17},{2,10},{10... | collective-permute-start | bytes 3686408 | tf_op jit(solution)/shard_map/ppermute | solution.py:234
  188.3 52.5 %collective-permute-start.32 = (bf16[2,240,1280]{2,1,0:T(8,128)(2,1)}, bf16[2,240,1280]{2,1,0:T(8,128)(2,1)}, u32[]{:S(2)}, u32[]{:S(2)}) collective-permute-start(bf16[2,240,1280]{2,1,0:T(8,128)(2,1)} %select_bitcast_fusion), channel_id=1, source_target_pairs={{0,8},{8,0},{16,24},{24,16},{1,9},{9,1},{17,25},{25,17},{2,10},{10... | collective-permute-start | bytes 3686408 | tf_op jit(solution)/shard_map/ppermute | solution.py:234
  219.1 92.2 %collective-permute-start.11 = (bf16[384,512]{1,0:T(8,128)(2,1)}, bf16[384,512]{1,0:T(8,128)(2,1)}, u32[]{:S(2)}, u32[]{:S(2)}) collective-permute-start(bf16[384,512]{1,0:T(8,128)(2,1)} %bitcast.28), channel_id=1, source_target_pairs={{6,0},{7,1},{14,8},{15,9},{22,16},{23,17},{30,24},{31,25}} | collective-permute-start | bytes 1179656 | tf_op jit(solution)/shard_map/ppermute | solution.py:229
  221.6 90.3 %collective-permute-start.10 = (bf16[384,512]{1,0:T(8,128)(2,1)}, bf16[384,512]{1,0:T(8,128)(2,1)}, u32[]{:S(2)}, u32[]{:S(2)}) collective-permute-start(bf16[384,512]{1,0:T(8,128)(2,1)} %bitcast.27), channel_id=1, source_target_pairs={{4,0},{6,2},{5,1},{7,3},{12,8},{14,10},{13,9},{15,11},{20,16},{22,... | collective-permute-start | bytes 1179656 | tf_op jit(solution)/shard_map/ppermute | solution.py:229
  231.8 62.8 %collective-permute-start.14 = (bf16[256,512]{1,0:T(8,128)(2,1)}, bf16[256,512]{1,0:T(8,128)(2,1)S(1)}, u32[]{:S(2)}, u32[]{:S(2)}) collective-permute-start(bf16[256,512]{1,0:T(8,128)(2,1)} %bitcast.255), channel_id=1, source_target_pairs={{6,0},{7,1},{14,8},{15,9},{22,16},{23,17},{30,24},{31,25}} | collective-permute-start | bytes 786440 | tf_op jit(solution)/shard_map/ppermute | solution.py:229
  236.4 73.2 %collective-permute-start.13 = (bf16[256,512]{1,0:T(8,128)(2,1)S(1)}, bf16[256,512]{1,0:T(8,128)(2,1)S(1)}, u32[]{:S(2)}, u32[]{:S(2)}) collective-permute-start(bf16[256,512]{1,0:T(8,128)(2,1)S(1)} %bitcast.254), channel_id=1, source_target_pairs={{4,0},{6,2},{5,1},{7,3},{12,8},{14,10},{13,9},{15,11},{20,16},{22,... | collective-permute-start | bytes 786440 | tf_op jit(solution)/shard_map/ppermute | solution.py:229
  240.8 68.8 %collective-permute-start.12 = (bf16[256,512]{1,0:T(8,128)(2,1)S(1)}, bf16[256,512]{1,0:T(8,128)(2,1)S(1)}, u32[]{:S(2)}, u32[]{:S(2)}) collective-permute-start(bf16[256,512]{1,0:T(8,128)(2,1)S(1)} %bitcast.253), channel_id=1, source_target_pairs={{2,0},{4,2},{6,4},{3,1},{5,3},{7,5},{10,8},{12,10},{14,12},{11,9},... | collective-permute-start | bytes 786440 | tf_op jit(solution)/shard_map/ppermute | solution.py:229
  309.6 50.2 %collective-permute-start.16 = (bf16[2,240,960]{2,1,0:T(8,128)(2,1)}, bf16[2,240,960]{2,1,0:T(8,128)(2,1)}, u32[]{:S(2)}, u32[]{:S(2)}) collective-permute-start(bf16[2,240,960]{2,1,0:T(8,128)(2,1)} %select_bitcast_fusion.3), channel_id=1, source_target_pairs={{0,8},{8,0},{16,24},{24,16},{1,9},{9,1},{17,25},{25,17},{2,10},{10... | collective-permute-start | bytes 2764808 | tf_op jit(solution)/shard_map/ppermute | solution.py:234
  311.4 30.7 %collective-permute-start.28 = (bf16[1,240,1280]{2,1,0:T(8,128)(2,1)}, bf16[1,240,1280]{2,1,0:T(8,128)(2,1)}, u32[]{:S(2)}, u32[]{:S(2)}) collective-permute-start(bf16[1,240,1280]{2,1,0:T(8,128)(2,1)} %select_bitcast_fusion.5), channel_id=1, source_target_pairs={{0,16},{8,24},{16,0},{24,8},{1,17},{9,25},{17,1},{25,9},{2,18},{10... | collective-permute-start | bytes 1843208 | tf_op jit(solution)/shard_map/ppermute | solution.py:234
  312.0 40.5 %collective-permute-start.33 = (bf16[1,240,1280]{2,1,0:T(8,128)(2,1)}, bf16[1,240,1280]{2,1,0:T(8,128)(2,1)}, u32[]{:S(2)}, u32[]{:S(2)}) collective-permute-start(bf16[1,240,1280]{2,1,0:T(8,128)(2,1)} %select_bitcast_fusion.4), channel_id=1, source_target_pairs={{0,16},{8,24},{16,0},{24,8},{1,17},{9,25},{17,1},{25,9},{2,18},{10... | collective-permute-start | bytes 1843208 | tf_op jit(solution)/shard_map/ppermute | solution.py:234
  339.0 171.7 %all-reduce.5.cloned.1.call-start = ((), (), s32[]{:S(2)}) async-start(), calls=%async_computation.7 | async-start | bytes 1597440 | tf_op jit(solution)/shard_map/psum | solution.py:410
  364.4 36.3 %collective-permute-start.30 = (bf16[120,1280]{1,0:T(8,128)(2,1)S(1)}, bf16[120,1280]{1,0:T(8,128)(2,1)S(1)}, u32[]{:S(2)}, u32[]{:S(2)}) collective-permute-start(bf16[120,1280]{1,0:T(8,128)(2,1)S(1)} %fusion.34), channel_id=1, source_target_pairs={{0,4},{2,6},{4,0},{6,2},{1,5},{3,7},{5,1},{7,3},{8,12},{10,14},{12... | collective-permute-start | bytes 921608 | tf_op jit(solution)/shard_map/ppermute | solution.py:234
  369.2 36.9 %collective-permute-start.35 = (bf16[120,1280]{1,0:T(8,128)(2,1)S(1)}, bf16[120,1280]{1,0:T(8,128)(2,1)S(1)}, u32[]{:S(2)}, u32[]{:S(2)}) collective-permute-start(bf16[120,1280]{1,0:T(8,128)(2,1)S(1)} %fusion.33), channel_id=1, source_target_pairs={{0,4},{2,6},{4,0},{6,2},{1,5},{3,7},{5,1},{7,3},{8,12},{10,14},{12... | collective-permute-start | bytes 921608 | tf_op jit(solution)/shard_map/ppermute | solution.py:234
  (75 other events, 1050.0 us)
Sparse Core Ops, SparseCore 0:
  10.2 31.5 all-gather.5
  43.3 21.8 all-gather.7
  66.8 24.6 all-gather.9
  92.8 24.6 all-gather.11
  118.9 24.6 all-gather.13
  339.1 54.0 reduce-scatter.1
  433.4 77.3 all-reduce.4
where the time goes:
time: 530 us; the launch traced here: 522 us
  waiting for transfers between devices  284 us (54%)
  matrix products  68.5 us (13%)
  starting transfers between devices  48 us (9%)
  other arithmetic  42.6 us (8%)
  local copies, waits for them, and re-layouts  34.1 us (6%)
  Pallas kernels  21.2 us (4%)
  between operations  16.3 us (3%)
  blocking collectives  6.88 us (1%)
    ppermute x9, waiting for transfers between devices, move_along(): return lax.ppermute(value, 'ctx', pairs)  99 us
    ppermute x21, waiting for transfers between devices, trade(): return lax.ppermute(value, axis, pairs)  88.1 us
    dot_general x25, matrix products, dot(): lax.dot_general(left, right, (((left_dim,), (right_dim,)), ((), ())), pre...  68.5 us
    psum x1, waiting for transfers between devices, on_device(): lax.psum(lax.psum_scatter(gradients.astype(jnp.bfloat16), 'fsdp', scatter...  48.8 us
    ppermute x7, waiting for transfers between devices, to_partner(): return lax.ppermute(value_rows, 'tp', pair)  29.2 us
    ppermute x21, starting transfers between devices, trade(): return lax.ppermute(value, axis, pairs)  20.9 us
    ppermute x9, starting transfers between devices, move_along(): return lax.ppermute(value, 'ctx', pairs)  18.1 us
    all_gather x1, waiting for transfers between devices, on_device(): full_down = lax.all_gather(w_down, 'fsdp', axis=0, tiled=True)  17.3 us
  transfers between devices with their start and end apart: 44, of which 22 were waited for; matrix products, arithmetic and copies ran while one was open for 23% of the time, Pallas kernels for 4%

commit v1 on v0

--- a/solution.py
+++ b/solution.py
@@ -1,3 +1,5 @@
+import functools
+
 import jax
 import jax.numpy as jnp
 from jax import lax
@@ -58,9 +60,11 @@
     return jnp.where(key_place <= query_place, scores, -jnp.inf)
 
 
-def forward_kernel(query_ref, key_ref, value_ref, mixed_ref, lse_ref):
+def forward_kernel(query_ref, key_ref, value_ref, mixed_ref, lse_ref, scaled=False):
     place = lax.axis_index("ctx")
-    queries = [query_ref[g] * jnp.bfloat16(SCALE) for g in range(GROUP)]
+    queries = [
+        query_ref[g] if scaled else query_ref[g] * jnp.bfloat16(SCALE) for g in range(GROUP)
+    ]
 
     def scores_of(keys_turned, g, masked):
         scores = dot(keys_turned, queries[g], 1, 0)
@@ -102,13 +106,13 @@
         lse_ref[g] = top + jnp.log(total)
 
 
-def attend_forward(query, keyval):
+def attend_forward(query, keyval, scaled=False):
     blocks, token_positions = keyval.shape[0], keyval.shape[-1]
     head_block = (GROUP, HEAD_WIDTH, token_positions)
     key_block = (blocks, 1, 1, HEAD_WIDTH, token_positions)
     area = QUERY_HEADS * token_positions * token_positions * blocks
     return pl.pallas_call(
-        forward_kernel,
+        functools.partial(forward_kernel, scaled=scaled),
         grid=(KEYVAL_HEADS,),
         in_specs=[
             pl.BlockSpec(head_block, lambda j: (j, 0, 0)),
@@ -271,6 +275,512 @@
     ).astype(jnp.float32)
 
 
+MESH = pl.DeviceIdType.MESH
+KERNEL_VMEM = 58 * 1024 * 1024
+CHUNK_ROWS = 80
+WIDE = 512
+
+
+def remote(source, target, send_sem, recv_sem, **place):
+    return pltpu.make_async_remote_copy(
+        src_ref=source, dst_ref=target, send_sem=send_sem, recv_sem=recv_sem,
+        device_id=place, device_id_type=MESH,
+    )
+
+
+def wide(value):
+    return value.astype(jnp.float32)
+
+
+def low(value):
+    return value.astype(jnp.bfloat16)
+
+
+def greet(**place):
+    pl.semaphore_signal(
+        pltpu.get_barrier_semaphore(), inc=1, device_id=place, device_id_type=MESH
+    )
+
+
+def backward_sum_kernel(
+    query_ref, keyval_ref, back_ref, mixed_ref, lse_ref, cosine_ref, sine_ref,
+    down_ref, gate_ref, up_ref,
+    back_query_ref, back_keyval_ref, share_ref,
+    own, mate_in, y_in, up_in, parts, part_out, part_in, back_total, row_sums,
+    own_sem, mate_send, mate_recv, y_send, y_recv, up_send, up_recv, down_send, down_recv,
+    part_send, part_recv,
+):
+    place = lax.axis_index("ctx")
+    last = lax.axis_size("ctx") - 1
+    blocks = last + 1
+    rank = lax.axis_index("fsdp")
+    core = rank % 2
+    y = rank // 2
+    mate = rank + 1 - 2 * core
+    across = rank + 2 - 4 * y
+    gradients = (down_ref, gate_ref, up_ref)
+    rows = share_ref.shape[1]
+    per = rows // CHUNK_ROWS
+    chunks = len(gradients) * per
+
+    for m, gradient in enumerate(gradients):
+        for half in range(2):
+            pltpu.make_async_copy(
+                gradient.at[2 * half + core], own.at[m, half], own_sem.at[m, half]
+            ).start()
+    greet(fsdp=mate)
+    greet(fsdp=across)
+
+    @pl.when(place > 0)
+    def _():
+        greet(ctx=place - 1)
+
+    @pl.when(place < last)
+    def _():
+        greet(ctx=place + 1)
+
+    neighbours = (place + last - 1) // last + (2 * last - place - 1) // last
+    pl.semaphore_wait(pltpu.get_barrier_semaphore(), 2 + neighbours)
+
+    def chunk_at(ref, m, r, *front):
+        return ref.at[(m,) + front + (pl.ds(r * CHUNK_ROWS, CHUNK_ROWS),)]
+
+    def mate_copy(m, r, half):
+        gradient = gradients[m]
+        return remote(
+            gradient.at[2 * half + 1 - core, pl.ds(r * CHUNK_ROWS, CHUNK_ROWS)],
+            chunk_at(mate_in, m, r, half),
+            mate_send.at[m * per + r, half], mate_recv.at[m * per + r, half], fsdp=mate,
+        )
+
+    for m in range(len(gradients)):
+        for r in range(per):
+            for half in range(2):
+                mate_copy(m, r, half).start()
+    for m, gradient in enumerate(gradients):
+        for half in range(2):
+            pltpu.make_async_copy(
+                gradient.at[2 * half + core], own.at[m, half], own_sem.at[m, half]
+            ).wait()
+
+    def split(k):
+        r = lax.rem(k, per)
+        return k // per, pl.ds(pl.multiple_of(r * CHUNK_ROWS, CHUNK_ROWS), CHUNK_ROWS)
+
+    def y_copy(k):
+        m, at = split(k)
+        return remote(
+            own.at[m, 1 - y, at], y_in.at[m, at], y_send.at[k], y_recv.at[k], fsdp=across
+        )
+
+    def up_copy(k):
+        m, at = split(k)
+        return remote(
+            own.at[m, y, at], up_in.at[m, at], up_send.at[k], up_recv.at[k], ctx=place + 1
+        )
+
+    def down_copy(k):
+        m, at = split(k)
+        return remote(
+            share_ref.at[m, at], share_ref.at[m, at], down_send.at[k], down_recv.at[k],
+            ctx=place - 1,
+        )
+
+    def to_across(k):
+        m, at = split(k)
+        for half in range(2):
+            pltpu.make_async_copy(
+                mate_in.at[m, half, at], mate_in.at[m, half, at], mate_recv.at[k, half]
+            ).wait()
+        own[m, 1 - y, at] = low(wide(own[m, 1 - y, at]) + wide(mate_in[m, 1 - y, at]))
+        y_copy(k).start()
+
+    def to_next(k):
+        m, at = split(k)
+        y_copy(k).wait_recv()
+        total = wide(own[m, y, at]) + wide(mate_in[m, y, at]) + wide(y_in[m, at])
+
+        @pl.when(place == 0)
+        def _():
+            own[m, y, at] = low(total)
+
+        @pl.when(place > 0)
+        def _():
+            up_copy(k).wait_recv()
+            own[m, y, at] = low(total + wide(up_in[m, at]))
+
+        @pl.when(place < last)
+        def _():
+            up_copy(k).start()
+
+        @pl.when(place == last)
+        def _():
+            share_ref[m, at] = own[m, y, at]
+            down_copy(k).start()
+
+    def to_previous(k):
+        down_copy(k).wait_recv()
+
+        @pl.when(place > 0)
+        def _():
+            down_copy(k).start()
+
+    def tick(t):
+        @pl.when(t < chunks)
+        def _():
+            to_across(t)
+
+        b = t - 3 - 2 * place
+
+        @pl.when((b >= 0) & (b < 2 * chunks) & (lax.rem(b, 2) == 0))
+        def _():
+            to_next(b // 2)
+
+        c = t - 3 - 2 * last - 2 * (last - place)
+
+        @pl.when((place < last) & (c >= 0) & (c < 2 * chunks) & (lax.rem(c, 2) == 0))
+        def _():
+            to_previous(c // 2)
+
+    def part_copy(j, s):
+        return remote(
+            part_out.at[j, s - 1], part_in.at[j, s - 1], part_send.at[j, s - 1],
+            part_recv.at[j, s - 1], ctx=place - 1,
+        )
+
+    def step(j, s, masked):
+        keys = keyval_ref[s, 0, j]
+        keys_turned = keys.T
+        values_turned = keyval_ref[s, 1, j].T
+        back_key = jnp.zeros(keys.shape, jnp.float32)
+        back_value = jnp.zeros(keys.shape, jnp.float32)
+        for g in range(GROUP):
+            head = GROUP * j + g
+            query = query_ref[head]
+            back = back_ref[head]
+            if masked:
+                row_sums[g] = jnp.sum(wide(back) * wide(mixed_ref[head]), 0, keepdims=True)
+            scores = dot(keys_turned, query, 1, 0)
+            if masked:
+                scores = causal(scores)
+            weights = jnp.exp(scores - lse_ref[head])
+            back_weights = dot(values_turned, back, 1, 0)
+            back_scores = low(weights * (back_weights - row_sums[g]))
+            added = dot(keys, back_scores, 1, 0)
+            if masked:
+                back_total[g] = added
+            else:
+                back_total[g] += added
+            back_key += dot(query, back_scores, 1, 1)
+            back_value += dot(back, low(weights), 1, 1)
+        parts[j, s, 0] = back_key
+        parts[j, s, 1] = back_value
+
+    def hand_on(j):
+        for s in range(blocks):
+            @pl.when(s <= place)
+            def _(s=s):
+                @pl.when(place < last)
+                def _():
+                    pltpu.make_async_copy(
+                        part_in.at[j, s], part_in.at[j, s], part_recv.at[j, s]
+                    ).wait()
+                    for side in range(2):
+                        parts[j, s, side] += wide(part_in[j, s, side])
+
+                if s > 0:
+                    for side in range(2):
+                        part_out[j, s - 1, side] = low(parts[j, s, side])
+                    part_copy(j, s).start()
+                else:
+                    leading = parts[j, 0, 0, :HALF]
+                    trailing = parts[j, 0, 0, HALF:]
+                    cosine, sine = cosine_ref[...], sine_ref[...]
+                    back_keyval_ref[0, j, :HALF] = low(leading * cosine + trailing * sine)
+                    back_keyval_ref[0, j, HALF:] = low(trailing * cosine - leading * sine)
+                    back_keyval_ref[1, j] = low(parts[j, 0, 1])
+
+    def head_loop(j, carry):
+        @pl.when(j < KEYVAL_HEADS)
+        def _():
+            step(j, 0, True)
+
+        tick(j * blocks)
+
+        def block_loop(s, inner):
+            @pl.when((j < KEYVAL_HEADS) & (s <= place))
+            def _():
+                step(j, s, False)
+
+            tick(j * blocks + s)
+            return inner
+
+        lax.fori_loop(1, blocks, block_loop, 0)
+
+        @pl.when(j < KEYVAL_HEADS)
+        def _():
+            cosine, sine = cosine_ref[...], sine_ref[...]
+            for g in range(GROUP):
+                leading = back_total[g, :HALF] * SCALE
+                trailing = back_total[g, HALF:] * SCALE
+                head = GROUP * j + g
+                back_query_ref[head, :HALF] = low(leading * cosine + trailing * sine)
+                back_query_ref[head, HALF:] = low(trailing * cosine - leading * sine)
+
+        ready = j - (last - place)
+
+        @pl.when((ready >= 0) & (ready < KEYVAL_HEADS))
+        def _():
+            hand_on(ready)
+
+        return carry
+
+    assert (KEYVAL_HEADS + last) * blocks >= 4 + 4 * last + 2 * (chunks - 1)
+    lax.fori_loop(0, KEYVAL_HEADS + last, head_loop, 0)
+
+    for m in range(len(gradients)):
+        for r in range(per):
+            for half in range(2):
+                mate_copy(m, r, half).wait_send()
+
+    def finish(k, carry):
+        y_copy(k).wait_send()
+
+        @pl.when(place < last)
+        def _():
+            up_copy(k).wait_send()
+
+        @pl.when(place > 0)
+        def _():
+            down_copy(k).wait_send()
+
+        return carry
+
+    lax.fori_loop(0, chunks, finish, 0)
+
+    def finish_parts(j, carry):
+        for s in range(1, blocks):
+            @pl.when(s <= place)
+            def _(s=s):
+                part_copy(j, s).wait_send()
+        return carry
+
+    lax.fori_loop(0, KEYVAL_HEADS, finish_parts, 0)
+
+
+def backward_sum(query, keyval, back_mixed, mixed, lse, cosine, sine, gradients):
+    blocks, positions = keyval.shape[0], keyval.shape[-1]
+    count, rows, columns = gradients[0].shape
+    chunks = len(gradients) * rows // CHUNK_ROWS
+    area = QUERY_HEADS * positions * positions * blocks
+    vmem = pl.BlockSpec(memory_space=pltpu.VMEM)
+    dma = pltpu.SemaphoreType.DMA
+    share = (len(gradients), rows, columns)
+    head = (2, HEAD_WIDTH, positions)
+    return pl.pallas_call(
+        backward_sum_kernel,
+        in_specs=[vmem] * 7 + [pl.BlockSpec(memory_space=pl.ANY)] * 3,
+        out_specs=[vmem] * 3,
+        out_shape=[
+            jax.ShapeDtypeStruct(query.shape, jnp.bfloat16),
+            jax.ShapeDtypeStruct((2, KEYVAL_HEADS, HEAD_WIDTH, positions), jnp.bfloat16),
+            jax.ShapeDtypeStruct(share, jnp.bfloat16),
+        ],
+        scratch_shapes=[
+            pltpu.VMEM((len(gradients), 2, rows, columns), jnp.bfloat16),
+            pltpu.VMEM((len(gradients), 2, rows, columns), jnp.bfloat16),
+            pltpu.VMEM(share, jnp.bfloat16),
+            pltpu.VMEM(share, jnp.bfloat16),
+            pltpu.VMEM((KEYVAL_HEADS, blocks) + head, jnp.float32),
+            pltpu.VMEM((KEYVAL_HEADS, blocks - 1) + head, jnp.bfloat16),
+            pltpu.VMEM((KEYVAL_HEADS, blocks - 1) + head, jnp.bfloat16),
+            pltpu.VMEM((GROUP, HEAD_WIDTH, positions), jnp.float32),
+            pltpu.VMEM((GROUP, 1, positions), jnp.float32),
+            dma((len(gradients), 2)),
+            dma((chunks, 2)), dma((chunks, 2)),
+            dma((chunks,)), dma((chunks,)),
+            dma((chunks,)), dma((chunks,)),
+            dma((chunks,)), dma((chunks,)),
+            dma((KEYVAL_HEADS, blocks - 1)), dma((KEYVAL_HEADS, blocks - 1)),
+        ],
+        compiler_params=pltpu.CompilerParams(
+            vmem_limit_bytes=KERNEL_VMEM, collective_id=0, has_side_effects=True
+        ),
+        cost_estimate=pl.CostEstimate(
+            flops=40 * HEAD_WIDTH * area, bytes_accessed=10 * query.size, transcendentals=area
+        ),
+        name="backward_sum",
+    )(query, keyval, back_mixed, mixed, lse, cosine, sine, *gradients)
+
+
+def gradient_sum_kernel(
+    value_ref, share_ref,
+    own, mate_in, y_out, y_in, x_out, x_in, z_out, z_in,
+    own_sem, mate_send, mate_recv, y_send, y_recv, x_send, x_recv, z_send, z_recv,
+    all_send, all_recv, back_send, back_recv,
+):
+    place = lax.axis_index("ctx")
+    blocks = lax.axis_size("ctx")
+    rank = lax.axis_index("fsdp")
+    side = lax.axis_index("tp")
+    core = rank % 2
+    y = rank // 2
+    mate = rank + 1 - 2 * core
+    across = rank + 2 - 4 * y
+    rows, columns = share_ref.shape
+    chunks = columns // WIDE
+    half_rows = rows // 2
+    piece = half_rows // blocks
+
+    own_copies = [
+        pltpu.make_async_copy(value_ref.at[2 * half + core], own.at[half], own_sem.at[half])
+        for half in range(2)
+    ]
+    for copy in own_copies:
+        copy.start()
+    greet(fsdp=mate)
+    greet(fsdp=across)
+    greet(tp=1 - side)
+    for d in range(1, blocks):
+        greet(ctx=lax.rem(place + d, blocks))
+    pl.semaphore_wait(pltpu.get_barrier_semaphore(), 2 + blocks)
+
+    def mate_copy(n, half):
+        return remote(
+            value_ref.at[2 * half + 1 - core, :, pl.ds(n * WIDE, WIDE)], mate_in.at[n, half],
+            mate_send.at[n, half], mate_recv.at[n, half], fsdp=mate,
+        )
+
+    def y_copy(n):
+        return remote(y_out.at[n], y_in.at[n], y_send.at[n], y_recv.at[n], fsdp=across)
+
+    def x_copy(n):
+        other = pl.ds(pl.multiple_of((1 - side) * half_rows, half_rows), half_rows)
+        return remote(
+            x_out.at[n, other], x_in.at[n], x_send.at[n], x_recv.at[n], tp=1 - side
+        )
+
+    def z_copy(n, d):
+        target = lax.rem(place + d, blocks)
+        at = pl.ds(pl.multiple_of(target * piece, piece), piece)
+        return remote(
+            z_out.at[n, at], z_in.at[n, d - 1], z_send.at[n, d - 1], z_recv.at[n, d - 1],
+            ctx=target,
+        )
+
+    def all_copy(n, d, origin):
+        at = pl.ds(pl.multiple_of(side * half_rows + origin * piece, piece), piece)
+        spot = share_ref.at[at, pl.ds(n * WIDE, WIDE)]
+        return remote(
+            spot, spot, all_send.at[n, d - 1], all_recv.at[n, d - 1],
+            ctx=lax.rem(place + d, blocks),
+        )
+
+    def back_copy(n, half):
+        at = pl.ds(pl.multiple_of(half * half_rows, half_rows), half_rows)
+        spot = share_ref.at[at, pl.ds(n * WIDE, WIDE)]
+        return remote(spot, spot, back_send.at[n], back_recv.at[n], tp=1 - side)
+
+    for n in range(chunks):
+        for half in range(2):
+            mate_copy(n, half).start()
+    for copy in own_copies:
+        copy.wait()
+
+    def to_y(n):
+        for half in range(2):
+            mate_copy(n, half).wait_recv()
+        at = pl.ds(n * WIDE, WIDE)
+        y_out[n] = low(wide(own[1 - y, :, at]) + wide(mate_in[n, 1 - y]))
+        y_copy(n).start()
+
+    def to_x(n):
+        y_copy(n).wait_recv()
+        at = pl.ds(n * WIDE, WIDE)
+        x_out[n] = low(wide(own[y, :, at]) + wide(mate_in[n, y]) + wide(y_in[n]))
+        x_copy(n).start()
+
+    def to_z(n):
+        x_copy(n).wait_recv()
+        at = pl.ds(pl.multiple_of(side * half_rows, half_rows), half_rows)
+        z_out[n] = low(wide(x_out[n, at]) + wide(x_in[n]))
+        for d in range(1, blocks):
+            z_copy(n, d).start()
+
+    def to_all(n):
+        at = pl.ds(pl.multiple_of(place * piece, piece), piece)
+        total = wide(z_out[n, at])
+        for d in range(1, blocks):
+            z_copy(n, d).wait_recv()
+            total += wide(z_in[n, d - 1])
+        at = pl.ds(pl.multiple_of(side * half_rows + place * piece, piece), piece)
+        share_ref[at, pl.ds(n * WIDE, WIDE)] = low(total)
+        for d in range(1, blocks):
+            all_copy(n, d, place).start()
+
+    def to_back(n):
+        for d in range(1, blocks):
+            all_copy(n, d, lax.rem(place + blocks - d, blocks)).wait_recv()
+        back_copy(n, side).start()
+
+    def last_wait(n):
+        back_copy(n, 1 - side).wait_recv()
+
+    stages = (to_y, to_x, to_z, to_all, to_back, last_wait)
+    for t in range(chunks + len(stages) - 1):
+        for index in reversed(range(len(stages))):
+            if 0 <= t - index < chunks:
+                stages[index](t - index)
+    for n in range(chunks):
+        for half in range(2):
+            mate_copy(n, half).wait_send()
+        y_copy(n).wait_send()
+        x_copy(n).wait_send()
+        for d in range(1, blocks):
+            z_copy(n, d).wait_send()
+            all_copy(n, d, place).wait_send()
+        back_copy(n, side).wait_send()
+
+
+def gradient_sum(value):
+    count, rows, columns = value.shape
+    blocks = lax.axis_size("ctx")
+    chunks = columns // WIDE
+    half_rows = rows // 2
+    dma = pltpu.SemaphoreType.DMA
+    low_type = jnp.bfloat16
+    return pl.pallas_call(
+        gradient_sum_kernel,
+        in_specs=[pl.BlockSpec(memory_space=pl.ANY)],
+        out_specs=pl.BlockSpec(memory_space=pltpu.VMEM),
+        out_shape=jax.ShapeDtypeStruct((rows, columns), low_type),
+        scratch_shapes=[
+            pltpu.VMEM((2, rows, columns), low_type),
+            pltpu.VMEM((chunks, 2, rows, WIDE), low_type),
+            pltpu.VMEM((chunks, rows, WIDE), low_type),
+            pltpu.VMEM((chunks, rows, WIDE), low_type),
+            pltpu.VMEM((chunks, rows, WIDE), low_type),
+            pltpu.VMEM((chunks, half_rows, WIDE), low_type),
+            pltpu.VMEM((chunks, half_rows, WIDE), low_type),
+            pltpu.VMEM((chunks, blocks - 1, half_rows // blocks, WIDE), low_type),
+            dma((2,)),
+            dma((chunks, 2)), dma((chunks, 2)),
+            dma((chunks,)), dma((chunks,)),
+            dma((chunks,)), dma((chunks,)),
+            dma((chunks, blocks - 1)), dma((chunks, blocks - 1)),
+            dma((chunks, blocks - 1)), dma((chunks, blocks - 1)),
+            dma((chunks,)), dma((chunks,)),
+        ],
+        compiler_params=pltpu.CompilerParams(
+            vmem_limit_bytes=KERNEL_VMEM, collective_id=1, has_side_effects=True
+        ),
+        cost_estimate=pl.CostEstimate(
+            flops=value.size, bytes_accessed=4 * value.size, transcendentals=0
+        ),
+        name="gradient_sum",
+    )(value)
+
+
 def on_device(
     tokens, cotangent, input_gain, w_query, w_keyval, w_output, middle_gain, w_gate, w_up, w_down
 ):
@@ -428,14 +938,167 @@
     )
 
 
+def fast_on_device(
+    tokens, cotangent, input_gain, w_query, w_keyval, w_output, middle_gain, w_gate, w_up, w_down
+):
+    half = lax.axis_index("tp")
+    low_half = half == 0
+    pair = [(0, 1), (1, 0)]
+
+    def to_partner(value_rows):
+        return lax.ppermute(value_rows, "tp", pair)
+
+    def in_order(mine, received):
+        return jnp.concatenate(
+            [jnp.where(low_half, mine, received), jnp.where(low_half, received, mine)], 0
+        )
+
+    def take(value_rows, index):
+        return lax.dynamic_index_in_dim(value_rows, index, 0, keepdims=False)
+
+    tokens_own = in_order(take(tokens, half), to_partner(take(tokens, 1 - half)))
+    full_gain_one, full_gain_two = (
+        lax.all_gather(input_gain, "fsdp", axis=0, tiled=True),
+        lax.all_gather(middle_gain, "fsdp", axis=0, tiled=True),
+    )
+    full_in = lax.all_gather(jnp.concatenate([w_query, w_keyval], 1), "fsdp", axis=0, tiled=True)
+    full_output = lax.all_gather(w_output, "fsdp", axis=0, tiled=True)
+    full_gate = lax.all_gather(w_gate, "fsdp", axis=0, tiled=True)
+    full_up = lax.all_gather(w_up, "fsdp", axis=0, tiled=True)
+    full_down = lax.all_gather(w_down, "fsdp", axis=0, tiled=True)
+    cotangent_received = to_partner(cotangent)
+    cotangent_own = in_order(take(cotangent, half), take(cotangent_received, half))
+    cotangent_other = in_order(take(cotangent, 1 - half), take(cotangent_received, 1 - half))
+
+    token_positions = tokens_own.shape[0]
+    cosine, sine = rope_tables(token_positions, lax.axis_index("ctx") * token_positions)
+    gain_one = full_gain_one.astype(jnp.float32)
+    inputs = tokens_own.astype(jnp.float32)
+    unit_one, inverse_one = normalize(inputs)
+    normed_one = (unit_one * gain_one).astype(jnp.bfloat16)
+    keyval_raw = dot(full_in[:, QUERY_WIDTH:], normed_one, 0, 1)
+    keyval_low = jnp.concatenate(
+        [apply_rotary(keyval_raw[:KEY_WIDTH], cosine, sine), keyval_raw[KEY_WIDTH:]], 0
+    ).astype(jnp.bfloat16)
+    blocks = lax.axis_size("ctx")
+    keyval = jnp.stack([keyval_low] + [move_along(keyval_low, s) for s in range(1, blocks)], 0)
+    keyval = keyval.reshape(blocks, 2, KEYVAL_HEADS, HEAD_WIDTH, token_positions)
+    query_raw = dot(full_in[:, :QUERY_WIDTH], normed_one, 0, 1)
+    query_low = (
+        (apply_rotary(query_raw, cosine, sine).astype(jnp.bfloat16) * jnp.bfloat16(SCALE))
+        .reshape(QUERY_HEADS, HEAD_WIDTH, token_positions)
+    )
+    mixed_heads, lse = attend_forward(query_low, keyval, True)
+    mixed_low = mixed_heads.reshape(QUERY_WIDTH, token_positions)
+    middle = inputs + dot(mixed_low, full_output, 0, 0)
+
+    gain_two = full_gain_two.astype(jnp.float32)
+    unit_two, inverse_two = normalize(middle)
+    normed_two = (unit_two * gain_two).astype(jnp.bfloat16)
+    normed_other = to_partner(normed_two)
+
+    def feed(rows, back_rows):
+        gate_proj = dot(rows, full_gate, 1, 0)
+        up_proj = dot(rows, full_up, 1, 0)
+        sigmoid_gate = jax.nn.sigmoid(gate_proj)
+        swish_gate = gate_proj * sigmoid_gate
+        hidden = (swish_gate * up_proj).astype(jnp.bfloat16)
+        back_hidden = dot(back_rows, full_down, 1, 0)
+        back_gate = (
+            back_hidden * up_proj * sigmoid_gate * (1.0 + gate_proj * (1.0 - sigmoid_gate))
+        ).astype(jnp.bfloat16)
+        back_up = (back_hidden * swish_gate).astype(jnp.bfloat16)
+        return (hidden, back_gate, back_up)
+
+    def feed_input_back(back_gate, back_up):
+        return dot(back_gate, full_gate, 1, 1) + dot(back_up, full_up, 1, 1)
+
+    hidden_own, back_gate_own, back_up_own = feed(normed_two, cotangent_own)
+    hidden_other, back_gate_other, back_up_other = feed(normed_other, cotangent_other)
+    back_two_received = to_partner(
+        feed_input_back(back_gate_other, back_up_other).astype(jnp.bfloat16)
+    )
+    back_two = feed_input_back(back_gate_own, back_up_own) + back_two_received.astype(jnp.float32)
+    feed_received = to_partner(dot(hidden_other, full_down, 1, 1).astype(jnp.bfloat16))
+    result_own = (
+        middle + dot(hidden_own, full_down, 1, 1) + feed_received.astype(jnp.float32)
+    ).astype(jnp.bfloat16)
+
+    def feed_gradient(left_own, right_own, left_other, right_other):
+        gradient = dot(left_own, right_own, 0, 0) + dot(left_other, right_other, 0, 0)
+        return gradient.astype(jnp.bfloat16).reshape(lax.axis_size("fsdp"), -1, gradient.shape[1])
+
+    gradients = (
+        feed_gradient(cotangent_own, hidden_own, cotangent_other, hidden_other),
+        feed_gradient(normed_two, back_gate_own, normed_other, back_gate_other),
+        feed_gradient(normed_two, back_up_own, normed_other, back_up_other),
+    )
+
+    grad_gain_two = jnp.sum(back_two * unit_two, axis=0)
+    back_middle = cotangent_own.astype(jnp.float32) + norm_back(
+        back_two * gain_two, unit_two, inverse_two
+    )
+    back_attention = back_middle.astype(jnp.bfloat16)
+    back_mixed = dot(full_output, back_attention, 1, 1).astype(jnp.bfloat16)
+    back_mixed = back_mixed.reshape(query_low.shape)
+    grad_output = dot(mixed_low, back_attention, 1, 0).astype(jnp.bfloat16)
+    back_query, back_keyval, share = backward_sum(
+        query_low, keyval, back_mixed, mixed_heads, lse, cosine, sine, gradients
+    )
+    back_in = jnp.concatenate(
+        [
+            back_query.reshape(QUERY_WIDTH, token_positions),
+            back_keyval.reshape(2 * KEY_WIDTH, token_positions),
+        ],
+        0,
+    )
+    grad_in = dot(normed_one, back_in, 0, 1)
+    back_one = dot(back_in, full_in, 0, 1)
+    grad_gain_one = jnp.sum(back_one * unit_one, axis=0)
+    back_inputs = back_middle + norm_back(back_one * gain_one, unit_one, inverse_one)
+
+    def to_positions(value_rows):
+        split = value_rows.reshape(2, token_positions // 2, value_rows.shape[-1])
+        received = to_partner(take(split, 1 - half))
+        return in_order(take(split, half)[None], received[None])
+
+    result = to_positions(result_own)
+    grad_tokens = to_positions(back_inputs.astype(jnp.bfloat16)).astype(jnp.float32)
+    parts = lax.axis_size("fsdp")
+    rows = grad_output.shape[0] // parts
+    width = QUERY_WIDTH + full_in.shape[1]
+    gains = jnp.concatenate(
+        [grad_gain_one.reshape(parts, rows), grad_gain_two.reshape(parts, rows)], 1
+    )
+    gains = jnp.pad(gains[:, None], ((0, 0), (0, 15), (0, width - 2 * rows)))
+    summed = jnp.concatenate([grad_output, grad_in.astype(jnp.bfloat16)], 1)
+    summed = jnp.concatenate(
+        [summed.reshape(parts, rows, width), gains.astype(jnp.bfloat16)], 1
+    )
+    share_in = gradient_sum(summed).astype(jnp.float32)
+    return (
+        result,
+        grad_tokens,
+        share_in[rows, :rows],
+        share_in[:rows, QUERY_WIDTH : 2 * QUERY_WIDTH],
+        share_in[:rows, 2 * QUERY_WIDTH :],
+        share_in[:rows, :QUERY_WIDTH],
+        share_in[rows, rows : 2 * rows],
+        share[1].astype(jnp.float32),
+        share[2].astype(jnp.float32),
+        share[0].astype(jnp.float32),
+    )
+
+
 def solution(mesh):
     rows = P("fsdp", ("ctx", "tp"), None)
     specs = (
         P("fsdp"), P("fsdp", None), P("fsdp", None), P("fsdp", None),
         P("fsdp"), P("fsdp", "tp"), P("fsdp", "tp"), P("fsdp", "tp"),
     )
+    kernels = mesh.shape["fsdp"] == 4 and mesh.shape["tp"] == 2 and mesh.shape["ctx"] == 4
     return jax.shard_map(
-        on_device,
+        fast_on_device if kernels else on_device,
         mesh=mesh,
         in_specs=(rows, rows) + specs,
         out_specs=(rows, rows) + specs,

time: 530 us -> 450 us (0.85)
  waiting for transfers between devices: 284 us -> 87.7 us
  Pallas kernels: 21.2 us -> 201 us
  starting transfers between devices: 48 us -> 18.7 us
  other arithmetic: 42.6 us -> 21.8 us
  local copies, waits for them, and re-layouts: 34.1 us -> 19 us
    pallas_call x3, Pallas kernels: 21.2 us -> 201 us  [the longest x1 134 us: backward_sum(): pl.pallas_call(backward_sum_kernel, in_specs=[vmem] * 7 + [pl.BlockSpec(m...]
    ppermute x21 -> x0, waiting for transfers between devices: 88.1 us -> none  [trade(): return lax.ppermute(value, axis, pairs)]
    ppermute x9 -> x3, waiting for transfers between devices: 99 us -> 35.5 us  [move_along(): return lax.ppermute(value, 'ctx', pairs)]
    psum x1 -> x0, waiting for transfers between devices: 48.8 us -> none  [on_device(): lax.psum(lax.psum_scatter(gradients.astype(jnp.bfloat16), 'fsdp', scatter...]
    ppermute x21 -> x0, starting transfers between devices: 20.9 us -> none  [trade(): return lax.ppermute(value, axis, pairs)]
    convert_element_type x23 -> x6, other arithmetic: 14.9 us -> 5.06 us  [the longest x1 1.92 us: fast_on_device(): share[0].astype(jnp.float32)]
    ppermute x9 -> x3, starting transfers between devices: 18.1 us -> 9.71 us  [move_along(): return lax.ppermute(value, 'ctx', pairs)]
    select_n x16 -> x0, other arithmetic: 7.86 us -> none  [the longest x8 7.53 us: scatter_sum(): sent = jnp.where(second, split[:, 0], split[:, 1])]
  transfers between devices with their start and end apart: 44 -> 15, of which waited for: 22 -> 7; matrix products, arithmetic and copies ran while one was open for 23% -> 19% of each run, Pallas kernels for 4% -> 45%
where the time goes in v1:
time: 450 us; the launch traced here: 444 us
  Pallas kernels  201 us (45%)
  waiting for transfers between devices  87.7 us (19%)
  matrix products  73 us (16%)
  other arithmetic  21.8 us (5%)
  local copies, waits for them, and re-layouts  19 us (4%)
  starting transfers between devices  18.7 us (4%)
  between operations  15.6 us (3%)
  blocking collectives  6.92 us (2%)
    pallas_call x1, Pallas kernels, backward_sum(): pl.pallas_call(backward_sum_kernel, in_specs=[vmem] * 7 + [pl.BlockSpec(m...  134 us
    dot_general x25, matrix products, dot(): lax.dot_general(left, right, (((left_dim,), (right_dim,)), ((), ())), pre...  73 us
    pallas_call x1, Pallas kernels, gradient_sum(): pl.pallas_call(gradient_sum_kernel, in_specs=[pl.BlockSpec(memory_space=p...  59.2 us
    ppermute x3, waiting for transfers between devices, move_along(): return lax.ppermute(value, 'ctx', pairs)  35.5 us
    ppermute x7, waiting for transfers between devices, to_partner(): return lax.ppermute(value_rows, 'tp', pair)  31 us
    all_gather x1, waiting for transfers between devices, fast_on_device(): full_down = lax.all_gather(w_down, 'fsdp', axis=0, tiled=True)  19.3 us
    ppermute x3, starting transfers between devices, move_along(): return lax.ppermute(value, 'ctx', pairs)  9.71 us
  transfers between devices with their start and end apart: 15, of which 7 were waited for; matrix products, arithmetic and copies ran while one was open for 19% of the time, Pallas kernels for 45%

profile of v1, /device:TPU:0, one launch (start us, length us, event | category | flops | bytes accessed | tf_op | source)
XLA Modules:
  0.0 443.6 jit_solution(14107784504320102805)
XLA Ops:
  16.6 6.9 %all-reduce.3 = (bf16[960]{0:T(1024)(128)(2,1)S(1)}, bf16[960]{0:T(1024)(128)(2,1)S(1)}) all-reduce(bf16[960]{0:T(1024)(128)(2,1)S(1)} %dynamic-update-slice, bf16[960]{0:T(1024)(128)(2,1)S(1)} %dynamic-update-slice.1), channel_id=1, replica_groups=mesh['fsdp'=4,'ctx'=4,'tp'=2] {'fsdp'}, use_global_device_ids=true, to_apply=%add.1 | all-reduce | flops 1920 | bytes 7680
  28.3 18.9 %collective-permute-done.7 = bf16[2,256,960]{1,2,0:T(8,128)(2,1)} collective-permute-done((bf16[2,256,960]{1,2,0:T(8,128)(2,1)S(1)}, bf16[2,256,960]{1,2,0:T(8,128)(2,1)}, u32[]{:S(2)}, u32[]{:S(2)}) %collective-permute-start.7) | collective-permute-done | bytes 983072 | tf_op jit(solution)/shard_map/ppermute | solution.py:949
  53.0 5.9 %collective-permute-start.3 = (bf16[640,512]{1,0:T(8,128)(2,1)S(1)}, bf16[640,512]{1,0:T(8,128)(2,1)S(1)}, u32[]{:S(2)}, u32[]{:S(2)}) collective-permute-start(bf16[640,512]{1,0:T(8,128)(2,1)S(1)} %pad_maximum_fusion.11), channel_id=1, source_target_pairs={{0,6},{1,7},{8,14},{9,15},{16,22},{17,23},{24,30},{25,31}} | collective-permute-start | bytes 1966088 | tf_op jit(solution)/shard_map/ppermute | solution.py:233
  64.6 9.5 %collective-permute-done.3 = bf16[640,512]{1,0:T(8,128)(2,1)S(1)} collective-permute-done((bf16[640,512]{1,0:T(8,128)(2,1)S(1)}, bf16[640,512]{1,0:T(8,128)(2,1)S(1)}, u32[]{:S(2)}, u32[]{:S(2)}) %collective-permute-start.3) | collective-permute-done | bytes 655392 | tf_op jit(solution)/shard_map/ppermute | solution.py:233
  74.1 14.0 %collective-permute-done.2 = bf16[640,512]{1,0:T(8,128)(2,1)S(1)} collective-permute-done((bf16[640,512]{1,0:T(8,128)(2,1)S(1)}, bf16[640,512]{1,0:T(8,128)(2,1)S(1)}, u32[]{:S(2)}, u32[]{:S(2)}) %collective-permute-start.2) | collective-permute-done | bytes 655392 | tf_op jit(solution)/shard_map/ppermute | solution.py:233
  88.1 12.0 %collective-permute-done.1 = bf16[640,512]{1,0:T(8,128)(2,1)S(1)} collective-permute-done((bf16[640,512]{1,0:T(8,128)(2,1)S(1)}, bf16[640,512]{1,0:T(8,128)(2,1)S(1)}, u32[]{:S(2)}, u32[]{:S(2)}) %collective-permute-start.1) | collective-permute-done | bytes 655392 | tf_op jit(solution)/shard_map/ppermute | solution.py:233
  100.5 7.7 %attend_forward.1 = (bf16[15,64,512]{2,1,0:T(8,128)(2,1)S(1)}, f32[15,1,512]{2,1,0:T(1,128)S(1)}) custom-call(bf16[15,64,512]{2,1,0:T(8,128)(2,1)S(1)} %bitcast.101, bf16[4,2,5,64,512]{4,3,2,1,0:T(8,128)(2,1)S(1)} %pad_maximum_fusion.1.key_ref.value_ref.keyval_ref, bf16[4,2,5,64,512]{4,3,2,1,0:T(8,128)(2,1)S(1)} %pad_maximum_fusion.1.key_ref.value_ref.keyval_ref), custom_call_target="tpu_custom_call" | custom-call | flops 16106127360 | bytes 2949120 | tf_op jit(solution)/shard_map/attend_forward/pallas_call | solution.py:114
  109.8 3.2 multiply_reduce_fusion.2
  114.8 4.8 %fusion.37 = f32[512,1280]{1,0:T(8,128)} fusion(bf16[512,960]{0,1:T(8,128)(2,1)S(1)} %multiply_convert_fusion.6, bf16[960,1280]{1,0:T(8,128)(2,1)} %all-gather.10.cloned.1.call-done), kind=kOutput, calls=%fused_computation.109 | convolution fusion | flops 1258291200 | bytes 6062080 | tf_op jit(solution)/shard_map/dot_general | solution.py:25
  119.6 4.7 %fusion.38 = f32[512,1280]{1,0:T(8,128)} fusion(bf16[512,960]{0,1:T(8,128)(2,1)S(1)} %multiply_convert_fusion.6, bf16[960,1280]{1,0:T(8,128)(2,1)} %all-gather.12.cloned.1.call-done), kind=kOutput, calls=%fused_computation.110 | convolution fusion | flops 1258291200 | bytes 6062080 | tf_op jit(solution)/shard_map/dot_general | solution.py:25
  124.3 19.3 %all-gather.14.cloned.1.call-done = bf16[960,1280]{1,0:T(8,128)(2,1)} async-done(((bf16[240,1280]{1,0:T(8,128)(2,1)}), bf16[960,1280]{1,0:T(8,128)(2,1)}) %all-gather.14.cloned.1.call-update) | async-done | bytes 2457616 | tf_op jit(solution)/shard_map/all_gather | solution.py:968
  143.6 6.0 %multiply_convert_fusion.2 = (bf16[512,1280]{1,0:T(8,128)(2,1)S(1)}, bf16[512,1280]{1,0:T(8,128)(2,1)S(1)}, bf16[512,1280]{1,0:T(8,128)(2,1)S(1)}) fusion(f32[512,1280]{1,0:T(8,128)} %fusion.37, f32[512,1280]{1,0:T(8,128)} %fusion.38, bf16[960,1280]{1,0:T(8,128)(2,1)} %all-gather.14.cloned.1.call-done, bf16[256,960]{0,1:T(8,128)(2,1)} %get-tuple-element.35, ...), kind=kOutput, calls=%fused_computation.18 | convolution fusion | flops 1270087680 | bytes 12615680 | tf_op jit(solution)/shard_map/dot_general | solution.py:25
  155.9 3.1 fusion.39
  172.1 4.1 add_convert_fusion.1
  179.1 4.1 add_convert_fusion
  183.1 9.1 %collective-permute-done.8 = bf16[512,960]{0,1:T(8,128)(2,1)S(1)} collective-permute-done((bf16[512,960]{0,1:T(8,128)(2,1)S(1)}, bf16[512,960]{0,1:T(8,128)(2,1)S(1)}, u32[]{:S(2)}, u32[]{:S(2)}) %collective-permute-start.8) | collective-permute-done | bytes 983072 | tf_op jit(solution)/shard_map/ppermute | solution.py:949
  197.8 134.0 %backward_sum.1 = (bf16[15,64,512]{2,1,0:T(8,128)(2,1)}, bf16[2,5,64,512]{3,2,1,0:T(8,128)(2,1)}, bf16[3,240,1280]{2,1,0:T(8,128)(2,1)}) custom-call(bf16[15,64,512]{2,1,0:T(8,128)(2,1)} %bitcast.102, bf16[4,2,5,64,512]{4,3,2,1,0:T(8,128)(2,1)} %copy-done, bf16[15,64,512]{2,1,0:T(8,128)(2,1)} %bitcast.121, bf16[15,64,512]{2,1,0:T(8,128)(2,1)} %copy-done.2, ...), custom_call_target="tpu_custom_call" | custom-call | flops 40265318400 | bytes 4915200 | tf_op jit(solution)/shard_map/backward_sum/pallas_call | solution.py:580
  331.8 4.6 %fusion.14 = (bf16[960]{0:T(1024)(128)(2,1)S(1)}, f32[512]{0:T(512)S(1)}, f32[512,960]{0,1:T(8,128)S(1)}) fusion(f32[512]{0:T(512)S(1)} %add_rsqrt_fusion.1, bf16[256,960]{0,1:T(8,128)(2,1)S(1)} %copy-done.11, bf16[256,960]{0,1:T(8,128)(2,1)S(1)} %get-tuple-element.45, f32[960]{0:T(1024)S(1)} %convert_element_type.135, ...), kind=kOutput, calls=%fused_computation.32 | convolution fusion | flops 1581054464 | bytes 7669376 | tf_op jit(solution)/shard_map/dot_general | solution.py:25
  337.9 3.3 reshape.217
  341.2 4.2 convolution_convert_fusion.1
  345.5 3.7 convolution_convert_fusion
  353.0 5.1 %constant_dynamic-slice_fusion.1 = (bf16[1,256,960]{1,0,2:T(2,128)(2,1)S(1)}, bf16[1,256,960]{1,0,2:T(2,128)(2,1)S(1)}, bf16[1,256,960]{1,0,2:T(2,128)(2,1)S(1)}, bf16[1,256,960]{1,0,2:T(2,128)(2,1)}) fusion(bf16[2,256,960]{1,0,2:T(2,128)(2,1)S(1)} %copy-done.8, s32[]{:T(128)S(6)} %select_n.77, s32[]{:T(128)S(6)} %select_n.78, ...), kind=kLoop, calls=%fused_computation.91 | loop fusion | bytes 3932168 | tf_op jit(solution)/shard_map/jit(dynamic_index_in_dim)/dynamic_slice | solution.py:957
  362.2 3.7 pad_maximum_fusion
  368.6 59.2 %gradient_sum.1 = bf16[256,2560]{1,0:T(8,128)(2,1)} custom-call(bf16[4,256,2560]{2,1,0:T(8,128)(2,1)} %fusion.1.value_ref), custom_call_target="tpu_custom_call" | custom-call | flops 2621440 | bytes 10485760 | tf_op jit(solution)/shard_map/gradient_sum/pallas_call | solution.py:752
  (161 shorter events, 77.0 us)
Async XLA Ops:
  7.2 42.4 %all-gather.6.cloned.1.call-start = ((), (), s32[]{:S(2)}) async-start(), calls=%async_computation | async-start | bytes 3993600 | tf_op jit(solution)/shard_map/all_gather | solution.py:964
  9.5 100.2 %all-gather.8.cloned.1.call-start = ((), (), s32[]{:S(2)}) async-start(), calls=%async_computation.1 | async-start | bytes 2457600 | tf_op jit(solution)/shard_map/all_gather | solution.py:965
  10.3 104.5 %all-gather.10.cloned.1.call-start = ((), (), s32[]{:S(2)}) async-start(), calls=%async_computation.2 | async-start | bytes 3072000 | tf_op jit(solution)/shard_map/all_gather | solution.py:966
  11.0 108.6 %all-gather.12.cloned.1.call-start = ((), (), s32[]{:S(2)}) async-start(), calls=%async_computation.3 | async-start | bytes 3072000 | tf_op jit(solution)/shard_map/all_gather | solution.py:967
  11.6 132.0 %all-gather.14.cloned.1.call-start = ((), (), s32[]{:S(2)}) async-start(), calls=%async_computation.4 | async-start | bytes 3072000 | tf_op jit(solution)/shard_map/all_gather | solution.py:968
  11.7 15.2 %collective-permute-start = (bf16[256,960]{0,1:T(8,128)(2,1)S(1)}, bf16[256,960]{0,1:T(8,128)(2,1)}, u32[]{:S(2)}, u32[]{:S(2)}) collective-permute-start(bf16[256,960]{0,1:T(8,128)(2,1)S(1)} %dynamic-slice_bitcast_fusion), channel_id=1, source_target_pairs={{0,1},{1,0},{2,3},{3,2},{4,5},{5,4},{6,7},{7,6},{8,9},{9,8},{10,11... | collective-permute-start | bytes 1474568 | tf_op jit(solution)/shard_map/ppermute | solution.py:949
  14.7 32.4 %collective-permute-start.7 = (bf16[2,256,960]{1,2,0:T(8,128)(2,1)S(1)}, bf16[2,256,960]{1,2,0:T(8,128)(2,1)}, u32[]{:S(2)}, u32[]{:S(2)}) collective-permute-start(bf16[2,256,960]{1,2,0:T(8,128)(2,1)S(1)} %copy-done.21), channel_id=1, source_target_pairs={{0,1},{1,0},{2,3},{3,2},{4,5},{5,4},{6,7},{7,6},{8,9},{9,8},{10,11... | collective-permute-start | bytes 2949128 | tf_op jit(solution)/shard_map/ppermute | solution.py:949
  23.8 40.2 %copy-start.22 = (f32[32,512]{1,0:T(8,128)}, f32[32,512]{1,0:T(8,128)S(1)}, u32[]{:S(2)}) copy-start(f32[32,512]{1,0:T(8,128)S(1)} %get-tuple-element.57.cosine_ref) | copy-start | bytes 196612
  23.9 40.2 %copy-start.23 = (f32[32,512]{1,0:T(8,128)}, f32[32,512]{1,0:T(8,128)S(1)}, u32[]{:S(2)}) copy-start(f32[32,512]{1,0:T(8,128)S(1)} %get-tuple-element.58.sine_ref) | copy-start | bytes 196612
  28.0 34.7 %copy-start.10 = (bf16[256,960]{0,1:T(8,128)(2,1)}, bf16[256,960]{0,1:T(8,128)(2,1)S(1)}, u32[]{:S(2)}) copy-start(bf16[256,960]{0,1:T(8,128)(2,1)S(1)} %get-tuple-element.46) | copy-start | bytes 1474564
  52.7 10.0 %copy-start.24 = (bf16[960,1600]{1,0:T(8,128)(2,1)S(1)}, bf16[960,1600]{1,0:T(8,128)(2,1)}, u32[]{:S(2)}) copy-start(bf16[960,1600]{1,0:T(8,128)(2,1)} %all-gather.6.cloned.1.call-done) | copy-start | bytes 9216004
  53.0 21.1 %collective-permute-start.3 = (bf16[640,512]{1,0:T(8,128)(2,1)S(1)}, bf16[640,512]{1,0:T(8,128)(2,1)S(1)}, u32[]{:S(2)}, u32[]{:S(2)}) collective-permute-start(bf16[640,512]{1,0:T(8,128)(2,1)S(1)} %pad_maximum_fusion.11), channel_id=1, source_target_pairs={{0,6},{1,7},{8,14},{9,15},{16,22},{17,23},{24,30},{25,31}} | collective-permute-start | bytes 1966088 | tf_op jit(solution)/shard_map/ppermute | solution.py:233
  58.9 29.2 %collective-permute-start.2 = (bf16[640,512]{1,0:T(8,128)(2,1)S(1)}, bf16[640,512]{1,0:T(8,128)(2,1)S(1)}, u32[]{:S(2)}, u32[]{:S(2)}) collective-permute-start(bf16[640,512]{1,0:T(8,128)(2,1)S(1)} %pad_maximum_fusion.11), channel_id=1, source_target_pairs={{0,4},{2,6},{1,5},{3,7},{8,12},{10,14},{9,13},{11,15},{16,20},{18,... | collective-permute-start | bytes 1966088 | tf_op jit(solution)/shard_map/ppermute | solution.py:233
  60.2 39.9 %collective-permute-start.1 = (bf16[640,512]{1,0:T(8,128)(2,1)S(1)}, bf16[640,512]{1,0:T(8,128)(2,1)S(1)}, u32[]{:S(2)}, u32[]{:S(2)}) collective-permute-start(bf16[640,512]{1,0:T(8,128)(2,1)S(1)} %pad_maximum_fusion.11), channel_id=1, source_target_pairs={{0,2},{2,4},{4,6},{1,3},{3,5},{5,7},{8,10},{10,12},{12,14},{9,11},... | collective-permute-start | bytes 1966088 | tf_op jit(solution)/shard_map/ppermute | solution.py:233
  64.6 35.9 %copy-start.1 = (bf16[15,2,32,512]{3,2,1,0:T(8,128)(2,1)}, bf16[15,2,32,512]{3,2,1,0:T(8,128)(2,1)S(1)}, u32[]{:S(2)}) copy-start(bf16[15,2,32,512]{3,2,1,0:T(8,128)(2,1)S(1)} %maximum_multiply_fusion) | copy-start | bytes 2949124
  100.4 7.8 %copy-start = (bf16[4,2,5,64,512]{4,3,2,1,0:T(8,128)(2,1)}, bf16[4,2,5,64,512]{4,3,2,1,0:T(8,128)(2,1)S(1)}, u32[]{:S(2)}) copy-start(bf16[4,2,5,64,512]{4,3,2,1,0:T(8,128)(2,1)S(1)} %pad_maximum_fusion.1.key_ref.value_ref.keyval_ref) | copy-start | bytes 7864324
  113.2 42.7 %collective-permute-start.4 = (bf16[512,960]{0,1:T(8,128)(2,1)S(1)}, bf16[512,960]{0,1:T(8,128)(2,1)}, u32[]{:S(2)}, u32[]{:S(2)}) collective-permute-start(bf16[512,960]{0,1:T(8,128)(2,1)S(1)} %multiply_convert_fusion.6), channel_id=1, source_target_pairs={{0,1},{1,0},{2,3},{3,2},{4,5},{5,4},{6,7},{7,6},{8,9},{9,8},{10,11... | collective-permute-start | bytes 2949128 | tf_op jit(solution)/shard_map/ppermute | solution.py:949
  167.6 24.7 %collective-permute-start.8 = (bf16[512,960]{0,1:T(8,128)(2,1)S(1)}, bf16[512,960]{0,1:T(8,128)(2,1)S(1)}, u32[]{:S(2)}, u32[]{:S(2)}) collective-permute-start(bf16[512,960]{0,1:T(8,128)(2,1)S(1)} %add_convert_fusion.3), channel_id=1, source_target_pairs={{0,1},{1,0},{2,3},{3,2},{4,5},{5,4},{6,7},{7,6},{8,9},{9,8},{10,11... | collective-permute-start | bytes 2949128 | tf_op jit(solution)/shard_map/ppermute | solution.py:949
  171.5 177.6 %collective-permute-start.5 = (bf16[512,960]{0,1:T(8,128)(2,1)}, bf16[512,960]{0,1:T(8,128)(2,1)}, u32[]{:S(2)}, u32[]{:S(2)}) collective-permute-start(bf16[512,960]{0,1:T(8,128)(2,1)} %convolution_convert_fusion.3), channel_id=1, source_target_pairs={{0,1},{1,0},{2,3},{3,2},{4,5},{5,4},{6,7},{7,6},{8,9},{9,8},{10,11... | collective-permute-start | bytes 2949128 | tf_op jit(solution)/shard_map/ppermute | solution.py:949
  195.6 140.8 %copy-start.9 = (f32[512,960]{0,1:T(8,128)}, f32[512,960]{0,1:T(8,128)S(1)}, u32[]{:S(2)}) copy-start(f32[512,960]{0,1:T(8,128)S(1)} %multiply_add_fusion) | copy-start | bytes 5898244
  197.8 134.1 %copy-start.11 = (bf16[256,960]{0,1:T(8,128)(2,1)S(1)}, bf16[256,960]{0,1:T(8,128)(2,1)}, u32[]{:S(2)}) copy-start(bf16[256,960]{0,1:T(8,128)(2,1)} %copy-done.10) | copy-start | bytes 1474564
  359.0 74.0 %collective-permute-start.6 = (bf16[256,960]{0,1:T(8,128)(2,1)}, bf16[256,960]{0,1:T(8,128)(2,1)}, u32[]{:S(2)}, u32[]{:S(2)}) collective-permute-start(bf16[256,960]{0,1:T(8,128)(2,1)} %bitcast.100), channel_id=1, source_target_pairs={{0,1},{1,0},{2,3},{3,2},{4,5},{5,4},{6,7},{7,6},{8,9},{9,8},{10,11... | collective-permute-start | bytes 1474568 | tf_op jit(solution)/shard_map/ppermute | solution.py:949
  361.2 73.9 %collective-permute-start.9 = (bf16[256,960]{0,1:T(8,128)(2,1)}, bf16[256,960]{0,1:T(8,128)(2,1)S(1)}, u32[]{:S(2)}, u32[]{:S(2)}) collective-permute-start(bf16[256,960]{0,1:T(8,128)(2,1)} %bitcast.99), channel_id=1, source_target_pairs={{0,1},{1,0},{2,3},{3,2},{4,5},{5,4},{6,7},{7,6},{8,9},{9,8},{10,11... | collective-permute-start | bytes 1474568 | tf_op jit(solution)/shard_map/ppermute | solution.py:949
  368.6 59.2 %copy-start.19 = (bf16[3,240,1280]{2,1,0:T(8,128)(2,1)S(1)}, bf16[3,240,1280]{2,1,0:T(8,128)(2,1)}, u32[]{:S(2)}) copy-start(bf16[3,240,1280]{2,1,0:T(8,128)(2,1)} %get-tuple-element.19) | copy-start | bytes 5529604
  (26 other events, 85.0 us)
Sparse Core Ops, SparseCore 0:
  10.2 31.5 all-gather.5
  43.3 21.8 all-gather.7
  66.8 24.6 all-gather.9
  92.8 24.6 all-gather.11
  118.9 24.6 all-gather.13

commit v2 on v1

--- a/solution.py
+++ b/solution.py
@@ -1,5 +1,3 @@
-import functools
-
 import jax
 import jax.numpy as jnp
 from jax import lax
@@ -60,11 +58,9 @@
     return jnp.where(key_place <= query_place, scores, -jnp.inf)
 
 
-def forward_kernel(query_ref, key_ref, value_ref, mixed_ref, lse_ref, scaled=False):
+def forward_kernel(query_ref, key_ref, value_ref, mixed_ref, lse_ref):
     place = lax.axis_index("ctx")
-    queries = [
-        query_ref[g] if scaled else query_ref[g] * jnp.bfloat16(SCALE) for g in range(GROUP)
-    ]
+    queries = [query_ref[g] * jnp.bfloat16(SCALE) for g in range(GROUP)]
 
     def scores_of(keys_turned, g, masked):
         scores = dot(keys_turned, queries[g], 1, 0)
@@ -106,13 +102,13 @@
         lse_ref[g] = top + jnp.log(total)
 
 
-def attend_forward(query, keyval, scaled=False):
+def attend_forward(query, keyval):
     blocks, token_positions = keyval.shape[0], keyval.shape[-1]
     head_block = (GROUP, HEAD_WIDTH, token_positions)
     key_block = (blocks, 1, 1, HEAD_WIDTH, token_positions)
     area = QUERY_HEADS * token_positions * token_positions * blocks
     return pl.pallas_call(
-        functools.partial(forward_kernel, scaled=scaled),
+        forward_kernel,
         grid=(KEYVAL_HEADS,),
         in_specs=[
             pl.BlockSpec(head_block, lambda j: (j, 0, 0)),
@@ -322,6 +318,7 @@
     rows = share_ref.shape[1]
     per = rows // CHUNK_ROWS
     chunks = len(gradients) * per
+    early = per
 
     for m, gradient in enumerate(gradients):
         for half in range(2):
@@ -416,7 +413,10 @@
         @pl.when(place == last)
         def _():
             share_ref[m, at] = own[m, y, at]
-            down_copy(k).start()
+
+            @pl.when(k < early)
+            def _():
+                down_copy(k).start()
 
     def to_previous(k):
         down_copy(k).wait_recv()
@@ -438,7 +438,7 @@
 
         c = t - 3 - 2 * last - 2 * (last - place)
 
-        @pl.when((place < last) & (c >= 0) & (c < 2 * chunks) & (lax.rem(c, 2) == 0))
+        @pl.when((place < last) & (c >= 0) & (c < 2 * early) & (lax.rem(c, 2) == 0))
         def _():
             to_previous(c // 2)
 
@@ -449,9 +449,9 @@
         )
 
     def step(j, s, masked):
-        keys = keyval_ref[s, 0, j]
+        keys = keyval_ref[s, j, 0]
         keys_turned = keys.T
-        values_turned = keyval_ref[s, 1, j].T
+        values_turned = keyval_ref[s, j, 1].T
         back_key = jnp.zeros(keys.shape, jnp.float32)
         back_value = jnp.zeros(keys.shape, jnp.float32)
         for g in range(GROUP):
@@ -550,7 +550,7 @@
         def _():
             up_copy(k).wait_send()
 
-        @pl.when(place > 0)
+        @pl.when((place > 0) & (k < early))
         def _():
             down_copy(k).wait_send()
 
@@ -600,7 +600,7 @@
             dma((chunks, 2)), dma((chunks, 2)),
             dma((chunks,)), dma((chunks,)),
             dma((chunks,)), dma((chunks,)),
-            dma((chunks,)), dma((chunks,)),
+            dma((rows // CHUNK_ROWS,)), dma((rows // CHUNK_ROWS,)),
             dma((KEYVAL_HEADS, blocks - 1)), dma((KEYVAL_HEADS, blocks - 1)),
         ],
         compiler_params=pltpu.CompilerParams(
@@ -614,10 +614,10 @@
 
 
 def gradient_sum_kernel(
-    value_ref, share_ref,
+    value_ref, feed_ref, share_ref, feed_share_ref,
     own, mate_in, y_out, y_in, x_out, x_in, z_out, z_in,
     own_sem, mate_send, mate_recv, y_send, y_recv, x_send, x_recv, z_send, z_recv,
-    all_send, all_recv, back_send, back_recv,
+    all_send, all_recv, back_send, back_recv, down_send, down_recv, feed_sem,
 ):
     place = lax.axis_index("ctx")
     blocks = lax.axis_size("ctx")
@@ -681,9 +681,38 @@
         spot = share_ref.at[at, pl.ds(n * WIDE, WIDE)]
         return remote(spot, spot, back_send.at[n], back_recv.at[n], tp=1 - side)
 
+    last = blocks - 1
+    per = feed_ref.shape[1] // CHUNK_ROWS
+    returned = feed_share_ref.shape[0] * per
+
+    def feed_at(ref, k, skip):
+        return ref.at[k // per + skip, pl.ds(k % per * CHUNK_ROWS, CHUNK_ROWS)]
+
+    def down_copy(k, source):
+        return remote(
+            source, feed_at(feed_share_ref, k, 0), down_send.at[k], down_recv.at[k],
+            ctx=place - 1,
+        )
+
+    feed_copy = pltpu.make_async_copy(feed_ref.at[pl.ds(1, 2)], feed_share_ref, feed_sem)
+
+    def to_previous(k):
+        down_copy(k, feed_at(feed_share_ref, k, 0)).wait_recv()
+
+        @pl.when(place > 0)
+        def _():
+            down_copy(k, feed_at(feed_share_ref, k, 0)).start()
+
     for n in range(chunks):
         for half in range(2):
             mate_copy(n, half).start()
+
+    @pl.when(place == last)
+    def _():
+        for k in range(returned):
+            down_copy(k, feed_at(feed_ref, k, 1)).start()
+        feed_copy.start()
+
     for copy in own_copies:
         copy.wait()
 
@@ -727,10 +756,25 @@
         back_copy(n, 1 - side).wait_recv()
 
     stages = (to_y, to_x, to_z, to_all, to_back, last_wait)
-    for t in range(chunks + len(stages) - 1):
+    for t in range(max(chunks + len(stages), returned + last) - 1):
         for index in reversed(range(len(stages))):
             if 0 <= t - index < chunks:
                 stages[index](t - index)
+        for index in range(last):
+            if 0 <= t - last + 1 + index < returned:
+                @pl.when(place == index)
+                def _(k=t - last + 1 + index):
+                    to_previous(k)
+
+    @pl.when(place == last)
+    def _():
+        feed_copy.wait()
+
+    @pl.when(place > 0)
+    def _():
+        for k in range(returned):
+            down_copy(k, feed_at(feed_ref, k, 1)).wait_send()
+
     for n in range(chunks):
         for half in range(2):
             mate_copy(n, half).wait_send()
@@ -742,8 +786,9 @@
         back_copy(n, side).wait_send()
 
 
-def gradient_sum(value):
+def gradient_sum(value, feed):
     count, rows, columns = value.shape
+    returned = (feed.shape[0] - 1) * feed.shape[1] // CHUNK_ROWS
     blocks = lax.axis_size("ctx")
     chunks = columns // WIDE
     half_rows = rows // 2
@@ -751,9 +796,12 @@
     low_type = jnp.bfloat16
     return pl.pallas_call(
         gradient_sum_kernel,
-        in_specs=[pl.BlockSpec(memory_space=pl.ANY)],
-        out_specs=pl.BlockSpec(memory_space=pltpu.VMEM),
-        out_shape=jax.ShapeDtypeStruct((rows, columns), low_type),
+        in_specs=[pl.BlockSpec(memory_space=pl.ANY)] * 2,
+        out_specs=[pl.BlockSpec(memory_space=pltpu.VMEM)] * 2,
+        out_shape=[
+            jax.ShapeDtypeStruct((rows, columns), low_type),
+            jax.ShapeDtypeStruct((feed.shape[0] - 1,) + feed.shape[1:], low_type),
+        ],
         scratch_shapes=[
             pltpu.VMEM((2, rows, columns), low_type),
             pltpu.VMEM((chunks, 2, rows, WIDE), low_type),
@@ -770,6 +818,7 @@
             dma((chunks, blocks - 1)), dma((chunks, blocks - 1)),
             dma((chunks, blocks - 1)), dma((chunks, blocks - 1)),
             dma((chunks,)), dma((chunks,)),
+            dma((returned,)), dma((returned,)), dma,
         ],
         compiler_params=pltpu.CompilerParams(
             vmem_limit_bytes=KERNEL_VMEM, collective_id=1, has_side_effects=True
@@ -778,7 +827,297 @@
             flops=value.size, bytes_accessed=4 * value.size, transcendentals=0
         ),
         name="gradient_sum",
-    )(value)
+    )(value, feed)
+
+
+def front_kernel(
+    tokens_ref, cotangent_ref, gains_ref, cosine_ref, sine_ref, *refs
+):
+    weights, refs = refs[:6], refs[6:]
+    (
+        tokens_own, cotangent_own, cotangent_other, gains_out, normed_out, query_out, keyval_ref,
+        mixed_out, lse_ref,
+    ), refs = refs[:9], refs[9:]
+    full, refs = refs[:6], refs[6:]
+    (
+        gain_in, raw, tops, totals, sums,
+        local_sem, gain_send, gain_recv, token_send, token_recv, cot_send, cot_recv,
+        y_send, y_recv, mate_send, mate_recv, pass_send, pass_recv, key_send, key_recv,
+    ) = refs
+    place = lax.axis_index("ctx")
+    last = lax.axis_size("ctx") - 1
+    rank = lax.axis_index("fsdp")
+    side = lax.axis_index("tp")
+    core = rank % 2
+    mate = rank + 1 - 2 * core
+    across = rank + 2 - 4 * (rank // 2)
+    part_rows = tokens_ref.shape[1]
+
+    local = [
+        pltpu.make_async_copy(tokens_ref.at[side], tokens_own.at[side], local_sem.at[0]),
+        pltpu.make_async_copy(cotangent_ref.at[side], cotangent_own.at[side], local_sem.at[1]),
+        pltpu.make_async_copy(
+            cotangent_ref.at[1 - side], cotangent_other.at[side], local_sem.at[2]
+        ),
+    ]
+    for w in range(len(weights)):
+        local.append(pltpu.make_async_copy(weights[w], full[w].at[rank], local_sem.at[3 + w]))
+    for copy in local:
+        copy.start()
+
+    greet(fsdp=mate)
+    greet(fsdp=across)
+    greet(tp=1 - side)
+
+    @pl.when(place > 0)
+    def _():
+        greet(ctx=place - 1)
+
+    @pl.when(place < last)
+    def _():
+        greet(ctx=place + 1)
+
+    neighbours = (place + last - 1) // last + (2 * last - place - 1) // last
+    pl.semaphore_wait(pltpu.get_barrier_semaphore(), 3 + neighbours)
+
+    gain_mate = remote(
+        gains_ref, gain_in.at[0], gain_send.at[0], gain_recv.at[0], fsdp=mate
+    )
+    gain_across = remote(
+        gain_in.at[2], gain_in.at[1], gain_send.at[1], gain_recv.at[1], fsdp=across
+    )
+    token_copy = remote(
+        tokens_ref.at[1 - side], tokens_own.at[side], token_send, token_recv, tp=1 - side
+    )
+    cot_copies = [
+        remote(
+            cotangent_ref.at[1 - side], cotangent_own.at[side], cot_send.at[0], cot_recv.at[0],
+            tp=1 - side,
+        ),
+        remote(
+            cotangent_ref.at[side], cotangent_other.at[side], cot_send.at[1], cot_recv.at[1],
+            tp=1 - side,
+        ),
+    ]
+
+    def y_copy(w):
+        return remote(
+            weights[w], full[w].at[rank], y_send.at[w], y_recv.at[w], fsdp=across
+        )
+
+    def mate_copy(w):
+        return remote(
+            weights[w], full[w].at[rank], mate_send.at[w], mate_recv.at[w], fsdp=mate
+        )
+
+    def pass_copy(w):
+        return remote(
+            full[w].at[across], full[w].at[across], pass_send.at[w], pass_recv.at[w], fsdp=mate
+        )
+
+    gain_mate.start()
+    token_copy.start()
+    for w in (1, 0):
+        y_copy(w).start()
+        mate_copy(w).start()
+    gain_mate.wait_recv()
+    gain_in[2] = gains_ref[...] + gain_in[0]
+    gain_across.start()
+    gain_across.wait_recv()
+    gains = gain_in[1] + gain_in[2]
+    gains_out[...] = gains
+    gain = wide(gains[:1])
+
+    def norm_rows(slot):
+        rows = wide(tokens_own[slot])
+        unit, inverse = normalize(rows)
+        normed_out[slot] = low(unit * gain)
+
+    local[0].wait()
+    norm_rows(side)
+    token_copy.wait_recv()
+    norm_rows(1 - side)
+    for copy in cot_copies:
+        copy.start()
+    for w in (1, 0):
+        y_copy(w).wait_recv()
+        pass_copy(w).start()
+    for w in range(2, len(weights)):
+        y_copy(w).start()
+        mate_copy(w).start()
+    normed = normed_out[...].reshape(2 * part_rows, -1)
+    cosine, sine = cosine_ref[...], sine_ref[...]
+
+    def turned(value, target):
+        target[:HALF] = low(value[:HALF] * cosine - value[HALF:] * sine)
+        target[HALF:] = low(value[HALF:] * cosine + value[:HALF] * sine)
+
+    def key_copy(s, j):
+        return remote(
+            keyval_ref.at[s, j], keyval_ref.at[s + 1, j], key_send.at[s, j], key_recv.at[s, j],
+            ctx=place + 1,
+        )
+
+    def arrived(w):
+        local[3 + w].wait()
+        mate_copy(w).wait_recv()
+        pass_copy(w).wait_recv()
+
+    arrived(1)
+    matrix = full[1][...].reshape(-1, 2 * KEY_WIDTH)
+    raw[: 2 * KEY_WIDTH] = dot(matrix, normed, 0, 1)
+    for j in range(KEYVAL_HEADS):
+        turned(raw[j * HEAD_WIDTH : (j + 1) * HEAD_WIDTH], keyval_ref.at[0, j, 0])
+        first = KEY_WIDTH + j * HEAD_WIDTH
+        keyval_ref[0, j, 1] = low(raw[first : first + HEAD_WIDTH])
+
+        @pl.when(place < last)
+        def _(j=j):
+            key_copy(0, j).start()
+
+    arrived(0)
+    matrix = full[0][...].reshape(-1, QUERY_WIDTH)
+    raw[...] = dot(matrix, normed, 0, 1)
+
+    def turn_query(h, carry):
+        value = raw[pl.ds(pl.multiple_of(h * HEAD_WIDTH, HEAD_WIDTH), HEAD_WIDTH)]
+        first = low(value[:HALF] * cosine - value[HALF:] * sine)
+        second = low(value[HALF:] * cosine + value[:HALF] * sine)
+        query_out[h, :HALF] = first * jnp.bfloat16(SCALE)
+        query_out[h, HALF:] = second * jnp.bfloat16(SCALE)
+        return carry
+
+    lax.fori_loop(0, QUERY_HEADS, turn_query, 0)
+
+    def attend(s, j, masked):
+        keys_turned = keyval_ref[s, j, 0].T
+        values = keyval_ref[s, j, 1]
+        for g in range(GROUP):
+            head = GROUP * j + g
+            scores = dot(keys_turned, query_out[head], 1, 0)
+            if masked:
+                scores = causal(scores)
+                top = jnp.max(scores, 0, keepdims=True)
+                lifted = jnp.exp(scores - top)
+                tops[head] = top
+                totals[head] = jnp.sum(lifted, 0, keepdims=True)
+                sums[head] = dot(values, low(lifted), 1, 0)
+            else:
+                old = tops[head]
+                top = jnp.maximum(old, jnp.max(scores, 0, keepdims=True))
+                lifted = jnp.exp(scores - top)
+                shrink = jnp.exp(old - top)
+                tops[head] = top
+                totals[head] = totals[head] * shrink + jnp.sum(lifted, 0, keepdims=True)
+                sums[head] = sums[head] * shrink + dot(values, low(lifted), 1, 0)
+
+    def hand_on(s, j):
+        @pl.when(s < place)
+        def _():
+            pltpu.make_async_copy(
+                keyval_ref.at[s + 1, j], keyval_ref.at[s + 1, j], key_recv.at[s, j]
+            ).wait()
+
+            @pl.when(place < last)
+            def _():
+                key_copy(s + 1, j).start()
+
+    def first_block(j, carry):
+        attend(0, j, True)
+        hand_on(0, j)
+        return carry
+
+    lax.fori_loop(0, KEYVAL_HEADS, first_block, 0)
+    passed = 2
+
+    def later_block(i, carry):
+        s = 1 + i // KEYVAL_HEADS
+        j = lax.rem(i, KEYVAL_HEADS)
+        attend(s, j, False)
+        hand_on(s, j)
+        return carry
+
+    lax.fori_loop(0, place * KEYVAL_HEADS, later_block, 0)
+
+    def divide(h, carry):
+        total = totals[h]
+        mixed_out[h] = low(sums[h] / total)
+        lse_ref[h] = tops[h] + jnp.log(total)
+        return carry
+
+    lax.fori_loop(0, QUERY_HEADS, divide, 0)
+
+    for w in range(passed, len(weights)):
+        y_copy(w).wait_recv()
+        pass_copy(w).start()
+    local[1].wait()
+    local[2].wait()
+    gain_mate.wait_send()
+    gain_across.wait_send()
+    token_copy.wait_send()
+    for copy in cot_copies:
+        copy.wait()
+    for w in range(passed, len(weights)):
+        arrived(w)
+    for w in range(len(weights)):
+        y_copy(w).wait_send()
+        mate_copy(w).wait_send()
+        pass_copy(w).wait_send()
+
+    @pl.when(place < last)
+    def _():
+        def sent(i, carry):
+            key_copy(i // KEYVAL_HEADS, lax.rem(i, KEYVAL_HEADS)).wait_send()
+            return carry
+
+        lax.fori_loop(0, (place + 1) * KEYVAL_HEADS, sent, 0)
+
+
+def front(tokens, cotangent, gains, cosine, sine, weights):
+    blocks = lax.axis_size("ctx")
+    parts = lax.axis_size("fsdp")
+    positions = cosine.shape[-1]
+    vmem = pl.BlockSpec(memory_space=pltpu.VMEM)
+    anywhere = pl.BlockSpec(memory_space=pl.ANY)
+    dma = pltpu.SemaphoreType.DMA
+    shape = lambda *dims: jax.ShapeDtypeStruct(dims, jnp.bfloat16)
+    count = len(weights)
+    area = QUERY_HEADS * positions * positions * blocks
+    return pl.pallas_call(
+        front_kernel,
+        in_specs=[anywhere, anywhere, vmem, vmem, vmem] + [anywhere] * count,
+        out_specs=[vmem, anywhere, anywhere] + [vmem] * 6 + [vmem] * 2 + [anywhere] * 4,
+        out_shape=[
+            shape(*tokens.shape), shape(*tokens.shape), shape(*tokens.shape),
+            shape(*gains.shape), shape(*tokens.shape),
+            shape(QUERY_HEADS, HEAD_WIDTH, positions),
+            shape(blocks, KEYVAL_HEADS, 2, HEAD_WIDTH, positions),
+            shape(QUERY_HEADS, HEAD_WIDTH, positions),
+            jax.ShapeDtypeStruct((QUERY_HEADS, 1, positions), jnp.float32),
+        ] + [shape(parts, *w.shape) for w in weights],
+        scratch_shapes=[
+            pltpu.VMEM((3,) + gains.shape, jnp.bfloat16),
+            pltpu.VMEM((QUERY_WIDTH, positions), jnp.float32),
+            pltpu.VMEM((QUERY_HEADS, 1, positions), jnp.float32),
+            pltpu.VMEM((QUERY_HEADS, 1, positions), jnp.float32),
+            pltpu.VMEM((QUERY_HEADS, HEAD_WIDTH, positions), jnp.float32),
+            dma((3 + count,)),
+            dma((2,)), dma((2,)),
+            dma, dma,
+            dma((2,)), dma((2,)),
+            dma((count,)), dma((count,)),
+            dma((count,)), dma((count,)),
+            dma((count,)), dma((count,)),
+            dma((blocks, KEYVAL_HEADS)), dma((blocks, KEYVAL_HEADS)),
+        ],
+        compiler_params=pltpu.CompilerParams(
+            vmem_limit_bytes=KERNEL_VMEM, collective_id=2, has_side_effects=True
+        ),
+        cost_estimate=pl.CostEstimate(
+            flops=16 * HEAD_WIDTH * area, bytes_accessed=10 * tokens.size, transcendentals=area
+        ),
+        name="front",
+    )(tokens, cotangent, gains, cosine, sine, *weights)
 
 
 def on_device(
@@ -956,39 +1295,33 @@
     def take(value_rows, index):
         return lax.dynamic_index_in_dim(value_rows, index, 0, keepdims=False)
 
-    tokens_own = in_order(take(tokens, half), to_partner(take(tokens, 1 - half)))
-    full_gain_one, full_gain_two = (
-        lax.all_gather(input_gain, "fsdp", axis=0, tiled=True),
-        lax.all_gather(middle_gain, "fsdp", axis=0, tiled=True),
-    )
-    full_in = lax.all_gather(jnp.concatenate([w_query, w_keyval], 1), "fsdp", axis=0, tiled=True)
-    full_output = lax.all_gather(w_output, "fsdp", axis=0, tiled=True)
-    full_gate = lax.all_gather(w_gate, "fsdp", axis=0, tiled=True)
-    full_up = lax.all_gather(w_up, "fsdp", axis=0, tiled=True)
-    full_down = lax.all_gather(w_down, "fsdp", axis=0, tiled=True)
-    cotangent_received = to_partner(cotangent)
-    cotangent_own = in_order(take(cotangent, half), take(cotangent_received, half))
-    cotangent_other = in_order(take(cotangent, 1 - half), take(cotangent_received, 1 - half))
-
-    token_positions = tokens_own.shape[0]
+    parts = lax.axis_size("fsdp")
+    width_in = tokens.shape[-1]
+    rows = width_in // parts
+    token_positions = 2 * tokens.shape[1]
     cosine, sine = rope_tables(token_positions, lax.axis_index("ctx") * token_positions)
-    gain_one = full_gain_one.astype(jnp.float32)
+    gains = lax.dynamic_update_slice(
+        jnp.zeros((16, width_in), jnp.bfloat16), jnp.stack([input_gain, middle_gain]),
+        (0, lax.axis_index("fsdp") * rows),
+    )
+    (
+        tokens_own, cotangent_own, cotangent_other, gains, normed_one, query_low, keyval,
+        mixed_heads, lse, *full,
+    ) = front(
+        tokens, cotangent, gains, cosine, sine,
+        (w_query, w_keyval, w_output, w_gate, w_up, w_down),
+    )
+    full_query, full_keyval, full_output, full_gate, full_up, full_down = [
+        w.reshape(width_in, -1) for w in full
+    ]
+    tokens_own, cotangent_own, cotangent_other, normed_one = [
+        v.reshape(token_positions, width_in)
+        for v in (tokens_own, cotangent_own, cotangent_other, normed_one)
+    ]
+    gain_one = gains[0].astype(jnp.float32)
+    full_gain_two = gains[1]
     inputs = tokens_own.astype(jnp.float32)
     unit_one, inverse_one = normalize(inputs)
-    normed_one = (unit_one * gain_one).astype(jnp.bfloat16)
-    keyval_raw = dot(full_in[:, QUERY_WIDTH:], normed_one, 0, 1)
-    keyval_low = jnp.concatenate(
-        [apply_rotary(keyval_raw[:KEY_WIDTH], cosine, sine), keyval_raw[KEY_WIDTH:]], 0
-    ).astype(jnp.bfloat16)
-    blocks = lax.axis_size("ctx")
-    keyval = jnp.stack([keyval_low] + [move_along(keyval_low, s) for s in range(1, blocks)], 0)
-    keyval = keyval.reshape(blocks, 2, KEYVAL_HEADS, HEAD_WIDTH, token_positions)
-    query_raw = dot(full_in[:, :QUERY_WIDTH], normed_one, 0, 1)
-    query_low = (
-        (apply_rotary(query_raw, cosine, sine).astype(jnp.bfloat16) * jnp.bfloat16(SCALE))
-        .reshape(QUERY_HEADS, HEAD_WIDTH, token_positions)
-    )
-    mixed_heads, lse = attend_forward(query_low, keyval, True)
     mixed_low = mixed_heads.reshape(QUERY_WIDTH, token_positions)
     middle = inputs + dot(mixed_low, full_output, 0, 0)
 
@@ -1045,15 +1378,11 @@
     back_query, back_keyval, share = backward_sum(
         query_low, keyval, back_mixed, mixed_heads, lse, cosine, sine, gradients
     )
-    back_in = jnp.concatenate(
-        [
-            back_query.reshape(QUERY_WIDTH, token_positions),
-            back_keyval.reshape(2 * KEY_WIDTH, token_positions),
-        ],
-        0,
-    )
-    grad_in = dot(normed_one, back_in, 0, 1)
-    back_one = dot(back_in, full_in, 0, 1)
+    back_query = back_query.reshape(QUERY_WIDTH, token_positions)
+    back_keyval = back_keyval.reshape(2 * KEY_WIDTH, token_positions)
+    grad_query = dot(normed_one, back_query, 0, 1).astype(jnp.bfloat16)
+    grad_keyval = dot(normed_one, back_keyval, 0, 1).astype(jnp.bfloat16)
+    back_one = dot(back_query, full_query, 0, 1) + dot(back_keyval, full_keyval, 0, 1)
     grad_gain_one = jnp.sum(back_one * unit_one, axis=0)
     back_inputs = back_middle + norm_back(back_one * gain_one, unit_one, inverse_one)
 
@@ -1064,18 +1393,17 @@
 
     result = to_positions(result_own)
     grad_tokens = to_positions(back_inputs.astype(jnp.bfloat16)).astype(jnp.float32)
-    parts = lax.axis_size("fsdp")
-    rows = grad_output.shape[0] // parts
-    width = QUERY_WIDTH + full_in.shape[1]
+    width = 2 * QUERY_WIDTH + 2 * KEY_WIDTH
     gains = jnp.concatenate(
         [grad_gain_one.reshape(parts, rows), grad_gain_two.reshape(parts, rows)], 1
     )
     gains = jnp.pad(gains[:, None], ((0, 0), (0, 15), (0, width - 2 * rows)))
-    summed = jnp.concatenate([grad_output, grad_in.astype(jnp.bfloat16)], 1)
+    summed = jnp.concatenate([grad_output, grad_query, grad_keyval], 1)
     summed = jnp.concatenate(
         [summed.reshape(parts, rows, width), gains.astype(jnp.bfloat16)], 1
     )
-    share_in = gradient_sum(summed).astype(jnp.float32)
+    share_in, share_rest = gradient_sum(summed, share)
+    share_in = share_in.astype(jnp.float32)
     return (
         result,
         grad_tokens,
@@ -1084,8 +1412,8 @@
         share_in[:rows, 2 * QUERY_WIDTH :],
         share_in[:rows, :QUERY_WIDTH],
         share_in[rows, rows : 2 * rows],
-        share[1].astype(jnp.float32),
-        share[2].astype(jnp.float32),
+        share_rest[0].astype(jnp.float32),
+        share_rest[1].astype(jnp.float32),
         share[0].astype(jnp.float32),
     )
 

time: 450 us -> 450 us (level)
  Pallas kernels: 201 us -> 273 us
  waiting for transfers between devices: 87.7 us -> 42.7 us
  between operations: 15.6 us -> 1.61 us
  local copies, waits for them, and re-layouts: 19 us -> 32.9 us
  starting transfers between devices: 18.7 us -> 7.25 us
  matrix products: 73 us -> 66 us
  blocking collectives: 6.92 us -> 0 us
    pallas_call x1, Pallas kernels: 7.75 us -> 109 us  [front(): pl.pallas_call(front_kernel, in_specs=[anywhere, anywhere, vmem, vmem, vm...]
    pallas_call x1, Pallas kernels: 134 us -> 90.3 us  [backward_sum(): pl.pallas_call(backward_sum_kernel, in_specs=[vmem] * 7 + [pl.BlockSpec(m...]
    ppermute x3 -> x0, waiting for transfers between devices: 35.5 us -> none  [move_along(): return lax.ppermute(value, 'ctx', pairs)]
    all_gather x5 -> x0, waiting for transfers between devices: 19.3 us -> none  [the longest x1 19.3 us: fast_on_device(): full_down = lax.all_gather(w_down, 'fsdp', axis=0, tiled=True)]
    pallas_call x1, Pallas kernels: 59.2 us -> 74 us  [gradient_sum(): pl.pallas_call(gradient_sum_kernel, in_specs=[pl.BlockSpec(memory_space=p...]
    ppermute x7 -> x5, waiting for transfers between devices: 31 us -> 42.7 us  [to_partner(): return lax.ppermute(value_rows, 'tp', pair)]
    ppermute x3 -> x0, starting transfers between devices: 9.71 us -> none  [move_along(): return lax.ppermute(value, 'ctx', pairs)]
    concatenate x1, local copies, waits for them, and re-layouts: 0.04 us -> 8.84 us  [fast_on_device(): summed = jnp.concatenate([grad_output, grad_query, grad_keyval], 1)]
  transfers between devices with their start and end apart: 15 -> 5, of which waited for: 7 -> 3; matrix products, arithmetic and copies ran while one was open for 19% -> 11% of each run, Pallas kernels for 45% -> 0%
where the time goes in v2:
time: 450 us; the launch traced here: 443 us
  Pallas kernels  273 us (61%)
  matrix products  66 us (15%)
  waiting for transfers between devices  42.7 us (9%)
  local copies, waits for them, and re-layouts  32.9 us (7%)
  other arithmetic  18.9 us (4%)
  starting transfers between devices  7.25 us (2%)
    pallas_call x1, Pallas kernels, front(): pl.pallas_call(front_kernel, in_specs=[anywhere, anywhere, vmem, vmem, vm...  109 us
    pallas_call x1, Pallas kernels, backward_sum(): pl.pallas_call(backward_sum_kernel, in_specs=[vmem] * 7 + [pl.BlockSpec(m...  90.3 us
    pallas_call x1, Pallas kernels, gradient_sum(): pl.pallas_call(gradient_sum_kernel, in_specs=[pl.BlockSpec(memory_space=p...  74 us
    dot_general x25, matrix products, dot(): lax.dot_general(left, right, (((left_dim,), (right_dim,)), ((), ())), pre...  66 us
    ppermute x5, waiting for transfers between devices, to_partner(): return lax.ppermute(value_rows, 'tp', pair)  42.7 us
  transfers between devices with their start and end apart: 5, of which 3 were waited for; matrix products, arithmetic and copies ran while one was open for 11% of the time, Pallas kernels for 0%

profile of v2, /device:TPU:0, one launch (start us, length us, event | category | flops | bytes accessed | tf_op | source)
XLA Modules:
  0.0 442.8 jit_solution(6648825372539150321)
XLA Ops:
  7.6 109.2 %front.1 = (bf16[2,256,960]{2,1,0:T(8,128)(2,1)}, bf16[2,256,960]{2,1,0:T(8,128)(2,1)}, bf16[2,256,960]{2,1,0:T(8,128)(2,1)}, bf16[16,960]{1,0:T(8,128)(2,1)}, b...) custom-call(bf16[2,256,960]{2,1,0:T(8,128)(2,1)} %copy.27.tokens_ref, ...), custom_call_target="tpu_custom_call" | custom-call | flops 16106127360 | bytes 4915200 | tf_op jit(solution)/shard_map/front/pallas_call | solution.py:1086
  120.2 3.4 multiply_reduce_fusion.5
  125.1 3.0 collective-permute-start
  129.6 2.7 copy.32
  138.4 3.7 fusion.14
  142.1 3.7 fusion.16
  145.8 3.7 fusion.15
  149.5 3.7 fusion.11
  154.8 2.9 fusion.10
  157.7 4.0 multiply_convert_fusion
  168.4 4.3 add_convert_fusion
  172.7 4.2 add_convert_fusion.1
  176.9 3.0 add_convert_fusion.2
  179.9 29.4 %collective-permute-done.3 = bf16[512,960]{0,1:T(8,128)(2,1)S(1)} collective-permute-done((bf16[512,960]{0,1:T(8,128)(2,1)S(1)}, bf16[512,960]{0,1:T(8,128)(2,1)S(1)}, u32[]{:S(2)}, u32[]{:S(2)}) %collective-permute-start.3) | collective-permute-done | bytes 983072 | tf_op jit(solution)/shard_map/ppermute | solution.py:1288
  219.2 90.3 %backward_sum.1 = (bf16[15,64,512]{2,1,0:T(8,128)(2,1)}, bf16[2,5,64,512]{3,2,1,0:T(8,128)(2,1)}, bf16[3,240,1280]{2,1,0:T(8,128)(2,1)}) custom-call(bf16[15,64,512]{2,1,0:T(8,128)(2,1)} %get-tuple-element.39.query_ref, bf16[4,5,2,64,512]{4,3,2,1,0:T(8,128)(2,1)} %get-tuple-element.40.keyval_ref, bf16[15,64,512]{2,1,0:T(8,128)(2,1)} %bitcast.150, ...), custom_call_target="tpu_custom_call" | custom-call | flops 40265318400 | bytes 4915200 | tf_op jit(solution)/shard_map/backward_sum/pallas_call | solution.py:580
  312.1 2.7 convolution_convert_fusion
  319.4 3.6 add_convert_fusion.3
  325.7 8.8 %concatenate.18 = bf16[960,2560]{1,0:T(8,128)(2,1)} concatenate(bf16[960,960]{1,0:T(8,128)(2,1)} %convolution_convert_fusion.1, bf16[960,960]{1,0:T(8,128)(2,1)} %convolution_convert_fusion, bf16[960,640]{1,0:T(8,128)(2,1)S(1)} %copy-done.16), dimensions={1} | concatenate | bytes 9830400 | tf_op jit(solution)/shard_map/concatenate | solution.py:1401
  334.6 5.1 %fusion.1.value_ref = bf16[4,256,2560]{2,1,0:T(8,128)(2,1)} fusion(bf16[4,1,480]{2,1,0:T(2,128)(2,1)S(1)} %copy.36, bf16[4,240,2560]{2,1,0:T(8,128)(2,1)} %bitcast.109), kind=kLoop, calls=%fused_computation.2 | loop fusion | flops 15728640 | bytes 10161920 | tf_op jit(solution)/shard_map/concatenate | solution.py:1402
  339.7 74.0 %gradient_sum.1 = (bf16[256,2560]{1,0:T(8,128)(2,1)}, bf16[2,240,1280]{2,1,0:T(8,128)(2,1)}) custom-call(bf16[4,256,2560]{2,1,0:T(8,128)(2,1)} %fusion.1.value_ref, bf16[3,240,1280]{2,1,0:T(8,128)(2,1)} %get-tuple-element.47.feed_ref), custom_call_target="tpu_custom_call" | custom-call | flops 2621440 | bytes 10485760 | tf_op jit(solution)/shard_map/gradient_sum/pallas_call | solution.py:797
  413.7 3.4 bitcast_convert_fusion.1
  417.1 4.1 constant_dynamic-slice_fusion.1
  426.5 9.1 %collective-permute-done.2 = bf16[256,960]{0,1:T(8,128)(2,1)S(1)} collective-permute-done((bf16[256,960]{0,1:T(8,128)(2,1)S(1)}, bf16[256,960]{0,1:T(8,128)(2,1)S(1)}, u32[]{:S(2)}, u32[]{:S(2)}) %collective-permute-start.2) | collective-permute-done | bytes 491552 | tf_op jit(solution)/shard_map/ppermute | solution.py:1288
  436.7 4.2 collective-permute-done.4
  (128 shorter events, 55.1 us)
Async XLA Ops:
  0.6 3.7 copy-start.17
  116.8 3.4 copy-start.26
  125.1 7.2 %copy-start = (bf16[4,240,1280]{2,1,0:T(8,128)(2,1)S(1)}, bf16[4,240,1280]{2,1,0:T(8,128)(2,1)}, u32[]{:S(2)}) copy-start(bf16[4,240,1280]{2,1,0:T(8,128)(2,1)} %get-tuple-element.35) | copy-start | bytes 7372804
  125.1 29.7 %collective-permute-start = (bf16[512,960]{0,1:T(8,128)(2,1)S(1)}, bf16[512,960]{0,1:T(8,128)(2,1)}, u32[]{:S(2)}, u32[]{:S(2)}) collective-permute-start(bf16[512,960]{0,1:T(8,128)(2,1)S(1)} %multiply_convert_fusion.6), channel_id=1, source_target_pairs={{0,1},{1,0},{2,3},{3,2},{4,5},{5,4},{6,7},{7,6},{8,9},{9,8},{10,11... | collective-permute-start | bytes 2949128 | tf_op jit(solution)/shard_map/ppermute | solution.py:1288
  138.3 3.8 copy-start.12
  138.3 3.8 copy-start.5
  138.3 7.5 %copy-start.14 = (bf16[512,1280]{1,0:T(8,128)(2,1)}, bf16[512,1280]{1,0:T(8,128)(2,1)S(1)}, u32[]{:S(2)}) copy-start(bf16[512,1280]{1,0:T(8,128)(2,1)S(1)} %get-tuple-element.55) | copy-start | bytes 3932164
  149.5 3.7 copy-start.21
  149.5 3.7 copy-start.25
  161.7 6.6 %slice-start.2 = ((s8[4915200]{0:T(1024)(128)(4,1)}), s8[4194304]{0:T(1024)(128)(4,1)S(1)}, s32[]{:S(2)}) async-start(s8[4915200]{0:T(1024)(128)(4,1)} %bitcast.107), calls=%async_computation.2 | async-start | bytes 8388608
  163.2 5.2 %slice-start.3 = ((s8[4915200]{0:T(1024)(128)(4,1)}), s8[720896]{0:T(1024)(128)(4,1)S(1)}, s32[]{:S(2)}) async-start(s8[4915200]{0:T(1024)(128)(4,1)} %bitcast.107), calls=%async_computation.3 | async-start | bytes 1441792
  164.7 52.7 %collective-permute-start.1 = (bf16[512,960]{0,1:T(8,128)(2,1)S(1)}, bf16[512,960]{0,1:T(8,128)(2,1)S(1)}, u32[]{:S(2)}, u32[]{:S(2)}) collective-permute-start(bf16[512,960]{0,1:T(8,128)(2,1)S(1)} %convolution_convert_fusion.4), channel_id=1, source_target_pairs={{0,1},{1,0},{2,3},{3,2},{4,5},{5,4},{6,7},{7,6},{8,9},{9,8},{10,11... | collective-permute-start | bytes 2949128 | tf_op jit(solution)/shard_map/ppermute | solution.py:1288
  164.9 7.7 %slice-start = ((s8[4915200]{0:T(1024)(128)(4,1)}), s8[4194304]{0:T(1024)(128)(4,1)S(1)}, s32[]{:S(2)}) async-start(s8[4915200]{0:T(1024)(128)(4,1)} %bitcast.105), calls=%async_computation | async-start | bytes 8388608
  166.4 6.2 %slice-start.1 = ((s8[4915200]{0:T(1024)(128)(4,1)}), s8[720896]{0:T(1024)(128)(4,1)S(1)}, s32[]{:S(2)}) async-start(s8[4915200]{0:T(1024)(128)(4,1)} %bitcast.105), calls=%async_computation.1 | async-start | bytes 1441792
  166.4 42.9 %collective-permute-start.3 = (bf16[512,960]{0,1:T(8,128)(2,1)S(1)}, bf16[512,960]{0,1:T(8,128)(2,1)S(1)}, u32[]{:S(2)}, u32[]{:S(2)}) collective-permute-start(bf16[512,960]{0,1:T(8,128)(2,1)S(1)} %add_convert_fusion.4), channel_id=1, source_target_pairs={{0,1},{1,0},{2,3},{3,2},{4,5},{5,4},{6,7},{7,6},{8,9},{9,8},{10,11... | collective-permute-start | bytes 2949128 | tf_op jit(solution)/shard_map/ppermute | solution.py:1288
  168.4 8.5 %slice-start.4 = ((s8[4915200]{0:T(1024)(128)(4,1)}), s8[4194304]{0:T(1024)(128)(4,1)S(1)}, s32[]{:S(2)}) async-start(s8[4915200]{0:T(1024)(128)(4,1)} %bitcast.110), calls=%async_computation.4 | async-start | bytes 8388608
  172.7 4.2 slice-start.5
  176.9 32.5 %copy-start.2 = (f32[512,960]{0,1:T(8,128)S(1)}, f32[512,960]{0,1:T(8,128)}, u32[]{:S(2)}) copy-start(f32[512,960]{0,1:T(8,128)} %copy-done.1) | copy-start | bytes 5898244
  176.9 32.5 %copy-start.6 = (bf16[512,1280]{1,0:T(8,128)(2,1)S(1)}, bf16[512,1280]{1,0:T(8,128)(2,1)}, u32[]{:S(2)}) copy-start(bf16[512,1280]{1,0:T(8,128)(2,1)} %copy-done.5) | copy-start | bytes 3932164
  179.9 31.4 %copy-start.9 = (bf16[512,960]{0,1:T(8,128)(2,1)S(1)}, bf16[512,960]{0,1:T(8,128)(2,1)}, u32[]{:S(2)}) copy-start(bf16[512,960]{0,1:T(8,128)(2,1)} %copy.32) | copy-start | bytes 2949124
  212.5 4.9 %copy-start.4 = (f32[512,960]{0,1:T(8,128)}, f32[512,960]{0,1:T(8,128)S(1)}, u32[]{:S(2)}) copy-start(f32[512,960]{0,1:T(8,128)S(1)} %multiply_add_fusion) | copy-start | bytes 5898244
  219.2 90.3 %copy-start.22 = (bf16[4,240,960]{2,1,0:T(8,128)(2,1)S(1)}, bf16[4,240,960]{2,1,0:T(8,128)(2,1)}, u32[]{:S(2)}) copy-start(bf16[4,240,960]{2,1,0:T(8,128)(2,1)} %get-tuple-element.43) | copy-start | bytes 5529604
  421.4 14.2 %collective-permute-start.2 = (bf16[256,960]{0,1:T(8,128)(2,1)S(1)}, bf16[256,960]{0,1:T(8,128)(2,1)S(1)}, u32[]{:S(2)}, u32[]{:S(2)}) collective-permute-start(bf16[256,960]{0,1:T(8,128)(2,1)S(1)} %bitcast.126), channel_id=1, source_target_pairs={{0,1},{1,0},{2,3},{3,2},{4,5},{5,4},{6,7},{7,6},{8,9},{9,8},{10,11... | collective-permute-start | bytes 1474568 | tf_op jit(solution)/shard_map/ppermute | solution.py:1288
  422.2 18.7 %collective-permute-start.4 = (bf16[256,960]{0,1:T(8,128)(2,1)S(1)}, bf16[256,960]{0,1:T(8,128)(2,1)S(1)}, u32[]{:S(2)}, u32[]{:S(2)}) collective-permute-start(bf16[256,960]{0,1:T(8,128)(2,1)S(1)} %bitcast.125), channel_id=1, source_target_pairs={{0,1},{1,0},{2,3},{3,2},{4,5},{5,4},{6,7},{7,6},{8,9},{9,8},{10,11... | collective-permute-start | bytes 1474568 | tf_op jit(solution)/shard_map/ppermute | solution.py:1288
  (16 other events, 33.2 us)

commit v3 on v2

--- a/solution.py
+++ b/solution.py
@@ -300,11 +300,11 @@
 
 def backward_sum_kernel(
     query_ref, keyval_ref, back_ref, mixed_ref, lse_ref, cosine_ref, sine_ref,
-    down_ref, gate_ref, up_ref,
-    back_query_ref, back_keyval_ref, share_ref,
+    base_ref, feed_ref, down_ref, gate_ref, up_ref,
+    back_query_ref, back_keyval_ref, share_ref, result_ref,
     own, mate_in, y_in, up_in, parts, part_out, part_in, back_total, row_sums,
     own_sem, mate_send, mate_recv, y_send, y_recv, up_send, up_recv, down_send, down_recv,
-    part_send, part_recv,
+    part_send, part_recv, feed_in, traded, feed_send, feed_recv, trade_send, trade_recv,
 ):
     place = lax.axis_index("ctx")
     last = lax.axis_size("ctx") - 1
@@ -312,6 +312,7 @@
     rank = lax.axis_index("fsdp")
     core = rank % 2
     y = rank // 2
+    side = lax.axis_index("tp")
     mate = rank + 1 - 2 * core
     across = rank + 2 - 4 * y
     gradients = (down_ref, gate_ref, up_ref)
@@ -327,6 +328,7 @@
             ).start()
     greet(fsdp=mate)
     greet(fsdp=across)
+    greet(tp=1 - side)
 
     @pl.when(place > 0)
     def _():
@@ -337,7 +339,26 @@
         greet(ctx=place + 1)
 
     neighbours = (place + last - 1) // last + (2 * last - place - 1) // last
-    pl.semaphore_wait(pltpu.get_barrier_semaphore(), 2 + neighbours)
+    pl.semaphore_wait(pltpu.get_barrier_semaphore(), 3 + neighbours)
+
+    feed_copy = remote(feed_ref, feed_in, feed_send, feed_recv, tp=1 - side)
+    trade_copy = remote(traded, result_ref.at[side], trade_send, trade_recv, tp=1 - side)
+    feed_copy.start()
+    width = traded.shape[-1]
+    step_rows = traded.shape[0] // 4
+
+    def finish_result():
+        feed_copy.wait_recv()
+
+        def some_rows(i, carry):
+            at = pl.ds(pl.multiple_of(i * step_rows, step_rows), step_rows)
+            for target, slot in ((result_ref.at[side], side), (traded, 1 - side)):
+                columns = pl.ds(pl.multiple_of(slot * width, width), width)
+                target[at] = low(base_ref[at, columns] + wide(feed_in[at, columns]))
+            return carry
+
+        lax.fori_loop(0, 4, some_rows, 0)
+        trade_copy.start()
 
     def chunk_at(ref, m, r, *front):
         return ref.at[(m,) + front + (pl.ds(r * CHUNK_ROWS, CHUNK_ROWS),)]
@@ -429,6 +450,10 @@
         @pl.when(t < chunks)
         def _():
             to_across(t)
+
+        @pl.when(t == chunks)
+        def _():
+            finish_result()
 
         b = t - 3 - 2 * place
 
@@ -566,9 +591,11 @@
         return carry
 
     lax.fori_loop(0, KEYVAL_HEADS, finish_parts, 0)
-
-
-def backward_sum(query, keyval, back_mixed, mixed, lse, cosine, sine, gradients):
+    feed_copy.wait_send()
+    trade_copy.wait()
+
+
+def backward_sum(query, keyval, back_mixed, mixed, lse, cosine, sine, base, feed, gradients):
     blocks, positions = keyval.shape[0], keyval.shape[-1]
     count, rows, columns = gradients[0].shape
     chunks = len(gradients) * rows // CHUNK_ROWS
@@ -579,12 +606,13 @@
     head = (2, HEAD_WIDTH, positions)
     return pl.pallas_call(
         backward_sum_kernel,
-        in_specs=[vmem] * 7 + [pl.BlockSpec(memory_space=pl.ANY)] * 3,
-        out_specs=[vmem] * 3,
+        in_specs=[vmem] * 9 + [pl.BlockSpec(memory_space=pl.ANY)] * 3,
+        out_specs=[vmem] * 4,
         out_shape=[
             jax.ShapeDtypeStruct(query.shape, jnp.bfloat16),
             jax.ShapeDtypeStruct((2, KEYVAL_HEADS, HEAD_WIDTH, positions), jnp.bfloat16),
             jax.ShapeDtypeStruct(share, jnp.bfloat16),
+            jax.ShapeDtypeStruct((2, feed.shape[0], positions // 2), jnp.bfloat16),
         ],
         scratch_shapes=[
             pltpu.VMEM((len(gradients), 2, rows, columns), jnp.bfloat16),
@@ -602,6 +630,9 @@
             dma((chunks,)), dma((chunks,)),
             dma((rows // CHUNK_ROWS,)), dma((rows // CHUNK_ROWS,)),
             dma((KEYVAL_HEADS, blocks - 1)), dma((KEYVAL_HEADS, blocks - 1)),
+            pltpu.VMEM(feed.shape, jnp.bfloat16),
+            pltpu.VMEM((feed.shape[0], positions // 2), jnp.bfloat16),
+            dma, dma, dma, dma,
         ],
         compiler_params=pltpu.CompilerParams(
             vmem_limit_bytes=KERNEL_VMEM, collective_id=0, has_side_effects=True
@@ -610,34 +641,59 @@
             flops=40 * HEAD_WIDTH * area, bytes_accessed=10 * query.size, transcendentals=area
         ),
         name="backward_sum",
-    )(query, keyval, back_mixed, mixed, lse, cosine, sine, *gradients)
-
-
-def gradient_sum_kernel(
-    value_ref, feed_ref, share_ref, feed_share_ref,
-    own, mate_in, y_out, y_in, x_out, x_in, z_out, z_in,
-    own_sem, mate_send, mate_recv, y_send, y_recv, x_send, x_recv, z_send, z_recv,
-    all_send, all_recv, back_send, back_recv, down_send, down_recv, feed_sem,
-):
+    )(query, keyval, back_mixed, mixed, lse, cosine, sine, base, feed, *gradients)
+
+
+def gradient_sum_kernel(out_ref, query_ref, keyval_ref, gains_ref, feed_ref, back_ref, *refs):
+    values = (out_ref, query_ref, keyval_ref)
+    chunks = len(values)
+    shares, (feed_share_ref, tokens_ref), refs = refs[:chunks], refs[chunks : chunks + 2], refs[chunks + 2 :]
+    own, mate_in, y_out, y_in, x_out, x_in, z_out, z_in = [
+        refs[i * chunks : (i + 1) * chunks] for i in range(8)
+    ]
+    (
+        own_sem, mate_send, mate_recv, y_send, y_recv, x_send, x_recv, z_send, z_recv,
+        all_send, all_recv, back_send, back_recv, down_send, down_recv, feed_sem,
+        token_send, token_recv, token_sem,
+    ) = refs[8 * chunks :]
     place = lax.axis_index("ctx")
     blocks = lax.axis_size("ctx")
+    last = blocks - 1
     rank = lax.axis_index("fsdp")
     side = lax.axis_index("tp")
     core = rank % 2
     y = rank // 2
     mate = rank + 1 - 2 * core
     across = rank + 2 - 4 * y
-    rows, columns = share_ref.shape
-    chunks = columns // WIDE
+    rows = shares[0].shape[0]
+    filled = values[0].shape[1]
     half_rows = rows // 2
     piece = half_rows // blocks
-
-    own_copies = [
-        pltpu.make_async_copy(value_ref.at[2 * half + core], own.at[half], own_sem.at[half])
-        for half in range(2)
-    ]
-    for copy in own_copies:
-        copy.start()
+    width = tokens_ref.shape[-1]
+
+    def columns(slot):
+        return back_ref.at[:, pl.ds(pl.multiple_of(slot * width, width), width)]
+
+    def own_copy(n, half):
+        return pltpu.make_async_copy(
+            values[n].at[2 * half + core], own[n].at[half, pl.ds(0, filled)], own_sem.at[n, half]
+        )
+
+    def own_gains(half):
+        return pltpu.make_async_copy(
+            gains_ref.at[2 * half + core], own[-1].at[half, pl.ds(filled, rows - filled)],
+            own_sem.at[chunks, half],
+        )
+
+    for half in range(2):
+        for n in range(chunks):
+            own_copy(n, half).start()
+        own_gains(half).start()
+    for n in range(chunks - 1):
+        tail = (2, rows - filled, own[n].shape[-1])
+        own[n][:, filled:] = jnp.zeros(tail, jnp.bfloat16)
+        mate_in[n][:, filled:] = jnp.zeros(tail, jnp.bfloat16)
+
     greet(fsdp=mate)
     greet(fsdp=across)
     greet(tp=1 - side)
@@ -647,41 +703,44 @@
 
     def mate_copy(n, half):
         return remote(
-            value_ref.at[2 * half + 1 - core, :, pl.ds(n * WIDE, WIDE)], mate_in.at[n, half],
+            values[n].at[2 * half + 1 - core], mate_in[n].at[half, pl.ds(0, filled)],
             mate_send.at[n, half], mate_recv.at[n, half], fsdp=mate,
         )
 
+    def mate_gains(half):
+        return remote(
+            gains_ref.at[2 * half + 1 - core], mate_in[-1].at[half, pl.ds(filled, rows - filled)],
+            mate_send.at[chunks, half], mate_recv.at[chunks, half], fsdp=mate,
+        )
+
     def y_copy(n):
-        return remote(y_out.at[n], y_in.at[n], y_send.at[n], y_recv.at[n], fsdp=across)
+        return remote(y_out[n], y_in[n], y_send.at[n], y_recv.at[n], fsdp=across)
 
     def x_copy(n):
         other = pl.ds(pl.multiple_of((1 - side) * half_rows, half_rows), half_rows)
-        return remote(
-            x_out.at[n, other], x_in.at[n], x_send.at[n], x_recv.at[n], tp=1 - side
-        )
+        return remote(x_out[n].at[other], x_in[n], x_send.at[n], x_recv.at[n], tp=1 - side)
 
     def z_copy(n, d):
         target = lax.rem(place + d, blocks)
         at = pl.ds(pl.multiple_of(target * piece, piece), piece)
         return remote(
-            z_out.at[n, at], z_in.at[n, d - 1], z_send.at[n, d - 1], z_recv.at[n, d - 1],
+            z_out[n].at[at], z_in[n].at[d - 1], z_send.at[n, d - 1], z_recv.at[n, d - 1],
             ctx=target,
         )
 
     def all_copy(n, d, origin):
-        at = pl.ds(pl.multiple_of(side * half_rows + origin * piece, piece), piece)
-        spot = share_ref.at[at, pl.ds(n * WIDE, WIDE)]
+        spot = shares[n].at[
+            pl.ds(pl.multiple_of(side * half_rows + origin * piece, piece), piece)
+        ]
         return remote(
             spot, spot, all_send.at[n, d - 1], all_recv.at[n, d - 1],
             ctx=lax.rem(place + d, blocks),
         )
 
     def back_copy(n, half):
-        at = pl.ds(pl.multiple_of(half * half_rows, half_rows), half_rows)
-        spot = share_ref.at[at, pl.ds(n * WIDE, WIDE)]
+        spot = shares[n].at[pl.ds(pl.multiple_of(half * half_rows, half_rows), half_rows)]
         return remote(spot, spot, back_send.at[n], back_recv.at[n], tp=1 - side)
 
-    last = blocks - 1
     per = feed_ref.shape[1] // CHUNK_ROWS
     returned = feed_share_ref.shape[0] * per
 
@@ -703,9 +762,17 @@
         def _():
             down_copy(k, feed_at(feed_share_ref, k, 0)).start()
 
+    token_copy = remote(
+        columns(1 - side), tokens_ref.at[side], token_send, token_recv, tp=1 - side
+    )
+    token_own = pltpu.make_async_copy(columns(side), tokens_ref.at[side], token_sem)
+
     for n in range(chunks):
         for half in range(2):
             mate_copy(n, half).start()
+    for half in range(2):
+        mate_gains(half).start()
+    token_own.start()
 
     @pl.when(place == last)
     def _():
@@ -713,37 +780,40 @@
             down_copy(k, feed_at(feed_ref, k, 1)).start()
         feed_copy.start()
 
-    for copy in own_copies:
-        copy.wait()
+    for half in range(2):
+        for n in range(chunks):
+            own_copy(n, half).wait()
+        own_gains(half).wait()
 
     def to_y(n):
         for half in range(2):
             mate_copy(n, half).wait_recv()
-        at = pl.ds(n * WIDE, WIDE)
-        y_out[n] = low(wide(own[1 - y, :, at]) + wide(mate_in[n, 1 - y]))
+            if n == chunks - 1:
+                mate_gains(half).wait_recv()
+        y_out[n][...] = low(wide(own[n][1 - y]) + wide(mate_in[n][1 - y]))
         y_copy(n).start()
+        if n == chunks - 1:
+            token_copy.start()
 
     def to_x(n):
         y_copy(n).wait_recv()
-        at = pl.ds(n * WIDE, WIDE)
-        x_out[n] = low(wide(own[y, :, at]) + wide(mate_in[n, y]) + wide(y_in[n]))
+        x_out[n][...] = low(wide(own[n][y]) + wide(mate_in[n][y]) + wide(y_in[n][...]))
         x_copy(n).start()
 
     def to_z(n):
         x_copy(n).wait_recv()
         at = pl.ds(pl.multiple_of(side * half_rows, half_rows), half_rows)
-        z_out[n] = low(wide(x_out[n, at]) + wide(x_in[n]))
+        z_out[n][...] = low(wide(x_out[n][at]) + wide(x_in[n][...]))
         for d in range(1, blocks):
             z_copy(n, d).start()
 
     def to_all(n):
-        at = pl.ds(pl.multiple_of(place * piece, piece), piece)
-        total = wide(z_out[n, at])
+        total = wide(z_out[n][pl.ds(pl.multiple_of(place * piece, piece), piece)])
         for d in range(1, blocks):
             z_copy(n, d).wait_recv()
-            total += wide(z_in[n, d - 1])
+            total += wide(z_in[n][d - 1])
         at = pl.ds(pl.multiple_of(side * half_rows + place * piece, piece), piece)
-        share_ref[at, pl.ds(n * WIDE, WIDE)] = low(total)
+        shares[n][at] = low(total)
         for d in range(1, blocks):
             all_copy(n, d, place).start()
 
@@ -784,64 +854,68 @@
             z_copy(n, d).wait_send()
             all_copy(n, d, place).wait_send()
         back_copy(n, side).wait_send()
-
-
-def gradient_sum(value, feed):
-    count, rows, columns = value.shape
+    for half in range(2):
+        mate_gains(half).wait_send()
+    token_own.wait()
+    token_copy.wait()
+
+
+def gradient_sum(values, gains, feed, back):
+    filled = values[0].shape[1]
+    rows = filled + gains.shape[1]
+    widths = [value.shape[-1] for value in values]
+    chunks = len(values)
     returned = (feed.shape[0] - 1) * feed.shape[1] // CHUNK_ROWS
     blocks = lax.axis_size("ctx")
-    chunks = columns // WIDE
     half_rows = rows // 2
     dma = pltpu.SemaphoreType.DMA
-    low_type = jnp.bfloat16
+    anywhere = pl.BlockSpec(memory_space=pl.ANY)
+    vmem = pl.BlockSpec(memory_space=pltpu.VMEM)
+    scratch = []
+    for front in ((2, rows), (2, rows), (rows,), (rows,), (rows,), (half_rows,), (half_rows,),
+                  (blocks - 1, half_rows // blocks)):
+        scratch += [pltpu.VMEM(front + (w,), jnp.bfloat16) for w in widths]
     return pl.pallas_call(
         gradient_sum_kernel,
-        in_specs=[pl.BlockSpec(memory_space=pl.ANY)] * 2,
-        out_specs=[pl.BlockSpec(memory_space=pltpu.VMEM)] * 2,
-        out_shape=[
-            jax.ShapeDtypeStruct((rows, columns), low_type),
-            jax.ShapeDtypeStruct((feed.shape[0] - 1,) + feed.shape[1:], low_type),
+        in_specs=[anywhere] * (chunks + 2) + [vmem],
+        out_specs=[vmem] * (chunks + 2),
+        out_shape=[jax.ShapeDtypeStruct((rows, w), jnp.bfloat16) for w in widths] + [
+            jax.ShapeDtypeStruct((feed.shape[0] - 1,) + feed.shape[1:], jnp.bfloat16),
+            jax.ShapeDtypeStruct((2, back.shape[0], back.shape[1] // 2), jnp.bfloat16),
         ],
-        scratch_shapes=[
-            pltpu.VMEM((2, rows, columns), low_type),
-            pltpu.VMEM((chunks, 2, rows, WIDE), low_type),
-            pltpu.VMEM((chunks, rows, WIDE), low_type),
-            pltpu.VMEM((chunks, rows, WIDE), low_type),
-            pltpu.VMEM((chunks, rows, WIDE), low_type),
-            pltpu.VMEM((chunks, half_rows, WIDE), low_type),
-            pltpu.VMEM((chunks, half_rows, WIDE), low_type),
-            pltpu.VMEM((chunks, blocks - 1, half_rows // blocks, WIDE), low_type),
-            dma((2,)),
-            dma((chunks, 2)), dma((chunks, 2)),
+        scratch_shapes=scratch + [
+            dma((chunks + 1, 2)),
+            dma((chunks + 1, 2)), dma((chunks + 1, 2)),
             dma((chunks,)), dma((chunks,)),
             dma((chunks,)), dma((chunks,)),
             dma((chunks, blocks - 1)), dma((chunks, blocks - 1)),
             dma((chunks, blocks - 1)), dma((chunks, blocks - 1)),
             dma((chunks,)), dma((chunks,)),
             dma((returned,)), dma((returned,)), dma,
+            dma, dma, dma,
         ],
         compiler_params=pltpu.CompilerParams(
             vmem_limit_bytes=KERNEL_VMEM, collective_id=1, has_side_effects=True
         ),
         cost_estimate=pl.CostEstimate(
-            flops=value.size, bytes_accessed=4 * value.size, transcendentals=0
+            flops=back.size, bytes_accessed=20 * back.size, transcendentals=0
         ),
         name="gradient_sum",
-    )(value, feed)
+    )(*values, gains, feed, back)
 
 
 def front_kernel(
-    tokens_ref, cotangent_ref, gains_ref, cosine_ref, sine_ref, *refs
+    tokens_ref, cotangent_ref, cosine_ref, sine_ref, *refs
 ):
-    weights, refs = refs[:6], refs[6:]
+    weights, refs = refs[:7], refs[7:]
     (
-        tokens_own, cotangent_own, cotangent_other, gains_out, normed_out, query_out, keyval_ref,
+        tokens_own, cotangent_own, cotangent_other, normed_out, query_out, keyval_ref,
         mixed_out, lse_ref,
-    ), refs = refs[:9], refs[9:]
-    full, refs = refs[:6], refs[6:]
+    ), refs = refs[:8], refs[8:]
+    full, refs = refs[:7], refs[7:]
     (
-        gain_in, raw, tops, totals, sums,
-        local_sem, gain_send, gain_recv, token_send, token_recv, cot_send, cot_recv,
+        raw, tops, totals, sums,
+        local_sem, token_send, token_recv, cot_send, cot_recv,
         y_send, y_recv, mate_send, mate_recv, pass_send, pass_recv, key_send, key_recv,
     ) = refs
     place = lax.axis_index("ctx")
@@ -851,13 +925,18 @@
     core = rank % 2
     mate = rank + 1 - 2 * core
     across = rank + 2 - 4 * (rank // 2)
-    part_rows = tokens_ref.shape[1]
+    width = tokens_ref.shape[-1]
+
+    def columns(ref, slot):
+        return ref.at[:, pl.ds(pl.multiple_of(slot * width, width), width)]
 
     local = [
-        pltpu.make_async_copy(tokens_ref.at[side], tokens_own.at[side], local_sem.at[0]),
-        pltpu.make_async_copy(cotangent_ref.at[side], cotangent_own.at[side], local_sem.at[1]),
+        pltpu.make_async_copy(tokens_ref.at[side], columns(tokens_own, side), local_sem.at[0]),
         pltpu.make_async_copy(
-            cotangent_ref.at[1 - side], cotangent_other.at[side], local_sem.at[2]
+            cotangent_ref.at[side], columns(cotangent_own, side), local_sem.at[1]
+        ),
+        pltpu.make_async_copy(
+            cotangent_ref.at[1 - side], columns(cotangent_other, side), local_sem.at[2]
         ),
     ]
     for w in range(len(weights)):
@@ -880,23 +959,17 @@
     neighbours = (place + last - 1) // last + (2 * last - place - 1) // last
     pl.semaphore_wait(pltpu.get_barrier_semaphore(), 3 + neighbours)
 
-    gain_mate = remote(
-        gains_ref, gain_in.at[0], gain_send.at[0], gain_recv.at[0], fsdp=mate
-    )
-    gain_across = remote(
-        gain_in.at[2], gain_in.at[1], gain_send.at[1], gain_recv.at[1], fsdp=across
-    )
     token_copy = remote(
-        tokens_ref.at[1 - side], tokens_own.at[side], token_send, token_recv, tp=1 - side
+        tokens_ref.at[1 - side], columns(tokens_own, side), token_send, token_recv, tp=1 - side
     )
     cot_copies = [
         remote(
-            cotangent_ref.at[1 - side], cotangent_own.at[side], cot_send.at[0], cot_recv.at[0],
-            tp=1 - side,
+            cotangent_ref.at[1 - side], columns(cotangent_own, side), cot_send.at[0],
+            cot_recv.at[0], tp=1 - side,
         ),
         remote(
-            cotangent_ref.at[side], cotangent_other.at[side], cot_send.at[1], cot_recv.at[1],
-            tp=1 - side,
+            cotangent_ref.at[side], columns(cotangent_other, side), cot_send.at[1],
+            cot_recv.at[1], tp=1 - side,
         ),
     ]
 
@@ -915,23 +988,27 @@
             full[w].at[across], full[w].at[across], pass_send.at[w], pass_recv.at[w], fsdp=mate
         )
 
-    gain_mate.start()
-    token_copy.start()
-    for w in (1, 0):
+    def arrived(w):
+        local[3 + w].wait()
+        mate_copy(w).wait_recv()
+        pass_copy(w).wait_recv()
+
+    for w in (6, 1):
         y_copy(w).start()
         mate_copy(w).start()
-    gain_mate.wait_recv()
-    gain_in[2] = gains_ref[...] + gain_in[0]
-    gain_across.start()
-    gain_across.wait_recv()
-    gains = gain_in[1] + gain_in[2]
-    gains_out[...] = gains
-    gain = wide(gains[:1])
+    token_copy.start()
+    y_copy(0).start()
+    mate_copy(0).start()
+    y_copy(6).wait_recv()
+    pass_copy(6).start()
+    arrived(6)
+    gain = wide(full[6][...].reshape(-1, full[6].shape[-1])[:, :1])
 
     def norm_rows(slot):
-        rows = wide(tokens_own[slot])
-        unit, inverse = normalize(rows)
-        normed_out[slot] = low(unit * gain)
+        at = pl.ds(pl.multiple_of(slot * width, width), width)
+        rows = wide(tokens_own[:, at])
+        inverse = lax.rsqrt(jnp.mean(rows * rows, 0, keepdims=True) + EPS)
+        normed_out[:, at] = low(rows * inverse * gain)
 
     local[0].wait()
     norm_rows(side)
@@ -942,10 +1019,10 @@
     for w in (1, 0):
         y_copy(w).wait_recv()
         pass_copy(w).start()
-    for w in range(2, len(weights)):
+    for w in range(2, 6):
         y_copy(w).start()
         mate_copy(w).start()
-    normed = normed_out[...].reshape(2 * part_rows, -1)
+    normed = normed_out[...]
     cosine, sine = cosine_ref[...], sine_ref[...]
 
     def turned(value, target):
@@ -958,14 +1035,9 @@
             ctx=place + 1,
         )
 
-    def arrived(w):
-        local[3 + w].wait()
-        mate_copy(w).wait_recv()
-        pass_copy(w).wait_recv()
-
     arrived(1)
     matrix = full[1][...].reshape(-1, 2 * KEY_WIDTH)
-    raw[: 2 * KEY_WIDTH] = dot(matrix, normed, 0, 1)
+    raw[: 2 * KEY_WIDTH] = dot(matrix, normed, 0, 0)
     for j in range(KEYVAL_HEADS):
         turned(raw[j * HEAD_WIDTH : (j + 1) * HEAD_WIDTH], keyval_ref.at[0, j, 0])
         first = KEY_WIDTH + j * HEAD_WIDTH
@@ -977,7 +1049,7 @@
 
     arrived(0)
     matrix = full[0][...].reshape(-1, QUERY_WIDTH)
-    raw[...] = dot(matrix, normed, 0, 1)
+    raw[...] = dot(matrix, normed, 0, 0)
 
     def turn_query(h, carry):
         value = raw[pl.ds(pl.multiple_of(h * HEAD_WIDTH, HEAD_WIDTH), HEAD_WIDTH)]
@@ -1047,17 +1119,15 @@
 
     lax.fori_loop(0, QUERY_HEADS, divide, 0)
 
-    for w in range(passed, len(weights)):
+    for w in range(passed, 6):
         y_copy(w).wait_recv()
         pass_copy(w).start()
     local[1].wait()
     local[2].wait()
-    gain_mate.wait_send()
-    gain_across.wait_send()
     token_copy.wait_send()
     for copy in cot_copies:
         copy.wait()
-    for w in range(passed, len(weights)):
+    for w in range(passed, 6):
         arrived(w)
     for w in range(len(weights)):
         y_copy(w).wait_send()
@@ -1073,7 +1143,7 @@
         lax.fori_loop(0, (place + 1) * KEYVAL_HEADS, sent, 0)
 
 
-def front(tokens, cotangent, gains, cosine, sine, weights):
+def front(tokens, cotangent, cosine, sine, weights):
     blocks = lax.axis_size("ctx")
     parts = lax.axis_size("fsdp")
     positions = cosine.shape[-1]
@@ -1082,27 +1152,26 @@
     dma = pltpu.SemaphoreType.DMA
     shape = lambda *dims: jax.ShapeDtypeStruct(dims, jnp.bfloat16)
     count = len(weights)
+    features = tokens.shape[1]
     area = QUERY_HEADS * positions * positions * blocks
     return pl.pallas_call(
         front_kernel,
-        in_specs=[anywhere, anywhere, vmem, vmem, vmem] + [anywhere] * count,
-        out_specs=[vmem, anywhere, anywhere] + [vmem] * 6 + [vmem] * 2 + [anywhere] * 4,
+        in_specs=[vmem] * (4 + count),
+        out_specs=[vmem] * 8 + [vmem] * 2 + [anywhere] * 4 + [vmem],
         out_shape=[
-            shape(*tokens.shape), shape(*tokens.shape), shape(*tokens.shape),
-            shape(*gains.shape), shape(*tokens.shape),
+            shape(features, positions), shape(features, positions), shape(features, positions),
+            shape(features, positions),
             shape(QUERY_HEADS, HEAD_WIDTH, positions),
             shape(blocks, KEYVAL_HEADS, 2, HEAD_WIDTH, positions),
             shape(QUERY_HEADS, HEAD_WIDTH, positions),
             jax.ShapeDtypeStruct((QUERY_HEADS, 1, positions), jnp.float32),
         ] + [shape(parts, *w.shape) for w in weights],
         scratch_shapes=[
-            pltpu.VMEM((3,) + gains.shape, jnp.bfloat16),
             pltpu.VMEM((QUERY_WIDTH, positions), jnp.float32),
             pltpu.VMEM((QUERY_HEADS, 1, positions), jnp.float32),
             pltpu.VMEM((QUERY_HEADS, 1, positions), jnp.float32),
             pltpu.VMEM((QUERY_HEADS, HEAD_WIDTH, positions), jnp.float32),
             dma((3 + count,)),
-            dma((2,)), dma((2,)),
             dma, dma,
             dma((2,)), dma((2,)),
             dma((count,)), dma((count,)),
@@ -1117,7 +1186,7 @@
             flops=16 * HEAD_WIDTH * area, bytes_accessed=10 * tokens.size, transcendentals=area
         ),
         name="front",
-    )(tokens, cotangent, gains, cosine, sine, *weights)
+    )(tokens, cotangent, cosine, sine, *weights)
 
 
 def on_device(
@@ -1280,46 +1349,32 @@
 def fast_on_device(
     tokens, cotangent, input_gain, w_query, w_keyval, w_output, middle_gain, w_gate, w_up, w_down
 ):
-    half = lax.axis_index("tp")
-    low_half = half == 0
     pair = [(0, 1), (1, 0)]
 
     def to_partner(value_rows):
         return lax.ppermute(value_rows, "tp", pair)
-
-    def in_order(mine, received):
-        return jnp.concatenate(
-            [jnp.where(low_half, mine, received), jnp.where(low_half, received, mine)], 0
-        )
-
-    def take(value_rows, index):
-        return lax.dynamic_index_in_dim(value_rows, index, 0, keepdims=False)
 
     parts = lax.axis_size("fsdp")
     width_in = tokens.shape[-1]
     rows = width_in // parts
     token_positions = 2 * tokens.shape[1]
     cosine, sine = rope_tables(token_positions, lax.axis_index("ctx") * token_positions)
-    gains = lax.dynamic_update_slice(
-        jnp.zeros((16, width_in), jnp.bfloat16), jnp.stack([input_gain, middle_gain]),
-        (0, lax.axis_index("fsdp") * rows),
-    )
+    gains = jnp.pad(jnp.stack([input_gain, middle_gain], 1), ((0, 0), (0, 126)))
     (
-        tokens_own, cotangent_own, cotangent_other, gains, normed_one, query_low, keyval,
+        tokens_own, cotangent_own, cotangent_other, normed_one, query_low, keyval,
         mixed_heads, lse, *full,
     ) = front(
-        tokens, cotangent, gains, cosine, sine,
-        (w_query, w_keyval, w_output, w_gate, w_up, w_down),
-    )
-    full_query, full_keyval, full_output, full_gate, full_up, full_down = [
+        tokens.swapaxes(1, 2), cotangent.swapaxes(1, 2), cosine, sine,
+        (w_query, w_keyval, w_output, w_gate, w_up, w_down, gains),
+    )
+    full_query, full_keyval, full_output, full_gate, full_up, full_down, gains = [
         w.reshape(width_in, -1) for w in full
     ]
     tokens_own, cotangent_own, cotangent_other, normed_one = [
-        v.reshape(token_positions, width_in)
-        for v in (tokens_own, cotangent_own, cotangent_other, normed_one)
+        v.T for v in (tokens_own, cotangent_own, cotangent_other, normed_one)
     ]
-    gain_one = gains[0].astype(jnp.float32)
-    full_gain_two = gains[1]
+    gain_one = gains[:, 0].astype(jnp.float32)
+    full_gain_two = gains[:, 1]
     inputs = tokens_own.astype(jnp.float32)
     unit_one, inverse_one = normalize(inputs)
     mixed_low = mixed_heads.reshape(QUERY_WIDTH, token_positions)
@@ -1352,10 +1407,8 @@
         feed_input_back(back_gate_other, back_up_other).astype(jnp.bfloat16)
     )
     back_two = feed_input_back(back_gate_own, back_up_own) + back_two_received.astype(jnp.float32)
-    feed_received = to_partner(dot(hidden_other, full_down, 1, 1).astype(jnp.bfloat16))
-    result_own = (
-        middle + dot(hidden_own, full_down, 1, 1) + feed_received.astype(jnp.float32)
-    ).astype(jnp.bfloat16)
+    feed_other = dot(hidden_other, full_down, 1, 1).astype(jnp.bfloat16)
+    base = middle + dot(hidden_own, full_down, 1, 1)
 
     def feed_gradient(left_own, right_own, left_other, right_other):
         gradient = dot(left_own, right_own, 0, 0) + dot(left_other, right_other, 0, 0)
@@ -1375,8 +1428,9 @@
     back_mixed = dot(full_output, back_attention, 1, 1).astype(jnp.bfloat16)
     back_mixed = back_mixed.reshape(query_low.shape)
     grad_output = dot(mixed_low, back_attention, 1, 0).astype(jnp.bfloat16)
-    back_query, back_keyval, share = backward_sum(
-        query_low, keyval, back_mixed, mixed_heads, lse, cosine, sine, gradients
+    back_query, back_keyval, share, result = backward_sum(
+        query_low, keyval, back_mixed, mixed_heads, lse, cosine, sine, base.T, feed_other.T,
+        gradients,
     )
     back_query = back_query.reshape(QUERY_WIDTH, token_positions)
     back_keyval = back_keyval.reshape(2 * KEY_WIDTH, token_positions)
@@ -1386,32 +1440,22 @@
     grad_gain_one = jnp.sum(back_one * unit_one, axis=0)
     back_inputs = back_middle + norm_back(back_one * gain_one, unit_one, inverse_one)
 
-    def to_positions(value_rows):
-        split = value_rows.reshape(2, token_positions // 2, value_rows.shape[-1])
-        received = to_partner(take(split, 1 - half))
-        return in_order(take(split, half)[None], received[None])
-
-    result = to_positions(result_own)
-    grad_tokens = to_positions(back_inputs.astype(jnp.bfloat16)).astype(jnp.float32)
-    width = 2 * QUERY_WIDTH + 2 * KEY_WIDTH
-    gains = jnp.concatenate(
-        [grad_gain_one.reshape(parts, rows), grad_gain_two.reshape(parts, rows)], 1
-    )
-    gains = jnp.pad(gains[:, None], ((0, 0), (0, 15), (0, width - 2 * rows)))
-    summed = jnp.concatenate([grad_output, grad_query, grad_keyval], 1)
-    summed = jnp.concatenate(
-        [summed.reshape(parts, rows, width), gains.astype(jnp.bfloat16)], 1
-    )
-    share_in, share_rest = gradient_sum(summed, share)
-    share_in = share_in.astype(jnp.float32)
+    gains = jnp.pad(
+        jnp.stack([grad_gain_one.reshape(parts, rows), grad_gain_two.reshape(parts, rows)], 1),
+        ((0, 0), (0, 14), (0, 2 * KEY_WIDTH - rows)),
+    )
+    share_output, share_query, share_keyval, share_rest, grad_tokens = gradient_sum(
+        [v.reshape(parts, rows, -1) for v in (grad_output, grad_query, grad_keyval)],
+        gains.astype(jnp.bfloat16), share, back_inputs.astype(jnp.bfloat16).T,
+    )
     return (
-        result,
-        grad_tokens,
-        share_in[rows, :rows],
-        share_in[:rows, QUERY_WIDTH : 2 * QUERY_WIDTH],
-        share_in[:rows, 2 * QUERY_WIDTH :],
-        share_in[:rows, :QUERY_WIDTH],
-        share_in[rows, rows : 2 * rows],
+        result.swapaxes(1, 2),
+        grad_tokens.swapaxes(1, 2).astype(jnp.float32),
+        share_keyval[rows, :rows].astype(jnp.float32),
+        share_query[:rows].astype(jnp.float32),
+        share_keyval[:rows].astype(jnp.float32),
+        share_output[:rows].astype(jnp.float32),
+        share_keyval[rows + 1, :rows].astype(jnp.float32),
         share_rest[0].astype(jnp.float32),
         share_rest[1].astype(jnp.float32),
         share[0].astype(jnp.float32),

time: 450 us -> 374 us (0.83)
  waiting for transfers between devices: 42.7 us -> 9.54 us
  local copies, waits for them, and re-layouts: 32.9 us -> 5.99 us
  Pallas kernels: 273 us -> 260 us
  matrix products: 66 us -> 72.3 us
  starting transfers between devices: 7.25 us -> 2.15 us
    ppermute x5 -> x2, waiting for transfers between devices: 42.7 us -> 9.54 us  [to_partner(): return lax.ppermute(value_rows, 'tp', pair)]
    pallas_call x3, Pallas kernels: 273 us -> 260 us  [the longest x1 95.7 us: backward_sum(): pl.pallas_call(backward_sum_kernel, in_specs=[vmem] * 9 + [pl.BlockSpec(m...]
    concatenate x1 -> x0, local copies, waits for them, and re-layouts: 8.84 us -> none  [fast_on_device(): summed = jnp.concatenate([grad_output, grad_query, grad_keyval], 1)]
    dot_general x25, matrix products: 66 us -> 72.3 us  [dot(): lax.dot_general(left, right, (((left_dim,), (right_dim,)), ((), ())), pre...]
    concatenate x2 -> x0, other arithmetic: 6.16 us -> none  [the longest x1 5.13 us: fast_on_device(): jnp.concatenate([summed.reshape(parts, rows, width), gains.astype(jnp.bfl...]
    reshape x5 -> x0, local copies, waits for them, and re-layouts: 5.69 us -> none  [the longest x2 2.82 us: to_positions(): split = value_rows.reshape(2, token_positions // 2, value_rows.shape[-1])]
    ppermute x5 -> x2, starting transfers between devices: 7.25 us -> 2.15 us  [to_partner(): return lax.ppermute(value_rows, 'tp', pair)]
    convert_element_type x2 -> x7, other arithmetic: 4.96 us -> 9.06 us  [the longest x1 2.24 us: fast_on_device(): share[0].astype(jnp.float32)]
  transfers between devices with their start and end apart: 5 -> 2, of which waited for: 3 -> 1; matrix products, arithmetic and copies ran while one was open for 11% -> 11% of each run, Pallas kernels for 0% -> 0%
where the time goes in v3:
time: 374 us; the launch traced here: 370 us
  Pallas kernels  260 us (70%)
  matrix products  72.3 us (19%)
  other arithmetic  17.9 us (5%)
  waiting for transfers between devices  9.54 us (3%)
  local copies, waits for them, and re-layouts  5.99 us (2%)
    pallas_call x1, Pallas kernels, backward_sum(): pl.pallas_call(backward_sum_kernel, in_specs=[vmem] * 9 + [pl.BlockSpec(m...  95.7 us
    pallas_call x1, Pallas kernels, front(): pl.pallas_call(front_kernel, in_specs=[vmem] * (4 + count), out_specs=[vm...  84.4 us
    pallas_call x1, Pallas kernels, gradient_sum(): pl.pallas_call(gradient_sum_kernel, in_specs=[anywhere] * (chunks + 2) +...  80.4 us
    dot_general x25, matrix products, dot(): lax.dot_general(left, right, (((left_dim,), (right_dim,)), ((), ())), pre...  72.3 us
    ppermute x2, waiting for transfers between devices, to_partner(): return lax.ppermute(value_rows, 'tp', pair)  9.54 us
  transfers between devices with their start and end apart: 2, of which 1 were waited for; matrix products, arithmetic and copies ran while one was open for 11% of the time, Pallas kernels for 0%

profile of v3, /device:TPU:0, one launch (start us, length us, event | category | flops | bytes accessed | tf_op | source)
XLA Modules:
  0.0 369.6 jit_solution(16141208557753842049)
XLA Ops:
  3.8 84.4 %front.1 = (bf16[960,512]{1,0:T(8,128)(2,1)}, bf16[960,512]{1,0:T(8,128)(2,1)}, bf16[960,512]{1,0:T(8,128)(2,1)}, bf16[960,512]{1,0:T(8,128)(2,1)}, bf16[15,64,5...) custom-call(bf16[2,960,256]{2,1,0:T(8,128)(2,1)} %bitcast.161, ...), custom_call_target="tpu_custom_call" | custom-call | flops 16106127360 | bytes 4915200 | tf_op jit(solution)/shard_map/front/pallas_call | solution.py:1157
  88.2 4.6 %multiply_reduce_fusion.2 = (f32[512]{0:T(512)S(1)}, f32[512,960]{0,1:T(8,128)}) fusion(bf16[960,512]{1,0:T(8,128)(2,1)} %get-tuple-element.38, bf16[960,512]{1,0:T(8,128)(2,1)} %bitcast.170, bf16[960,960]{1,0:T(8,128)(2,1)} %bitcast.168), kind=kOutput, calls=%fused_computation.36 | convolution fusion | flops 945683968 | bytes 5777408 | tf_op jit(solution)/shard_map/dot_general | solution.py:23
  99.5 3.1 fusion.28
  104.3 2.5 multiply_convert_fusion.1
  106.8 3.7 %fusion.31 = f32[960,1280]{1,0:T(8,128)} fusion(bf16[960,512]{1,0:T(8,128)(2,1)S(1)} %copy-done.5, bf16[512,1280]{1,0:T(8,128)(2,1)S(1)} %get-tuple-element.66), kind=kOutput, calls=%fused_computation.79 | convolution fusion | flops 1258291200 | bytes 7208960 | tf_op jit(solution)/shard_map/dot_general | solution.py:23
  110.5 3.7 fusion.32
  114.2 3.7 fusion.33
  118.0 4.1 %fusion.27 = f32[512,960]{0,1:T(8,128)S(1)} fusion(bf16[512,1280]{1,0:T(8,128)(2,1)} %copy-done.16, bf16[960,1280]{1,0:T(8,128)(2,1)} %bitcast.139), kind=kOutput, calls=%fused_computation.75 | convolution fusion | flops 1258291200 | bytes 5734400 | tf_op jit(solution)/shard_map/dot_general | solution.py:23
  122.2 2.7 fusion.15.base_ref
  124.9 2.9 fusion.29
  127.9 3.8 %multiply_convert_fusion = (bf16[512,1280]{1,0:T(8,128)(2,1)S(1)}, bf16[512,1280]{1,0:T(8,128)(2,1)S(1)}, bf16[512,1280]{1,0:T(8,128)(2,1)S(1)}) fusion(f32[512,1280]{1,0:T(8,128)S(1)} %fusion.29, f32[512,1280]{1,0:T(8,128)S(1)} %copy-done.11, bf16[512,960]{0,1:T(8,128)(2,1)} %collective-permute-done, bf16[960,1280]{1,0:T(8,128)(2,1)S(1)} %bitcast.164), kind=kOutput, calls=%fused_computation.3 | convolution fusion | flops 1268121600 | bytes 12615680 | tf_op jit(solution)/shard_map/dot_general | solution.py:23
  135.3 2.9 add_convert_fusion.2
  138.2 4.2 %add_convert_fusion.1 = bf16[960,1280]{1,0:T(8,128)(2,1)} fusion(f32[960,1280]{1,0:T(8,128)S(1)} %bitcast.132, bf16[512,960]{0,1:T(8,128)(2,1)} %collective-permute-done, bf16[512,1280]{1,0:T(8,128)(2,1)S(1)} %get-tuple-element.64), kind=kOutput, calls=%fused_computation.1 | convolution fusion | flops 1260748800 | bytes 9666560 | tf_op jit(solution)/shard_map/dot_general | solution.py:23
  142.4 2.4 convolution_convert_fusion.3.feed_ref
  144.8 4.2 %add_convert_fusion = bf16[960,1280]{1,0:T(8,128)(2,1)} fusion(f32[960,1280]{1,0:T(8,128)S(1)} %bitcast.130, bf16[512,960]{0,1:T(8,128)(2,1)} %collective-permute-done, bf16[512,1280]{1,0:T(8,128)(2,1)S(1)} %get-tuple-element.65), kind=kOutput, calls=%fused_computation | convolution fusion | flops 1260748800 | bytes 9666560 | tf_op jit(solution)/shard_map/dot_general | solution.py:23
  149.0 9.5 %collective-permute-done.1 = bf16[512,960]{0,1:T(8,128)(2,1)S(1)} collective-permute-done((bf16[512,960]{0,1:T(8,128)(2,1)S(1)}, bf16[512,960]{0,1:T(8,128)(2,1)S(1)}, u32[]{:S(2)}, u32[]{:S(2)}) %collective-permute-start.1) | collective-permute-done | bytes 983072 | tf_op jit(solution)/shard_map/ppermute | solution.py:1355
  158.6 2.3 multiply_reduce_fusion
  164.6 2.5 convolution_convert_fusion.1
  167.1 95.7 %backward_sum.1 = (bf16[15,64,512]{2,1,0:T(8,128)(2,1)}, bf16[2,5,64,512]{3,2,1,0:T(8,128)(2,1)}, bf16[3,240,1280]{2,1,0:T(8,128)(2,1)}, bf16[2,960,256]{2,1,0:T(8,128)(2,1)}) custom-call(bf16[15,64,512]{2,1,0:T(8,128)(2,1)} %get-tuple-element.34.query_ref, bf16[4,5,2,64,512]{4,3,2,1,0:T(8,128)(2,1)} %get-tuple-element.35.keyval_ref, ...), custom_call_target="tpu_custom_call" | custom-call | flops 40265318400 | bytes 4915200 | tf_op jit(solution)/shard_map/backward_sum/pallas_call | solution.py:607
  262.8 3.8 %convolution_convert_fusion = bf16[960,960]{1,0:T(8,128)(2,1)} fusion(bf16[960,512]{1,0:T(8,128)(2,1)S(1)} %copy-done.31, bf16[960,512]{1,0:T(8,128)(2,1)} %bitcast.172), kind=kOutput, calls=%fused_computation.37 | convolution fusion | flops 944640000 | bytes 3809280 | tf_op jit(solution)/shard_map/dot_general | solution.py:23
  268.7 2.5 fusion.34
  271.2 2.5 fusion.9
  274.5 3.0 fusion.16.back_ref
  277.5 80.4 %gradient_sum.1 = (bf16[256,960]{1,0:T(8,128)(2,1)}, bf16[256,960]{1,0:T(8,128)(2,1)}, bf16[256,640]{1,0:T(8,128)(2,1)}, bf16[2,240,1280]{2,1,0:T(8,128)(2,1)}, bf16[2,960,256]{2,1,0:T(8,128)(2,1)}) custom-call(bf16[4,240,960]{2,1,0:T(8,128)(2,1)} %bitcast.146, bf16[4,240,960]{2,1,0:T(8,128)(2,1)} %bitcast.147, bf16[4,240,640]{2,1,0:T(8,128)(2,1)} %bitcast.149, ...), custom_call_target="tpu_custom_call" | custom-call | flops 491520 | bytes 9830400 | tf_op jit(solution)/shard_map/gradient_sum/pallas_call | solution.py:878
  (115 shorter events, 33.3 us)
Async XLA Ops:
  88.2 4.7 %copy-start.21 = (bf16[4,240,128]{2,1,0:T(8,128)(2,1)S(1)}, bf16[4,240,128]{2,1,0:T(8,128)(2,1)}, u32[]{:S(2)}) copy-start(bf16[4,240,128]{2,1,0:T(8,128)(2,1)} %get-tuple-element.41) | copy-start | bytes 737284
  94.0 3.6 copy-start.3
  96.0 28.9 %collective-permute-start = (bf16[512,960]{0,1:T(8,128)(2,1)S(1)}, bf16[512,960]{0,1:T(8,128)(2,1)}, u32[]{:S(2)}, u32[]{:S(2)}) collective-permute-start(bf16[512,960]{0,1:T(8,128)(2,1)S(1)} %multiply_convert_fusion.6), channel_id=1, source_target_pairs={{0,1},{1,0},{2,3},{3,2},{4,5},{5,4},{6,7},{7,6},{8,9},{9,8},{10,11... | collective-permute-start | bytes 2949128 | tf_op jit(solution)/shard_map/ppermute | solution.py:1355
  99.5 3.1 copy-start.5
  106.8 3.7 %copy-start.14 = (bf16[512,1280]{1,0:T(8,128)(2,1)}, bf16[512,1280]{1,0:T(8,128)(2,1)S(1)}, u32[]{:S(2)}) copy-start(bf16[512,1280]{1,0:T(8,128)(2,1)S(1)} %get-tuple-element.66) | copy-start | bytes 3932164
  106.8 3.7 %copy-start.16 = (bf16[512,1280]{1,0:T(8,128)(2,1)}, bf16[512,1280]{1,0:T(8,128)(2,1)S(1)}, u32[]{:S(2)}) copy-start(bf16[512,1280]{1,0:T(8,128)(2,1)S(1)} %get-tuple-element.67) | copy-start | bytes 3932164
  106.8 7.4 %copy-start.12 = (bf16[512,1280]{1,0:T(8,128)(2,1)}, bf16[512,1280]{1,0:T(8,128)(2,1)S(1)}, u32[]{:S(2)}) copy-start(bf16[512,1280]{1,0:T(8,128)(2,1)S(1)} %get-tuple-element.68) | copy-start | bytes 3932164
  118.0 4.1 %copy-start.2 = (bf16[4,240,1280]{2,1,0:T(8,128)(2,1)S(1)}, bf16[4,240,1280]{2,1,0:T(8,128)(2,1)}, u32[]{:S(2)}) copy-start(bf16[4,240,1280]{2,1,0:T(8,128)(2,1)} %get-tuple-element.40) | copy-start | bytes 7372804
  118.0 4.1 %copy-start.6 = (f32[512,960]{0,1:T(8,128)S(1)}, f32[512,960]{0,1:T(8,128)}, u32[]{:S(2)}) copy-start(f32[512,960]{0,1:T(8,128)} %get-tuple-element.78) | copy-start | bytes 5898244
  118.0 4.1 %copy-start.15 = (bf16[512,1280]{1,0:T(8,128)(2,1)S(1)}, bf16[512,1280]{1,0:T(8,128)(2,1)}, u32[]{:S(2)}) copy-start(bf16[512,1280]{1,0:T(8,128)(2,1)} %copy-done.14) | copy-start | bytes 3932164
  124.9 2.9 copy-start.11
  124.9 2.9 copy-start.27
  124.9 10.3 %slice-start.4 = ((s8[4915200]{0:T(1024)(128)(4,1)}), s8[4194304]{0:T(1024)(128)(4,1)S(1)}, s32[]{:S(2)}) async-start(s8[4915200]{0:T(1024)(128)(4,1)} %bitcast.133), calls=%async_computation.4 | async-start | bytes 8388608
  127.9 7.4 %slice-start.5 = ((s8[4915200]{0:T(1024)(128)(4,1)}), s8[720896]{0:T(1024)(128)(4,1)S(1)}, s32[]{:S(2)}) async-start(s8[4915200]{0:T(1024)(128)(4,1)} %bitcast.133), calls=%async_computation.5 | async-start | bytes 1441792
  133.1 5.1 %slice-start.2 = ((s8[4915200]{0:T(1024)(128)(4,1)}), s8[4194304]{0:T(1024)(128)(4,1)S(1)}, s32[]{:S(2)}) async-start(s8[4915200]{0:T(1024)(128)(4,1)} %bitcast.131), calls=%async_computation.2 | async-start | bytes 8388608
  134.6 23.9 %collective-permute-start.1 = (bf16[512,960]{0,1:T(8,128)(2,1)S(1)}, bf16[512,960]{0,1:T(8,128)(2,1)S(1)}, u32[]{:S(2)}, u32[]{:S(2)}) collective-permute-start(bf16[512,960]{0,1:T(8,128)(2,1)S(1)} %add_convert_fusion.3), channel_id=1, source_target_pairs={{0,1},{1,0},{2,3},{3,2},{4,5},{5,4},{6,7},{7,6},{8,9},{9,8},{10,11... | collective-permute-start | bytes 2949128 | tf_op jit(solution)/shard_map/ppermute | solution.py:1355
  135.2 3.0 slice-start.3
  138.2 6.6 %slice-start = ((s8[4915200]{0:T(1024)(128)(4,1)}), s8[4194304]{0:T(1024)(128)(4,1)S(1)}, s32[]{:S(2)}) async-start(s8[4915200]{0:T(1024)(128)(4,1)} %bitcast.129), calls=%async_computation | async-start | bytes 8388608
  144.8 13.8 %copy-start.13 = (bf16[512,1280]{1,0:T(8,128)(2,1)S(1)}, bf16[512,1280]{1,0:T(8,128)(2,1)}, u32[]{:S(2)}) copy-start(bf16[512,1280]{1,0:T(8,128)(2,1)} %copy-done.12) | copy-start | bytes 3932164
  167.1 95.8 %copy-start.31 = (bf16[960,512]{1,0:T(8,128)(2,1)S(1)}, bf16[960,512]{1,0:T(8,128)(2,1)}, u32[]{:S(2)}) copy-start(bf16[960,512]{1,0:T(8,128)(2,1)} %get-tuple-element.47) | copy-start | bytes 2949124
  262.8 3.8 %copy-start.22 = (bf16[2,5,64,512]{3,2,1,0:T(8,128)(2,1)S(1)}, bf16[2,5,64,512]{3,2,1,0:T(8,128)(2,1)}, u32[]{:S(2)}) copy-start(bf16[2,5,64,512]{3,2,1,0:T(8,128)(2,1)} %get-tuple-element.49) | copy-start | bytes 1966084
  271.2 3.3 copy-start.8
  357.9 5.4 %copy-start.20 = (bf16[2,960,256]{2,1,0:T(8,128)(2,1)S(1)}, bf16[2,960,256]{2,1,0:T(8,128)(2,1)}, u32[]{:S(2)}) copy-start(bf16[2,960,256]{2,1,0:T(8,128)(2,1)} %get-tuple-element.53) | copy-start | bytes 2949124
  361.1 3.7 copy-start.25
  (16 other events, 33.0 us)

commit v4 on v3

--- a/solution.py
+++ b/solution.py
@@ -272,9 +272,8 @@
 
 
 MESH = pl.DeviceIdType.MESH
-KERNEL_VMEM = 58 * 1024 * 1024
+KERNEL_VMEM = 60 * 1024 * 1024
 CHUNK_ROWS = 80
-WIDE = 512
 
 
 def remote(source, target, send_sem, recv_sem, **place):
@@ -300,12 +299,23 @@
 
 def backward_sum_kernel(
     query_ref, keyval_ref, back_ref, mixed_ref, lse_ref, cosine_ref, sine_ref,
-    base_ref, feed_ref, down_ref, gate_ref, up_ref,
-    back_query_ref, back_keyval_ref, share_ref, result_ref,
-    own, mate_in, y_in, up_in, parts, part_out, part_in, back_total, row_sums,
+    base_ref, feed_ref, tokens_ref, normed_ref, middle_ref, gains_ref, gain_two_ref,
+    full_query, full_keyval, down_ref, gate_ref, up_ref, out_ref,
+    share_ref, result_ref, back_tokens_ref, *refs,
+):
+    chunks_in = 4
+    shares, refs = refs[:chunks_in], refs[chunks_in:]
+    whole, mate_part, y_part, x_part, z_part = [
+        refs[i * chunks_in : (i + 1) * chunks_in] for i in range(5)
+    ]
+    (
+    own, mate_in, y_in, up_in, parts, part_in, back_total, row_sums,
     own_sem, mate_send, mate_recv, y_send, y_recv, up_send, up_recv, down_send, down_recv,
     part_send, part_recv, feed_in, traded, feed_send, feed_recv, trade_send, trade_recv,
-):
+    back_query_ref, back_keyval_ref, back_one, token_traded,
+    whole_sem, sum_mate_send, sum_mate_recv, sum_y_send, sum_y_recv, sum_x_send, sum_x_recv,
+    sum_z_send, sum_z_recv, all_send, all_recv, back_send, back_recv, token_send, token_recv,
+    ) = refs[5 * chunks_in :]
     place = lax.axis_index("ctx")
     last = lax.axis_size("ctx") - 1
     blocks = last + 1
@@ -329,22 +339,24 @@
     greet(fsdp=mate)
     greet(fsdp=across)
     greet(tp=1 - side)
-
-    @pl.when(place > 0)
-    def _():
-        greet(ctx=place - 1)
-
-    @pl.when(place < last)
-    def _():
-        greet(ctx=place + 1)
-
-    neighbours = (place + last - 1) // last + (2 * last - place - 1) // last
-    pl.semaphore_wait(pltpu.get_barrier_semaphore(), 3 + neighbours)
+    for d in range(1, blocks):
+        greet(ctx=lax.rem(place + d, blocks))
+    filled = out_ref.shape[1]
+    tail = whole[0].shape[1] - filled
+    for n in range(chunks_in):
+        width = whole[n].shape[-1]
+        whole[n][:, filled:] = jnp.zeros((whole[n].shape[0], tail, width), jnp.bfloat16)
+        mate_part[n][:, filled:] = jnp.zeros((2, tail, width), jnp.bfloat16)
+    for f in range(whole[0].shape[0]):
+        pltpu.make_async_copy(
+            out_ref.at[f], whole[0].at[f, pl.ds(0, filled)], whole_sem.at[f]
+        ).start()
+    pl.semaphore_wait(pltpu.get_barrier_semaphore(), 3 + last)
 
     feed_copy = remote(feed_ref, feed_in, feed_send, feed_recv, tp=1 - side)
     trade_copy = remote(traded, result_ref.at[side], trade_send, trade_recv, tp=1 - side)
     feed_copy.start()
-    width = traded.shape[-1]
+    pair_width = traded.shape[-1]
     step_rows = traded.shape[0] // 4
 
     def finish_result():
@@ -353,12 +365,156 @@
         def some_rows(i, carry):
             at = pl.ds(pl.multiple_of(i * step_rows, step_rows), step_rows)
             for target, slot in ((result_ref.at[side], side), (traded, 1 - side)):
-                columns = pl.ds(pl.multiple_of(slot * width, width), width)
+                columns = pl.ds(pl.multiple_of(slot * pair_width, pair_width), pair_width)
                 target[at] = low(base_ref[at, columns] + wide(feed_in[at, columns]))
             return carry
 
         lax.fori_loop(0, 4, some_rows, 0)
         trade_copy.start()
+
+    half_rows = whole[0].shape[1] // 2
+    piece = half_rows // blocks
+    kept = 2 * y + core
+
+    def sum_mate(n, half):
+        return remote(
+            whole[n].at[2 * half + 1 - core, pl.ds(0, filled)],
+            mate_part[n].at[half, pl.ds(0, filled)],
+            sum_mate_send.at[n, half], sum_mate_recv.at[n, half], fsdp=mate,
+        )
+
+    def sum_y(n):
+        return remote(
+            mate_part[n].at[1 - y], y_part[n], sum_y_send.at[n], sum_y_recv.at[n], fsdp=across
+        )
+
+    def sum_x(n):
+        other = pl.ds(pl.multiple_of((1 - side) * half_rows, half_rows), half_rows)
+        return remote(
+            whole[n].at[kept, other], x_part[n], sum_x_send.at[n], sum_x_recv.at[n],
+            tp=1 - side,
+        )
+
+    def sum_z(n, d):
+        target = lax.rem(place + d, blocks)
+        at = pl.ds(pl.multiple_of(side * half_rows + target * piece, piece), piece)
+        return remote(
+            whole[n].at[kept, at], z_part[n].at[d - 1], sum_z_send.at[n, d - 1],
+            sum_z_recv.at[n, d - 1], ctx=target,
+        )
+
+    def all_copy(n, d, origin):
+        spot = shares[n].at[
+            pl.ds(pl.multiple_of(side * half_rows + origin * piece, piece), piece)
+        ]
+        return remote(
+            spot, spot, all_send.at[n, d - 1], all_recv.at[n, d - 1],
+            ctx=lax.rem(place + d, blocks),
+        )
+
+    def back_copy(n, half):
+        spot = shares[n].at[pl.ds(pl.multiple_of(half * half_rows, half_rows), half_rows)]
+        return remote(spot, spot, back_send.at[n], back_recv.at[n], tp=1 - side)
+
+    def to_mate(n):
+        for half in range(2):
+            sum_mate(n, half).start()
+
+    def to_y(n):
+        for half in range(2):
+            sum_mate(n, half).wait_recv()
+        quarter = 2 * (1 - y) + core
+        mate_part[n][1 - y] = low(wide(whole[n][quarter]) + wide(mate_part[n][1 - y]))
+        sum_y(n).start()
+
+    def to_x(n):
+        sum_y(n).wait_recv()
+        whole[n][kept] = low(
+            wide(whole[n][kept]) + wide(mate_part[n][y]) + wide(y_part[n][...])
+        )
+        sum_x(n).start()
+
+    def to_z(n):
+        sum_x(n).wait_recv()
+        at = pl.ds(pl.multiple_of(side * half_rows, half_rows), half_rows)
+        whole[n][kept, at] = low(wide(whole[n][kept, at]) + wide(x_part[n][...]))
+        for d in range(1, blocks):
+            sum_z(n, d).start()
+
+    def to_all(n):
+        at = pl.ds(pl.multiple_of(side * half_rows + place * piece, piece), piece)
+        total = wide(whole[n][kept, at])
+        for d in range(1, blocks):
+            sum_z(n, d).wait_recv()
+            total += wide(z_part[n][d - 1])
+        shares[n][at] = low(total)
+        for d in range(1, blocks):
+            all_copy(n, d, place).start()
+
+    def to_back(n):
+        for d in range(1, blocks):
+            all_copy(n, d, lax.rem(place + blocks - d, blocks)).wait_recv()
+        back_copy(n, side).start()
+
+    def finish_sum(n):
+        back_copy(n, 1 - side).wait_recv()
+        for half in range(2):
+            sum_mate(n, half).wait_send()
+        sum_y(n).wait_send()
+        sum_x(n).wait_send()
+        for d in range(1, blocks):
+            sum_z(n, d).wait_send()
+            all_copy(n, d, place).wait_send()
+        back_copy(n, side).wait_send()
+
+    def weight_gradient(n, back_ref):
+        def quarter(f, carry):
+            rows_of = normed_ref[pl.ds(pl.multiple_of(f * filled, filled), filled)]
+            whole[n][f, :filled] = low(dot(rows_of, back_ref[...], 1, 1))
+            return carry
+
+        lax.fori_loop(0, whole[n].shape[0], quarter, 0)
+
+    token_copy = remote(
+        token_traded, back_tokens_ref.at[side], token_send, token_recv, tp=1 - side
+    )
+
+    def input_gradient():
+        tokens = wide(tokens_ref[...])
+        inverse = lax.rsqrt(jnp.mean(tokens * tokens, 0, keepdims=True) + EPS)
+
+        def quarter(f, total):
+            at = pl.ds(pl.multiple_of(f * filled, filled), filled)
+            unit = wide(tokens_ref[at]) * inverse
+            back = dot(full_query[at], back_query_ref[...], 1, 0) + dot(
+                full_keyval[at], back_keyval_ref[...], 1, 0
+            )
+            gain_sum = jnp.sum(back * unit, 1, keepdims=True)
+            lane = lax.broadcasted_iota(jnp.int32, (filled, whole[3].shape[-1]), 1)
+            whole[3][f, :filled] = low(
+                jnp.where(lane == 0, gain_sum, jnp.where(lane == 1, gain_two_ref[at], 0.0))
+            )
+            back = back * wide(gains_ref[at])[:, :1]
+            back_one[at] = back
+            return total + jnp.sum(back * unit, 0, keepdims=True)
+
+        total = lax.fori_loop(
+            0, whole[0].shape[0], quarter, jnp.zeros((1, tokens_ref.shape[-1]), jnp.float32)
+        )
+        to_mate(3)
+        mean = total / tokens_ref.shape[0]
+
+        def rows_back(f, carry):
+            at = pl.ds(pl.multiple_of(f * filled, filled), filled)
+            unit = wide(tokens_ref[at]) * inverse
+            back_one[at] = middle_ref[at] + inverse * (back_one[at] - unit * mean)
+            for target, slot in ((back_tokens_ref.at[side], side), (token_traded, 1 - side)):
+                columns = pl.ds(pl.multiple_of(slot * pair_width, pair_width), pair_width)
+                target[at] = low(back_one[at, columns])
+            return carry
+
+        lax.fori_loop(0, whole[0].shape[0], rows_back, 0)
+        token_copy.start()
 
     def chunk_at(ref, m, r, *front):
         return ref.at[(m,) + front + (pl.ds(r * CHUNK_ROWS, CHUNK_ROWS),)]
@@ -375,6 +531,11 @@
         for r in range(per):
             for half in range(2):
                 mate_copy(m, r, half).start()
+    for f in range(whole[0].shape[0]):
+        pltpu.make_async_copy(
+            out_ref.at[f], whole[0].at[f, pl.ds(0, filled)], whole_sem.at[f]
+        ).wait()
+    to_mate(0)
     for m, gradient in enumerate(gradients):
         for half in range(2):
             pltpu.make_async_copy(
@@ -435,10 +596,6 @@
         def _():
             share_ref[m, at] = own[m, y, at]
 
-            @pl.when(k < early)
-            def _():
-                down_copy(k).start()
-
     def to_previous(k):
         down_copy(k).wait_recv()
 
@@ -446,6 +603,10 @@
         def _():
             down_copy(k).start()
 
+    def query_gradient(n):
+        weight_gradient(n, back_query_ref)
+        to_mate(n)
+
     def tick(t):
         @pl.when(t < chunks)
         def _():
@@ -461,15 +622,28 @@
         def _():
             to_next(b // 2)
 
-        c = t - 3 - 2 * last - 2 * (last - place)
-
-        @pl.when((place < last) & (c >= 0) & (c < 2 * early) & (lax.rem(c, 2) == 0))
-        def _():
-            to_previous(c // 2)
+        c = t - KEYVAL_HEADS * blocks - (last - place)
+
+        @pl.when((place == last) & (c >= 0) & (c < chunks))
+        def _():
+            down_copy(c).start()
+
+        @pl.when((place < last) & (c >= 0) & (c < early))
+        def _():
+            to_previous(c)
+
+        for at, stage, n in (
+            (chunks + 1, to_y, 0), (20, query_gradient, 1), (20, to_x, 0), (21, to_y, 1),
+            (22, to_z, 0), (24, to_all, 0), (26, to_x, 1), (26, to_back, 0), (28, to_z, 1),
+            (30, to_all, 1),
+        ):
+            @pl.when(t == at)
+            def _(stage=stage, n=n):
+                stage(n)
 
     def part_copy(j, s):
         return remote(
-            part_out.at[j, s - 1], part_in.at[j, s - 1], part_send.at[j, s - 1],
+            parts.at[j, s], part_in.at[j, s - 1], part_send.at[j, s - 1],
             part_recv.at[j, s - 1], ctx=place - 1,
         )
 
@@ -498,8 +672,8 @@
                 back_total[g] += added
             back_key += dot(query, back_scores, 1, 1)
             back_value += dot(back, low(weights), 1, 1)
-        parts[j, s, 0] = back_key
-        parts[j, s, 1] = back_value
+        parts[j, s, 0] = low(back_key)
+        parts[j, s, 1] = low(back_value)
 
     def hand_on(j):
         for s in range(blocks):
@@ -510,20 +684,25 @@
                     pltpu.make_async_copy(
                         part_in.at[j, s], part_in.at[j, s], part_recv.at[j, s]
                     ).wait()
-                    for side in range(2):
-                        parts[j, s, side] += wide(part_in[j, s, side])
+                    for kind in range(2):
+                        total = wide(parts[j, s, kind]) + wide(part_in[j, s, kind])
+                        parts[j, s, kind] = low(total)
 
                 if s > 0:
-                    for side in range(2):
-                        part_out[j, s - 1, side] = low(parts[j, s, side])
                     part_copy(j, s).start()
                 else:
-                    leading = parts[j, 0, 0, :HALF]
-                    trailing = parts[j, 0, 0, HALF:]
+                    leading = wide(parts[j, 0, 0, :HALF])
+                    trailing = wide(parts[j, 0, 0, HALF:])
                     cosine, sine = cosine_ref[...], sine_ref[...]
-                    back_keyval_ref[0, j, :HALF] = low(leading * cosine + trailing * sine)
-                    back_keyval_ref[0, j, HALF:] = low(trailing * cosine - leading * sine)
-                    back_keyval_ref[1, j] = low(parts[j, 0, 1])
+                    at = j * HEAD_WIDTH
+                    back_keyval_ref[pl.ds(pl.multiple_of(at, HALF), HALF)] = low(
+                        leading * cosine + trailing * sine
+                    )
+                    back_keyval_ref[pl.ds(pl.multiple_of(at + HALF, HALF), HALF)] = low(
+                        trailing * cosine - leading * sine
+                    )
+                    at = pl.ds(pl.multiple_of(KEY_WIDTH + at, HEAD_WIDTH), HEAD_WIDTH)
+                    back_keyval_ref[at] = low(wide(parts[j, 0, 1]))
 
     def head_loop(j, carry):
         @pl.when(j < KEYVAL_HEADS)
@@ -548,9 +727,13 @@
             for g in range(GROUP):
                 leading = back_total[g, :HALF] * SCALE
                 trailing = back_total[g, HALF:] * SCALE
-                head = GROUP * j + g
-                back_query_ref[head, :HALF] = low(leading * cosine + trailing * sine)
-                back_query_ref[head, HALF:] = low(trailing * cosine - leading * sine)
+                at = (GROUP * j + g) * HEAD_WIDTH
+                back_query_ref[pl.ds(pl.multiple_of(at, HALF), HALF)] = low(
+                    leading * cosine + trailing * sine
+                )
+                back_query_ref[pl.ds(pl.multiple_of(at + HALF, HALF), HALF)] = low(
+                    trailing * cosine - leading * sine
+                )
 
         ready = j - (last - place)
 
@@ -562,6 +745,29 @@
 
     assert (KEYVAL_HEADS + last) * blocks >= 4 + 4 * last + 2 * (chunks - 1)
     lax.fori_loop(0, KEYVAL_HEADS + last, head_loop, 0)
+
+    def keyval_gradient(n):
+        weight_gradient(n, back_keyval_ref)
+        to_mate(n)
+
+    later = (
+        ((keyval_gradient, 2), (to_back, 1)), ((to_y, 2),), ((lambda n: input_gradient(), 3),),
+        ((to_x, 2),), ((to_y, 3),), ((to_z, 2), (to_x, 3)), ((to_all, 2), (to_z, 3)),
+        ((to_back, 2), (to_all, 3)), ((to_back, 3),),
+    )
+    for slot, stages in enumerate(later):
+        for stage, n in stages:
+            stage(n)
+        for index in range(last):
+            if early <= early + slot - last + 1 + index < chunks:
+                @pl.when(place == index)
+                def _(k=early + slot - last + 1 + index):
+                    to_previous(k)
+
+    assert len(later) >= chunks - early + last - 1
+    for n in range(chunks_in):
+        finish_sum(n)
+    token_copy.wait()
 
     for m in range(len(gradients)):
         for r in range(per):
@@ -575,7 +781,7 @@
         def _():
             up_copy(k).wait_send()
 
-        @pl.when((place > 0) & (k < early))
+        @pl.when(place > 0)
         def _():
             down_copy(k).wait_send()
 
@@ -595,44 +801,67 @@
     trade_copy.wait()
 
 
-def backward_sum(query, keyval, back_mixed, mixed, lse, cosine, sine, base, feed, gradients):
+def backward_sum(
+    query, keyval, back_mixed, mixed, lse, cosine, sine, base, feed, tokens, normed, middle,
+    gains, gain_two, full_query, full_keyval, gradients, gradient_out,
+):
     blocks, positions = keyval.shape[0], keyval.shape[-1]
     count, rows, columns = gradients[0].shape
     chunks = len(gradients) * rows // CHUNK_ROWS
     area = QUERY_HEADS * positions * positions * blocks
     vmem = pl.BlockSpec(memory_space=pltpu.VMEM)
+    anywhere = pl.BlockSpec(memory_space=pl.ANY)
     dma = pltpu.SemaphoreType.DMA
     share = (len(gradients), rows, columns)
     head = (2, HEAD_WIDTH, positions)
+    features = feed.shape[0]
+    widths = (QUERY_WIDTH, QUERY_WIDTH, 2 * KEY_WIDTH, gains.shape[-1])
+    padded = rows + 16
+    half_rows = padded // 2
+    low_type = jnp.bfloat16
+    scratch = []
+    for first in ((count, padded), (2, padded), (padded,), (half_rows,),
+                  (blocks - 1, half_rows // blocks)):
+        scratch += [pltpu.VMEM(first + (w,), low_type) for w in widths]
+    each = len(widths)
+    pairs = jax.ShapeDtypeStruct((2, features, positions // 2), low_type)
     return pl.pallas_call(
         backward_sum_kernel,
-        in_specs=[vmem] * 9 + [pl.BlockSpec(memory_space=pl.ANY)] * 3,
-        out_specs=[vmem] * 4,
-        out_shape=[
-            jax.ShapeDtypeStruct(query.shape, jnp.bfloat16),
-            jax.ShapeDtypeStruct((2, KEYVAL_HEADS, HEAD_WIDTH, positions), jnp.bfloat16),
-            jax.ShapeDtypeStruct(share, jnp.bfloat16),
-            jax.ShapeDtypeStruct((2, feed.shape[0], positions // 2), jnp.bfloat16),
+        in_specs=[vmem] * 16 + [anywhere] * 4,
+        out_specs=[vmem] * (3 + each),
+        out_shape=[jax.ShapeDtypeStruct(share, low_type), pairs, pairs] + [
+            jax.ShapeDtypeStruct((padded, w), low_type) for w in widths
         ],
-        scratch_shapes=[
-            pltpu.VMEM((len(gradients), 2, rows, columns), jnp.bfloat16),
-            pltpu.VMEM((len(gradients), 2, rows, columns), jnp.bfloat16),
-            pltpu.VMEM(share, jnp.bfloat16),
-            pltpu.VMEM(share, jnp.bfloat16),
-            pltpu.VMEM((KEYVAL_HEADS, blocks) + head, jnp.float32),
-            pltpu.VMEM((KEYVAL_HEADS, blocks - 1) + head, jnp.bfloat16),
-            pltpu.VMEM((KEYVAL_HEADS, blocks - 1) + head, jnp.bfloat16),
+        scratch_shapes=scratch + [
+            pltpu.VMEM((len(gradients), 2, rows, columns), low_type),
+            pltpu.VMEM((len(gradients), 2, rows, columns), low_type),
+            pltpu.VMEM(share, low_type),
+            pltpu.VMEM(share, low_type),
+            pltpu.VMEM((KEYVAL_HEADS, blocks) + head, low_type),
+            pltpu.VMEM((KEYVAL_HEADS, blocks - 1) + head, low_type),
             pltpu.VMEM((GROUP, HEAD_WIDTH, positions), jnp.float32),
             pltpu.VMEM((GROUP, 1, positions), jnp.float32),
             dma((len(gradients), 2)),
             dma((chunks, 2)), dma((chunks, 2)),
             dma((chunks,)), dma((chunks,)),
             dma((chunks,)), dma((chunks,)),
-            dma((rows // CHUNK_ROWS,)), dma((rows // CHUNK_ROWS,)),
+            dma((chunks,)), dma((chunks,)),
             dma((KEYVAL_HEADS, blocks - 1)), dma((KEYVAL_HEADS, blocks - 1)),
-            pltpu.VMEM(feed.shape, jnp.bfloat16),
-            pltpu.VMEM((feed.shape[0], positions // 2), jnp.bfloat16),
+            pltpu.VMEM(feed.shape, low_type),
+            pltpu.VMEM((features, positions // 2), low_type),
             dma, dma, dma, dma,
+            pltpu.VMEM((QUERY_WIDTH, positions), low_type),
+            pltpu.VMEM((2 * KEY_WIDTH, positions), low_type),
+            pltpu.VMEM((features, positions), jnp.float32),
+            pltpu.VMEM((features, positions // 2), low_type),
+            dma((count,)),
+            dma((each, 2)), dma((each, 2)),
+            dma((each,)), dma((each,)),
+            dma((each,)), dma((each,)),
+            dma((each, blocks - 1)), dma((each, blocks - 1)),
+            dma((each, blocks - 1)), dma((each, blocks - 1)),
+            dma((each,)), dma((each,)),
+            dma, dma,
         ],
         compiler_params=pltpu.CompilerParams(
             vmem_limit_bytes=KERNEL_VMEM, collective_id=0, has_side_effects=True
@@ -641,267 +870,10 @@
             flops=40 * HEAD_WIDTH * area, bytes_accessed=10 * query.size, transcendentals=area
         ),
         name="backward_sum",
-    )(query, keyval, back_mixed, mixed, lse, cosine, sine, base, feed, *gradients)
-
-
-def gradient_sum_kernel(out_ref, query_ref, keyval_ref, gains_ref, feed_ref, back_ref, *refs):
-    values = (out_ref, query_ref, keyval_ref)
-    chunks = len(values)
-    shares, (feed_share_ref, tokens_ref), refs = refs[:chunks], refs[chunks : chunks + 2], refs[chunks + 2 :]
-    own, mate_in, y_out, y_in, x_out, x_in, z_out, z_in = [
-        refs[i * chunks : (i + 1) * chunks] for i in range(8)
-    ]
-    (
-        own_sem, mate_send, mate_recv, y_send, y_recv, x_send, x_recv, z_send, z_recv,
-        all_send, all_recv, back_send, back_recv, down_send, down_recv, feed_sem,
-        token_send, token_recv, token_sem,
-    ) = refs[8 * chunks :]
-    place = lax.axis_index("ctx")
-    blocks = lax.axis_size("ctx")
-    last = blocks - 1
-    rank = lax.axis_index("fsdp")
-    side = lax.axis_index("tp")
-    core = rank % 2
-    y = rank // 2
-    mate = rank + 1 - 2 * core
-    across = rank + 2 - 4 * y
-    rows = shares[0].shape[0]
-    filled = values[0].shape[1]
-    half_rows = rows // 2
-    piece = half_rows // blocks
-    width = tokens_ref.shape[-1]
-
-    def columns(slot):
-        return back_ref.at[:, pl.ds(pl.multiple_of(slot * width, width), width)]
-
-    def own_copy(n, half):
-        return pltpu.make_async_copy(
-            values[n].at[2 * half + core], own[n].at[half, pl.ds(0, filled)], own_sem.at[n, half]
-        )
-
-    def own_gains(half):
-        return pltpu.make_async_copy(
-            gains_ref.at[2 * half + core], own[-1].at[half, pl.ds(filled, rows - filled)],
-            own_sem.at[chunks, half],
-        )
-
-    for half in range(2):
-        for n in range(chunks):
-            own_copy(n, half).start()
-        own_gains(half).start()
-    for n in range(chunks - 1):
-        tail = (2, rows - filled, own[n].shape[-1])
-        own[n][:, filled:] = jnp.zeros(tail, jnp.bfloat16)
-        mate_in[n][:, filled:] = jnp.zeros(tail, jnp.bfloat16)
-
-    greet(fsdp=mate)
-    greet(fsdp=across)
-    greet(tp=1 - side)
-    for d in range(1, blocks):
-        greet(ctx=lax.rem(place + d, blocks))
-    pl.semaphore_wait(pltpu.get_barrier_semaphore(), 2 + blocks)
-
-    def mate_copy(n, half):
-        return remote(
-            values[n].at[2 * half + 1 - core], mate_in[n].at[half, pl.ds(0, filled)],
-            mate_send.at[n, half], mate_recv.at[n, half], fsdp=mate,
-        )
-
-    def mate_gains(half):
-        return remote(
-            gains_ref.at[2 * half + 1 - core], mate_in[-1].at[half, pl.ds(filled, rows - filled)],
-            mate_send.at[chunks, half], mate_recv.at[chunks, half], fsdp=mate,
-        )
-
-    def y_copy(n):
-        return remote(y_out[n], y_in[n], y_send.at[n], y_recv.at[n], fsdp=across)
-
-    def x_copy(n):
-        other = pl.ds(pl.multiple_of((1 - side) * half_rows, half_rows), half_rows)
-        return remote(x_out[n].at[other], x_in[n], x_send.at[n], x_recv.at[n], tp=1 - side)
-
-    def z_copy(n, d):
-        target = lax.rem(place + d, blocks)
-        at = pl.ds(pl.multiple_of(target * piece, piece), piece)
-        return remote(
-            z_out[n].at[at], z_in[n].at[d - 1], z_send.at[n, d - 1], z_recv.at[n, d - 1],
-            ctx=target,
-        )
-
-    def all_copy(n, d, origin):
-        spot = shares[n].at[
-            pl.ds(pl.multiple_of(side * half_rows + origin * piece, piece), piece)
-        ]
-        return remote(
-            spot, spot, all_send.at[n, d - 1], all_recv.at[n, d - 1],
-            ctx=lax.rem(place + d, blocks),
-        )
-
-    def back_copy(n, half):
-        spot = shares[n].at[pl.ds(pl.multiple_of(half * half_rows, half_rows), half_rows)]
-        return remote(spot, spot, back_send.at[n], back_recv.at[n], tp=1 - side)
-
-    per = feed_ref.shape[1] // CHUNK_ROWS
-    returned = feed_share_ref.shape[0] * per
-
-    def feed_at(ref, k, skip):
-        return ref.at[k // per + skip, pl.ds(k % per * CHUNK_ROWS, CHUNK_ROWS)]
-
-    def down_copy(k, source):
-        return remote(
-            source, feed_at(feed_share_ref, k, 0), down_send.at[k], down_recv.at[k],
-            ctx=place - 1,
-        )
-
-    feed_copy = pltpu.make_async_copy(feed_ref.at[pl.ds(1, 2)], feed_share_ref, feed_sem)
-
-    def to_previous(k):
-        down_copy(k, feed_at(feed_share_ref, k, 0)).wait_recv()
-
-        @pl.when(place > 0)
-        def _():
-            down_copy(k, feed_at(feed_share_ref, k, 0)).start()
-
-    token_copy = remote(
-        columns(1 - side), tokens_ref.at[side], token_send, token_recv, tp=1 - side
-    )
-    token_own = pltpu.make_async_copy(columns(side), tokens_ref.at[side], token_sem)
-
-    for n in range(chunks):
-        for half in range(2):
-            mate_copy(n, half).start()
-    for half in range(2):
-        mate_gains(half).start()
-    token_own.start()
-
-    @pl.when(place == last)
-    def _():
-        for k in range(returned):
-            down_copy(k, feed_at(feed_ref, k, 1)).start()
-        feed_copy.start()
-
-    for half in range(2):
-        for n in range(chunks):
-            own_copy(n, half).wait()
-        own_gains(half).wait()
-
-    def to_y(n):
-        for half in range(2):
-            mate_copy(n, half).wait_recv()
-            if n == chunks - 1:
-                mate_gains(half).wait_recv()
-        y_out[n][...] = low(wide(own[n][1 - y]) + wide(mate_in[n][1 - y]))
-        y_copy(n).start()
-        if n == chunks - 1:
-            token_copy.start()
-
-    def to_x(n):
-        y_copy(n).wait_recv()
-        x_out[n][...] = low(wide(own[n][y]) + wide(mate_in[n][y]) + wide(y_in[n][...]))
-        x_copy(n).start()
-
-    def to_z(n):
-        x_copy(n).wait_recv()
-        at = pl.ds(pl.multiple_of(side * half_rows, half_rows), half_rows)
-        z_out[n][...] = low(wide(x_out[n][at]) + wide(x_in[n][...]))
-        for d in range(1, blocks):
-            z_copy(n, d).start()
-
-    def to_all(n):
-        total = wide(z_out[n][pl.ds(pl.multiple_of(place * piece, piece), piece)])
-        for d in range(1, blocks):
-            z_copy(n, d).wait_recv()
-            total += wide(z_in[n][d - 1])
-        at = pl.ds(pl.multiple_of(side * half_rows + place * piece, piece), piece)
-        shares[n][at] = low(total)
-        for d in range(1, blocks):
-            all_copy(n, d, place).start()
-
-    def to_back(n):
-        for d in range(1, blocks):
-            all_copy(n, d, lax.rem(place + blocks - d, blocks)).wait_recv()
-        back_copy(n, side).start()
-
-    def last_wait(n):
-        back_copy(n, 1 - side).wait_recv()
-
-    stages = (to_y, to_x, to_z, to_all, to_back, last_wait)
-    for t in range(max(chunks + len(stages), returned + last) - 1):
-        for index in reversed(range(len(stages))):
-            if 0 <= t - index < chunks:
-                stages[index](t - index)
-        for index in range(last):
-            if 0 <= t - last + 1 + index < returned:
-                @pl.when(place == index)
-                def _(k=t - last + 1 + index):
-                    to_previous(k)
-
-    @pl.when(place == last)
-    def _():
-        feed_copy.wait()
-
-    @pl.when(place > 0)
-    def _():
-        for k in range(returned):
-            down_copy(k, feed_at(feed_ref, k, 1)).wait_send()
-
-    for n in range(chunks):
-        for half in range(2):
-            mate_copy(n, half).wait_send()
-        y_copy(n).wait_send()
-        x_copy(n).wait_send()
-        for d in range(1, blocks):
-            z_copy(n, d).wait_send()
-            all_copy(n, d, place).wait_send()
-        back_copy(n, side).wait_send()
-    for half in range(2):
-        mate_gains(half).wait_send()
-    token_own.wait()
-    token_copy.wait()
-
-
-def gradient_sum(values, gains, feed, back):
-    filled = values[0].shape[1]
-    rows = filled + gains.shape[1]
-    widths = [value.shape[-1] for value in values]
-    chunks = len(values)
-    returned = (feed.shape[0] - 1) * feed.shape[1] // CHUNK_ROWS
-    blocks = lax.axis_size("ctx")
-    half_rows = rows // 2
-    dma = pltpu.SemaphoreType.DMA
-    anywhere = pl.BlockSpec(memory_space=pl.ANY)
-    vmem = pl.BlockSpec(memory_space=pltpu.VMEM)
-    scratch = []
-    for front in ((2, rows), (2, rows), (rows,), (rows,), (rows,), (half_rows,), (half_rows,),
-                  (blocks - 1, half_rows // blocks)):
-        scratch += [pltpu.VMEM(front + (w,), jnp.bfloat16) for w in widths]
-    return pl.pallas_call(
-        gradient_sum_kernel,
-        in_specs=[anywhere] * (chunks + 2) + [vmem],
-        out_specs=[vmem] * (chunks + 2),
-        out_shape=[jax.ShapeDtypeStruct((rows, w), jnp.bfloat16) for w in widths] + [
-            jax.ShapeDtypeStruct((feed.shape[0] - 1,) + feed.shape[1:], jnp.bfloat16),
-            jax.ShapeDtypeStruct((2, back.shape[0], back.shape[1] // 2), jnp.bfloat16),
-        ],
-        scratch_shapes=scratch + [
-            dma((chunks + 1, 2)),
-            dma((chunks + 1, 2)), dma((chunks + 1, 2)),
-            dma((chunks,)), dma((chunks,)),
-            dma((chunks,)), dma((chunks,)),
-            dma((chunks, blocks - 1)), dma((chunks, blocks - 1)),
-            dma((chunks, blocks - 1)), dma((chunks, blocks - 1)),
-            dma((chunks,)), dma((chunks,)),
-            dma((returned,)), dma((returned,)), dma,
-            dma, dma, dma,
-        ],
-        compiler_params=pltpu.CompilerParams(
-            vmem_limit_bytes=KERNEL_VMEM, collective_id=1, has_side_effects=True
-        ),
-        cost_estimate=pl.CostEstimate(
-            flops=back.size, bytes_accessed=20 * back.size, transcendentals=0
-        ),
-        name="gradient_sum",
-    )(*values, gains, feed, back)
+    )(
+        query, keyval, back_mixed, mixed, lse, cosine, sine, base, feed, tokens, normed, middle,
+        gains, gain_two, full_query, full_keyval, *gradients, gradient_out,
+    )
 
 
 def front_kernel(
@@ -1180,7 +1152,7 @@
             dma((blocks, KEYVAL_HEADS)), dma((blocks, KEYVAL_HEADS)),
         ],
         compiler_params=pltpu.CompilerParams(
-            vmem_limit_bytes=KERNEL_VMEM, collective_id=2, has_side_effects=True
+            vmem_limit_bytes=KERNEL_VMEM, collective_id=1, has_side_effects=True
         ),
         cost_estimate=pl.CostEstimate(
             flops=16 * HEAD_WIDTH * area, bytes_accessed=10 * tokens.size, transcendentals=area
@@ -1373,10 +1345,8 @@
     tokens_own, cotangent_own, cotangent_other, normed_one = [
         v.T for v in (tokens_own, cotangent_own, cotangent_other, normed_one)
     ]
-    gain_one = gains[:, 0].astype(jnp.float32)
     full_gain_two = gains[:, 1]
     inputs = tokens_own.astype(jnp.float32)
-    unit_one, inverse_one = normalize(inputs)
     mixed_low = mixed_heads.reshape(QUERY_WIDTH, token_positions)
     middle = inputs + dot(mixed_low, full_output, 0, 0)
 
@@ -1428,36 +1398,21 @@
     back_mixed = dot(full_output, back_attention, 1, 1).astype(jnp.bfloat16)
     back_mixed = back_mixed.reshape(query_low.shape)
     grad_output = dot(mixed_low, back_attention, 1, 0).astype(jnp.bfloat16)
-    back_query, back_keyval, share, result = backward_sum(
+    share, result, grad_tokens, share_output, share_query, share_keyval, share_gains = backward_sum(
         query_low, keyval, back_mixed, mixed_heads, lse, cosine, sine, base.T, feed_other.T,
-        gradients,
-    )
-    back_query = back_query.reshape(QUERY_WIDTH, token_positions)
-    back_keyval = back_keyval.reshape(2 * KEY_WIDTH, token_positions)
-    grad_query = dot(normed_one, back_query, 0, 1).astype(jnp.bfloat16)
-    grad_keyval = dot(normed_one, back_keyval, 0, 1).astype(jnp.bfloat16)
-    back_one = dot(back_query, full_query, 0, 1) + dot(back_keyval, full_keyval, 0, 1)
-    grad_gain_one = jnp.sum(back_one * unit_one, axis=0)
-    back_inputs = back_middle + norm_back(back_one * gain_one, unit_one, inverse_one)
-
-    gains = jnp.pad(
-        jnp.stack([grad_gain_one.reshape(parts, rows), grad_gain_two.reshape(parts, rows)], 1),
-        ((0, 0), (0, 14), (0, 2 * KEY_WIDTH - rows)),
-    )
-    share_output, share_query, share_keyval, share_rest, grad_tokens = gradient_sum(
-        [v.reshape(parts, rows, -1) for v in (grad_output, grad_query, grad_keyval)],
-        gains.astype(jnp.bfloat16), share, back_inputs.astype(jnp.bfloat16).T,
+        tokens_own.T, normed_one.T, back_middle.T, gains, grad_gain_two[:, None],
+        full_query, full_keyval, gradients, grad_output.reshape(parts, rows, -1),
     )
     return (
         result.swapaxes(1, 2),
         grad_tokens.swapaxes(1, 2).astype(jnp.float32),
-        share_keyval[rows, :rows].astype(jnp.float32),
+        share_gains[:rows, 0].astype(jnp.float32),
         share_query[:rows].astype(jnp.float32),
         share_keyval[:rows].astype(jnp.float32),
         share_output[:rows].astype(jnp.float32),
-        share_keyval[rows + 1, :rows].astype(jnp.float32),
-        share_rest[0].astype(jnp.float32),
-        share_rest[1].astype(jnp.float32),
+        share_gains[:rows, 1].astype(jnp.float32),
+        share[1].astype(jnp.float32),
+        share[2].astype(jnp.float32),
         share[0].astype(jnp.float32),
     )
 

time: 374 us -> 354 us (0.947)
  matrix products: 72.3 us -> 47.3 us
  other arithmetic: 17.9 us -> 9.97 us
  waiting for transfers between devices: 9.54 us -> 16.7 us
  Pallas kernels: 260 us -> 266 us
    dot_general x25 -> x21, matrix products: 72.3 us -> 47.3 us  [dot(): lax.dot_general(left, right, (((left_dim,), (right_dim,)), ((), ())), pre...]
    ppermute x2, waiting for transfers between devices: 9.54 us -> 16.7 us  [to_partner(): return lax.ppermute(value_rows, 'tp', pair)]
    pallas_call x2 -> x1, Pallas kernels: 176 us -> 182 us  [backward_sum(): pl.pallas_call(backward_sum_kernel, in_specs=[vmem] * 16 + [anywhere] * 4...]
  transfers between devices with their start and end apart: 2 -> 2, of which waited for: 1 -> 2; matrix products, arithmetic and copies ran while one was open for 11% -> 8% of each run, Pallas kernels for 0% -> 0%
where the time goes in v4:
time: 354 us; the launch traced here: 350 us
  Pallas kernels  266 us (75%)
  matrix products  47.3 us (13%)
  waiting for transfers between devices  16.7 us (5%)
  other arithmetic  9.97 us (3%)
  local copies, waits for them, and re-layouts  5.55 us (2%)
    pallas_call x1, Pallas kernels, backward_sum(): pl.pallas_call(backward_sum_kernel, in_specs=[vmem] * 16 + [anywhere] * 4...  182 us
    pallas_call x1, Pallas kernels, front(): pl.pallas_call(front_kernel, in_specs=[vmem] * (4 + count), out_specs=[vm...  84.3 us
    dot_general x21, matrix products, dot(): lax.dot_general(left, right, (((left_dim,), (right_dim,)), ((), ())), pre...  47.3 us
    ppermute x2, waiting for transfers between devices, to_partner(): return lax.ppermute(value_rows, 'tp', pair)  16.7 us
  transfers between devices with their start and end apart: 2, of which 2 were waited for; matrix products, arithmetic and copies ran while one was open for 8% of the time, Pallas kernels for 0%

profile of v4, /device:TPU:0, one launch (start us, length us, event | category | flops | bytes accessed | tf_op | source)
XLA Modules:
  0.0 349.6 jit_solution(5522139180343998956)
XLA Ops:
  3.8 84.3 %front.1 = (bf16[960,512]{1,0:T(8,128)(2,1)}, bf16[960,512]{1,0:T(8,128)(2,1)}, bf16[960,512]{1,0:T(8,128)(2,1)}, bf16[960,512]{1,0:T(8,128)(2,1)}, bf16[15,64,5...) custom-call(bf16[2,960,256]{2,1,0:T(8,128)(2,1)} %bitcast.107, ...), custom_call_target="tpu_custom_call" | custom-call | flops 16106127360 | bytes 4915200 | tf_op jit(solution)/shard_map/front/pallas_call | solution.py:1129
  88.1 3.4 multiply_reduce_fusion.2
  92.1 1.6 collective-permute-start
  93.7 1.6 fusion.7
  95.6 1.6 fusion.9
  97.2 1.6 fusion.6
  98.9 2.5 multiply_convert_fusion.1
  105.7 1.9 fusion.8
  107.6 2.7 fusion.3.base_ref
  110.3 6.0 %collective-permute-done = bf16[512,960]{0,1:T(8,128)(2,1)S(1)} collective-permute-done((bf16[512,960]{0,1:T(8,128)(2,1)S(1)}, bf16[512,960]{0,1:T(8,128)(2,1)S(1)}, u32[]{:S(2)}, u32[]{:S(2)}) %collective-permute-start) | collective-permute-done | bytes 983072 | tf_op jit(solution)/shard_map/ppermute | solution.py:1327
  116.4 1.6 fusion.10
  117.9 4.0 %multiply_convert_fusion = (bf16[512,1280]{1,0:T(8,128)(2,1)}, bf16[512,1280]{1,0:T(8,128)(2,1)}, bf16[512,1280]{1,0:T(8,128)(2,1)S(1)}) fusion(f32[512,1280]{1,0:T(8,128)S(1)} %fusion.10, f32[512,1280]{1,0:T(8,128)S(1)} %fusion.9, bf16[512,960]{0,1:T(8,128)(2,1)S(1)} %collective-permute-done, bf16[960,1280]{1,0:T(8,128)(2,1)S(1)} %bitcast.96), kind=kOutput, calls=%fused_computation.3 | convolution fusion | flops 1268121600 | bytes 12615680 | tf_op jit(solution)/shard_map/dot_general | solution.py:23
  121.9 2.8 fusion.11
  127.8 2.9 add_convert_fusion.2
  130.7 2.9 add_convert_fusion.1
  133.6 2.4 convolution_convert_fusion.1.feed_ref
  136.0 2.9 add_convert_fusion
  139.0 10.7 %collective-permute-done.1 = bf16[512,960]{0,1:T(8,128)(2,1)S(1)} collective-permute-done((bf16[512,960]{0,1:T(8,128)(2,1)S(1)}, bf16[512,960]{0,1:T(8,128)(2,1)S(1)}, u32[]{:S(2)}, u32[]{:S(2)}) %collective-permute-start.1) | collective-permute-done | bytes 983072 | tf_op jit(solution)/shard_map/ppermute | solution.py:1327
  149.7 2.2 multiply_reduce_fusion
  153.4 2.1 convolution_convert_fusion.2
  155.5 2.5 convolution_convert_fusion
  159.0 181.6 %backward_sum.1 = (bf16[3,240,1280]{2,1,0:T(8,128)(2,1)}, bf16[2,960,256]{2,1,0:T(8,128)(2,1)}, bf16[2,960,256]{2,1,0:T(8,128)(2,1)}, bf16[256,960]{1,0:T(8,128)...) custom-call(bf16[15,64,512]{2,1,0:T(8,128)(2,1)} %get-tuple-element.32.query_ref, ...), custom_call_target="tpu_custom_call" | custom-call | flops 40265318400 | bytes 4915200 | tf_op jit(solution)/shard_map/backward_sum/pallas_call | solution.py:828
  340.7 2.8 convert_bitcast_fusion.1
  345.1 1.9 bitcast_convert_fusion
  (59 shorter events, 18.2 us)
Async XLA Ops:
  88.1 3.5 copy-start.14
  88.1 3.7 %copy-start.3 = (bf16[960,512]{1,0:T(8,128)(2,1)S(1)}, bf16[960,512]{1,0:T(8,128)(2,1)}, u32[]{:S(2)}) copy-start(bf16[960,512]{1,0:T(8,128)(2,1)} %get-tuple-element.36.tokens_ref) | copy-start | bytes 2949124
  91.8 1.9 copy-start.1
  92.1 24.2 %collective-permute-start = (bf16[512,960]{0,1:T(8,128)(2,1)S(1)}, bf16[512,960]{0,1:T(8,128)(2,1)S(1)}, u32[]{:S(2)}, u32[]{:S(2)}) collective-permute-start(bf16[512,960]{0,1:T(8,128)(2,1)S(1)} %multiply_convert_fusion.6), channel_id=1, source_target_pairs={{0,1},{1,0},{2,3},{3,2},{4,5},{5,4},{6,7},{7,6},{8,9},{9,8},{10,11... | collective-permute-start | bytes 2949128 | tf_op jit(solution)/shard_map/ppermute | solution.py:1327
  93.7 1.7 copy-start
  93.7 1.9 copy-start.4
  95.6 1.6 copy-start.2
  97.2 1.7 copy-start.5
  124.7 3.0 copy-start.8
  126.2 23.4 %collective-permute-start.1 = (bf16[512,960]{0,1:T(8,128)(2,1)S(1)}, bf16[512,960]{0,1:T(8,128)(2,1)S(1)}, u32[]{:S(2)}, u32[]{:S(2)}) collective-permute-start(bf16[512,960]{0,1:T(8,128)(2,1)S(1)} %add_convert_fusion.3), channel_id=1, source_target_pairs={{0,1},{1,0},{2,3},{3,2},{4,5},{5,4},{6,7},{7,6},{8,9},{9,8},{10,11... | collective-permute-start | bytes 2949128 | tf_op jit(solution)/shard_map/ppermute | solution.py:1327
  127.8 2.9 copy-start.9
  151.8 1.5 copy-start.16
  153.4 2.2 copy-start.6
  153.4 2.2 copy-start.17
  340.6 2.8 copy-start.15
  340.6 3.6 %copy-start.13 = (bf16[256,640]{1,0:T(8,128)(2,1)S(1)}, bf16[256,640]{1,0:T(8,128)(2,1)}, u32[]{:S(2)}) copy-start(bf16[256,640]{1,0:T(8,128)(2,1)} %get-tuple-element.51) | copy-start | bytes 983044
  340.6 4.4 %copy-start.7 = (bf16[3,240,1280]{2,1,0:T(8,128)(2,1)S(1)}, bf16[3,240,1280]{2,1,0:T(8,128)(2,1)}, u32[]{:S(2)}) copy-start(bf16[3,240,1280]{2,1,0:T(8,128)(2,1)} %get-tuple-element.53) | copy-start | bytes 5529604
  345.1 1.9 copy-start.11
  345.1 1.9 copy-start.12
  347.0 1.5 copy-start.10

commit v5 on v4

--- a/solution.py
+++ b/solution.py
@@ -596,8 +596,10 @@
         def _():
             share_ref[m, at] = own[m, y, at]
 
-    def to_previous(k):
-        down_copy(k).wait_recv()
+    def give_back(k):
+        @pl.when(place < last)
+        def _():
+            down_copy(k).wait_recv()
 
         @pl.when(place > 0)
         def _():
@@ -622,15 +624,11 @@
         def _():
             to_next(b // 2)
 
-        c = t - KEYVAL_HEADS * blocks - (last - place)
-
-        @pl.when((place == last) & (c >= 0) & (c < chunks))
-        def _():
-            down_copy(c).start()
-
-        @pl.when((place < last) & (c >= 0) & (c < early))
-        def _():
-            to_previous(c)
+        c = t - KEYVAL_HEADS * blocks - 2 * (last - place)
+
+        @pl.when((c >= 0) & (c < 2 * early) & (lax.rem(c, 2) == 0))
+        def _():
+            give_back(c // 2)
 
         for at, stage, n in (
             (chunks + 1, to_y, 0), (20, query_gradient, 1), (20, to_x, 0), (21, to_y, 1),
@@ -758,13 +756,13 @@
     for slot, stages in enumerate(later):
         for stage, n in stages:
             stage(n)
-        for index in range(last):
-            if early <= early + slot - last + 1 + index < chunks:
+        for index in range(blocks):
+            if early <= early + slot - last + index < chunks:
                 @pl.when(place == index)
-                def _(k=early + slot - last + 1 + index):
-                    to_previous(k)
-
-    assert len(later) >= chunks - early + last - 1
+                def _(k=early + slot - last + index):
+                    give_back(k)
+
+    assert len(later) >= chunks - early + last
     for n in range(chunks_in):
         finish_sum(n)
     token_copy.wait()
@@ -882,13 +880,14 @@
     weights, refs = refs[:7], refs[7:]
     (
         tokens_own, cotangent_own, cotangent_other, normed_out, query_out, keyval_ref,
-        mixed_out, lse_ref,
-    ), refs = refs[:8], refs[8:]
+        mixed_out, lse_ref, tokens_other, mixed_other,
+    ), refs = refs[:10], refs[10:]
     full, refs = refs[:7], refs[7:]
     (
         raw, tops, totals, sums,
         local_sem, token_send, token_recv, cot_send, cot_recv,
         y_send, y_recv, mate_send, mate_recv, pass_send, pass_recv, key_send, key_recv,
+        mixed_send, mixed_recv,
     ) = refs
     place = lax.axis_index("ctx")
     last = lax.axis_size("ctx") - 1
@@ -910,9 +909,12 @@
         pltpu.make_async_copy(
             cotangent_ref.at[1 - side], columns(cotangent_other, side), local_sem.at[2]
         ),
+        pltpu.make_async_copy(
+            tokens_ref.at[1 - side], columns(tokens_other, side), local_sem.at[3]
+        ),
     ]
     for w in range(len(weights)):
-        local.append(pltpu.make_async_copy(weights[w], full[w].at[rank], local_sem.at[3 + w]))
+        local.append(pltpu.make_async_copy(weights[w], full[w].at[rank], local_sem.at[4 + w]))
     for copy in local:
         copy.start()
 
@@ -943,7 +945,19 @@
             cotangent_ref.at[side], columns(cotangent_other, side), cot_send.at[1],
             cot_recv.at[1], tp=1 - side,
         ),
+        remote(
+            tokens_ref.at[side], columns(tokens_other, side), cot_send.at[2], cot_recv.at[2],
+            tp=1 - side,
+        ),
     ]
+
+    def mixed_copy(j):
+        heads = pl.ds(GROUP * j, GROUP)
+        return remote(
+            mixed_out.at[heads], mixed_other.at[heads], mixed_send.at[j], mixed_recv.at[j],
+            tp=1 - side,
+        )
+
 
     def y_copy(w):
         return remote(
@@ -961,7 +975,7 @@
         )
 
     def arrived(w):
-        local[3 + w].wait()
+        local[4 + w].wait()
         mate_copy(w).wait_recv()
         pass_copy(w).wait_recv()
 
@@ -1066,8 +1080,21 @@
             def _():
                 key_copy(s + 1, j).start()
 
+    def finish_heads(j):
+        for g in range(GROUP):
+            head = GROUP * j + g
+            total = totals[head]
+            mixed_out[head] = low(sums[head] / total)
+            lse_ref[head] = tops[head] + jnp.log(total)
+        mixed_copy(j).start()
+
     def first_block(j, carry):
         attend(0, j, True)
+
+        @pl.when(place == 0)
+        def _():
+            finish_heads(j)
+
         hand_on(0, j)
         return carry
 
@@ -1078,24 +1105,23 @@
         s = 1 + i // KEYVAL_HEADS
         j = lax.rem(i, KEYVAL_HEADS)
         attend(s, j, False)
+
+        @pl.when(s == place)
+        def _():
+            finish_heads(j)
+
         hand_on(s, j)
         return carry
 
     lax.fori_loop(0, place * KEYVAL_HEADS, later_block, 0)
-
-    def divide(h, carry):
-        total = totals[h]
-        mixed_out[h] = low(sums[h] / total)
-        lse_ref[h] = tops[h] + jnp.log(total)
-        return carry
-
-    lax.fori_loop(0, QUERY_HEADS, divide, 0)
 
     for w in range(passed, 6):
         y_copy(w).wait_recv()
         pass_copy(w).start()
-    local[1].wait()
-    local[2].wait()
+    for copy in local[1:4]:
+        copy.wait()
+    for j in range(KEYVAL_HEADS):
+        mixed_copy(j).wait()
     token_copy.wait_send()
     for copy in cot_copies:
         copy.wait()
@@ -1129,7 +1155,7 @@
     return pl.pallas_call(
         front_kernel,
         in_specs=[vmem] * (4 + count),
-        out_specs=[vmem] * 8 + [vmem] * 2 + [anywhere] * 4 + [vmem],
+        out_specs=[vmem] * 12 + [anywhere] * 4 + [vmem],
         out_shape=[
             shape(features, positions), shape(features, positions), shape(features, positions),
             shape(features, positions),
@@ -1137,19 +1163,22 @@
             shape(blocks, KEYVAL_HEADS, 2, HEAD_WIDTH, positions),
             shape(QUERY_HEADS, HEAD_WIDTH, positions),
             jax.ShapeDtypeStruct((QUERY_HEADS, 1, positions), jnp.float32),
+            shape(features, positions),
+            shape(QUERY_HEADS, HEAD_WIDTH, positions),
         ] + [shape(parts, *w.shape) for w in weights],
         scratch_shapes=[
             pltpu.VMEM((QUERY_WIDTH, positions), jnp.float32),
             pltpu.VMEM((QUERY_HEADS, 1, positions), jnp.float32),
             pltpu.VMEM((QUERY_HEADS, 1, positions), jnp.float32),
             pltpu.VMEM((QUERY_HEADS, HEAD_WIDTH, positions), jnp.float32),
-            dma((3 + count,)),
+            dma((4 + count,)),
             dma, dma,
-            dma((2,)), dma((2,)),
+            dma((3,)), dma((3,)),
             dma((count,)), dma((count,)),
             dma((count,)), dma((count,)),
             dma((count,)), dma((count,)),
             dma((blocks, KEYVAL_HEADS)), dma((blocks, KEYVAL_HEADS)),
+            dma((KEYVAL_HEADS,)), dma((KEYVAL_HEADS,)),
         ],
         compiler_params=pltpu.CompilerParams(
             vmem_limit_bytes=KERNEL_VMEM, collective_id=1, has_side_effects=True
@@ -1334,7 +1363,7 @@
     gains = jnp.pad(jnp.stack([input_gain, middle_gain], 1), ((0, 0), (0, 126)))
     (
         tokens_own, cotangent_own, cotangent_other, normed_one, query_low, keyval,
-        mixed_heads, lse, *full,
+        mixed_heads, lse, tokens_other, mixed_other, *full,
     ) = front(
         tokens.swapaxes(1, 2), cotangent.swapaxes(1, 2), cosine, sine,
         (w_query, w_keyval, w_output, w_gate, w_up, w_down, gains),
@@ -1342,8 +1371,8 @@
     full_query, full_keyval, full_output, full_gate, full_up, full_down, gains = [
         w.reshape(width_in, -1) for w in full
     ]
-    tokens_own, cotangent_own, cotangent_other, normed_one = [
-        v.T for v in (tokens_own, cotangent_own, cotangent_other, normed_one)
+    tokens_own, cotangent_own, cotangent_other, normed_one, tokens_other = [
+        v.T for v in (tokens_own, cotangent_own, cotangent_other, normed_one, tokens_other)
     ]
     full_gain_two = gains[:, 1]
     inputs = tokens_own.astype(jnp.float32)
@@ -1353,7 +1382,9 @@
     gain_two = full_gain_two.astype(jnp.float32)
     unit_two, inverse_two = normalize(middle)
     normed_two = (unit_two * gain_two).astype(jnp.bfloat16)
-    normed_other = to_partner(normed_two)
+    mixed_other = mixed_other.reshape(QUERY_WIDTH, token_positions)
+    middle_other = tokens_other.astype(jnp.float32) + dot(mixed_other, full_output, 0, 0)
+    normed_other = (normalize(middle_other)[0] * gain_two).astype(jnp.bfloat16)
 
     def feed(rows, back_rows):
         gate_proj = dot(rows, full_gate, 1, 0)
@@ -1371,11 +1402,11 @@
     def feed_input_back(back_gate, back_up):
         return dot(back_gate, full_gate, 1, 1) + dot(back_up, full_up, 1, 1)
 
-    hidden_own, back_gate_own, back_up_own = feed(normed_two, cotangent_own)
     hidden_other, back_gate_other, back_up_other = feed(normed_other, cotangent_other)
     back_two_received = to_partner(
         feed_input_back(back_gate_other, back_up_other).astype(jnp.bfloat16)
     )
+    hidden_own, back_gate_own, back_up_own = feed(normed_two, cotangent_own)
     back_two = feed_input_back(back_gate_own, back_up_own) + back_two_received.astype(jnp.float32)
     feed_other = dot(hidden_other, full_down, 1, 1).astype(jnp.bfloat16)
     base = middle + dot(hidden_own, full_down, 1, 1)

time: 354 us -> 345 us (0.975)
  waiting for transfers between devices: 16.7 us -> 0.01 us
  Pallas kernels: 266 us -> 274 us
    ppermute x2 -> x1, waiting for transfers between devices: 16.7 us -> 0.01 us  [to_partner(): return lax.ppermute(value_rows, 'tp', pair)]
    pallas_call x1, Pallas kernels: 182 us -> 189 us  [backward_sum(): pl.pallas_call(backward_sum_kernel, in_specs=[vmem] * 16 + [anywhere] * 4...]
    dot_general x21 -> x22, matrix products: 47.3 us -> 46 us  [dot(): lax.dot_general(left, right, (((left_dim,), (right_dim,)), ((), ())), pre...]
  transfers between devices with their start and end apart: 2 -> 1, of which waited for: 2 -> 0; matrix products, arithmetic and copies ran while one was open for 8% -> 8% of each run, Pallas kernels for 0% -> 0%
where the time goes in v5:
time: 345 us; the launch traced here: 340 us
  Pallas kernels  274 us (79%)
  matrix products  46 us (13%)
  other arithmetic  11.7 us (3%)
  local copies, waits for them, and re-layouts  5.74 us (2%)
    pallas_call x1, Pallas kernels, backward_sum(): pl.pallas_call(backward_sum_kernel, in_specs=[vmem] * 16 + [anywhere] * 4...  189 us
    pallas_call x1, Pallas kernels, front(): pl.pallas_call(front_kernel, in_specs=[vmem] * (4 + count), out_specs=[vm...  85.1 us
    dot_general x22, matrix products, dot(): lax.dot_general(left, right, (((left_dim,), (right_dim,)), ((), ())), pre...  46 us
  transfers between devices with their start and end apart: 1, of which 0 were waited for; matrix products, arithmetic and copies ran while one was open for 8% of the time, Pallas kernels for 0%

profile of v5, /device:TPU:0, one launch (start us, length us, event | category | flops | bytes accessed | tf_op | source)
XLA Modules:
  0.0 339.8 jit_solution(17541086616555483978)
XLA Ops:
  3.8 85.1 %front.1 = (bf16[960,512]{1,0:T(8,128)(2,1)}, bf16[960,512]{1,0:T(8,128)(2,1)}, bf16[960,512]{1,0:T(8,128)(2,1)}, bf16[960,512]{1,0:T(8,128)(2,1)}, bf16[15,64,5...) custom-call(bf16[2,960,256]{2,1,0:T(8,128)(2,1)} %bitcast.112, ...), custom_call_target="tpu_custom_call" | custom-call | flops 16106127360 | bytes 4915200 | tf_op jit(solution)/shard_map/front/pallas_call | solution.py:1155
  90.1 3.5 %multiply_reduce_fusion.2 = (f32[512]{0:T(512)S(1)}, f32[512,960]{0,1:T(8,128)S(1)}) fusion(bf16[960,512]{1,0:T(8,128)(2,1)} %bitcast.123, bf16[960,960]{1,0:T(8,128)(2,1)} %bitcast.115, bf16[960,512]{1,0:T(8,128)(2,1)} %get-tuple-element.45), kind=kOutput, calls=%fused_computation.25 | convolution fusion | flops 945683968 | bytes 5777408 | tf_op jit(solution)/shard_map/dot_general | solution.py:23
  96.6 1.6 fusion.10
  98.5 1.6 fusion.9
  100.2 2.5 multiply_convert_fusion
  102.7 1.5 fusion.11
  104.2 1.5 add_convert_fusion.3
  105.7 1.6 collective-permute-start
  107.2 1.6 fusion.7
  108.8 2.0 fusion.6
  110.8 2.5 multiply_convert_fusion.1
  113.3 1.4 fusion.12
  116.2 2.9 add_convert_fusion.1
  120.6 2.9 add_convert_fusion
  123.5 2.9 add_convert_fusion.2
  126.4 1.5 fusion.8
  127.9 2.4 convolution_convert_fusion.1.feed_ref
  130.3 2.9 fusion.3.base_ref
  133.2 2.1 multiply_reduce_fusion
  136.0 2.2 convolution_convert_fusion.2
  138.1 2.5 convolution_convert_fusion
  141.6 188.7 %backward_sum.1 = (bf16[3,240,1280]{2,1,0:T(8,128)(2,1)}, bf16[2,960,256]{2,1,0:T(8,128)(2,1)}, bf16[2,960,256]{2,1,0:T(8,128)(2,1)}, bf16[256,960]{1,0:T(8,128)...) custom-call(bf16[15,64,512]{2,1,0:T(8,128)(2,1)} %get-tuple-element.34.query_ref, ...), custom_call_target="tpu_custom_call" | custom-call | flops 40265318400 | bytes 4915200 | tf_op jit(solution)/shard_map/backward_sum/pallas_call | solution.py:826
  330.3 2.7 convert_bitcast_fusion.1
  336.8 1.9 bitcast_convert_fusion
  (53 shorter events, 16.9 us)
Async XLA Ops:
  90.0 3.5 %copy-start.3 = (bf16[960,512]{1,0:T(8,128)(2,1)S(1)}, bf16[960,512]{1,0:T(8,128)(2,1)}, u32[]{:S(2)}) copy-start(bf16[960,512]{1,0:T(8,128)(2,1)} %get-tuple-element.38.tokens_ref) | copy-start | bytes 2949124
  90.1 3.5 %copy-start.13 = (bf16[4,240,960]{2,1,0:T(8,128)(2,1)S(1)}, bf16[4,240,960]{2,1,0:T(8,128)(2,1)}, u32[]{:S(2)}) copy-start(bf16[4,240,960]{2,1,0:T(8,128)(2,1)} %get-tuple-element.36) | copy-start | bytes 5529604
  90.1 3.5 %copy-start.14 = (bf16[15,64,512]{2,1,0:T(8,128)(2,1)S(1)}, bf16[15,64,512]{2,1,0:T(8,128)(2,1)}, u32[]{:S(2)}) copy-start(bf16[15,64,512]{2,1,0:T(8,128)(2,1)} %get-tuple-element.39.mixed_ref) | copy-start | bytes 2949124
  94.9 1.7 copy-start.1
  96.6 1.7 copy-start
  96.6 1.9 copy-start.4
  98.5 1.7 copy-start.5
  105.7 27.6 %collective-permute-start = (bf16[512,960]{0,1:T(8,128)(2,1)S(1)}, bf16[512,960]{0,1:T(8,128)(2,1)S(1)}, u32[]{:S(2)}, u32[]{:S(2)}) collective-permute-start(bf16[512,960]{0,1:T(8,128)(2,1)S(1)} %add_convert_fusion.3), channel_id=1, source_target_pairs={{0,1},{1,0},{2,3},{3,2},{4,5},{5,4},{6,7},{7,6},{8,9},{9,8},{10,11... | collective-permute-start | bytes 2949128 | tf_op jit(solution)/shard_map/ppermute | solution.py:1356
  107.2 1.6 copy-start.2
  136.0 2.2 copy-start.6
  330.3 2.7 copy-start.12
  330.3 3.5 %copy-start.10 = (bf16[256,960]{1,0:T(8,128)(2,1)S(1)}, bf16[256,960]{1,0:T(8,128)(2,1)}, u32[]{:S(2)}) copy-start(bf16[256,960]{1,0:T(8,128)(2,1)} %get-tuple-element.54) | copy-start | bytes 1474564
  330.3 4.5 %copy-start.11 = (bf16[256,640]{1,0:T(8,128)(2,1)S(1)}, bf16[256,640]{1,0:T(8,128)(2,1)}, u32[]{:S(2)}) copy-start(bf16[256,640]{1,0:T(8,128)(2,1)} %get-tuple-element.55) | copy-start | bytes 983044
  333.0 2.7 copy-start.9
  333.8 3.0 copy-start.7
  336.8 1.9 copy-start.8

commit v6 on v5

--- a/solution.py
+++ b/solution.py
@@ -329,7 +329,7 @@
     rows = share_ref.shape[1]
     per = rows // CHUNK_ROWS
     chunks = len(gradients) * per
-    early = per
+    early = 2 * per
 
     for m, gradient in enumerate(gradients):
         for half in range(2):
@@ -614,26 +614,26 @@
         def _():
             to_across(t)
 
-        @pl.when(t == chunks)
+        @pl.when(t == chunks + 1)
         def _():
             finish_result()
 
-        b = t - 3 - 2 * place
+        b = t - 4 - 2 * place
 
         @pl.when((b >= 0) & (b < 2 * chunks) & (lax.rem(b, 2) == 0))
         def _():
             to_next(b // 2)
 
-        c = t - KEYVAL_HEADS * blocks - 2 * (last - place)
+        c = t - 6 - 3 * last - 2 * (last - place)
 
         @pl.when((c >= 0) & (c < 2 * early) & (lax.rem(c, 2) == 0))
         def _():
             give_back(c // 2)
 
         for at, stage, n in (
-            (chunks + 1, to_y, 0), (20, query_gradient, 1), (20, to_x, 0), (21, to_y, 1),
-            (22, to_z, 0), (24, to_all, 0), (26, to_x, 1), (26, to_back, 0), (28, to_z, 1),
-            (30, to_all, 1),
+            (4, to_y, 0), (15, to_x, 0), (18, to_z, 0), (20, query_gradient, 1),
+            (20, to_all, 0), (21, to_y, 1), (23, to_back, 0), (25, to_x, 1), (27, to_z, 1),
+            (29, to_all, 1),
         ):
             @pl.when(t == at)
             def _(stage=stage, n=n):
@@ -1029,9 +1029,10 @@
         first = KEY_WIDTH + j * HEAD_WIDTH
         keyval_ref[0, j, 1] = low(raw[first : first + HEAD_WIDTH])
 
-        @pl.when(place < last)
-        def _(j=j):
-            key_copy(0, j).start()
+        if j == 0:
+            @pl.when(place < last)
+            def _():
+                key_copy(0, 0).start()
 
     arrived(0)
     matrix = full[0][...].reshape(-1, QUERY_WIDTH)
@@ -1088,32 +1089,25 @@
             lse_ref[head] = tops[head] + jnp.log(total)
         mixed_copy(j).start()
 
-    def first_block(j, carry):
+    def one_head(j, carry):
+        @pl.when((place < last) & (j + 1 < KEYVAL_HEADS))
+        def _():
+            key_copy(0, j + 1).start()
+
         attend(0, j, True)
-
-        @pl.when(place == 0)
-        def _():
-            finish_heads(j)
-
         hand_on(0, j)
+
+        def later_block(s, inner):
+            attend(s, j, False)
+            hand_on(s, j)
+            return inner
+
+        lax.fori_loop(1, place + 1, later_block, 0)
+        finish_heads(j)
         return carry
 
-    lax.fori_loop(0, KEYVAL_HEADS, first_block, 0)
+    lax.fori_loop(0, KEYVAL_HEADS, one_head, 0)
     passed = 2
-
-    def later_block(i, carry):
-        s = 1 + i // KEYVAL_HEADS
-        j = lax.rem(i, KEYVAL_HEADS)
-        attend(s, j, False)
-
-        @pl.when(s == place)
-        def _():
-            finish_heads(j)
-
-        hand_on(s, j)
-        return carry
-
-    lax.fori_loop(0, place * KEYVAL_HEADS, later_block, 0)
 
     for w in range(passed, 6):
         y_copy(w).wait_recv()

time: 345 us -> 334 us (0.968)
  Pallas kernels: 274 us -> 263 us
    pallas_call x1, Pallas kernels: 189 us -> 178 us  [backward_sum(): pl.pallas_call(backward_sum_kernel, in_specs=[vmem] * 16 + [anywhere] * 4...]
where the time goes in v6:
time: 334 us; the launch traced here: 329 us
  Pallas kernels  263 us (79%)
  matrix products  46 us (14%)
  other arithmetic  11.7 us (4%)
  local copies, waits for them, and re-layouts  5.74 us (2%)
    pallas_call x1, Pallas kernels, backward_sum(): pl.pallas_call(backward_sum_kernel, in_specs=[vmem] * 16 + [anywhere] * 4...  178 us
    pallas_call x1, Pallas kernels, front(): pl.pallas_call(front_kernel, in_specs=[vmem] * (4 + count), out_specs=[vm...  85.1 us
    dot_general x22, matrix products, dot(): lax.dot_general(left, right, (((left_dim,), (right_dim,)), ((), ())), pre...  46 us
  transfers between devices with their start and end apart: 1, of which 0 were waited for; matrix products, arithmetic and copies ran while one was open for 8% of the time, Pallas kernels for 0%

profile of v6, /device:TPU:0, one launch (start us, length us, event | category | flops | bytes accessed | tf_op | source)
XLA Modules:
  0.0 329.4 jit_solution(1402112298200859345)
XLA Ops:
  3.8 85.1 %front.1 = (bf16[960,512]{1,0:T(8,128)(2,1)}, bf16[960,512]{1,0:T(8,128)(2,1)}, bf16[960,512]{1,0:T(8,128)(2,1)}, bf16[960,512]{1,0:T(8,128)(2,1)}, bf16[15,64,5...) custom-call(bf16[2,960,256]{2,1,0:T(8,128)(2,1)} %bitcast.112, ...), custom_call_target="tpu_custom_call" | custom-call | flops 16106127360 | bytes 4915200 | tf_op jit(solution)/shard_map/front/pallas_call | solution.py:1149
  90.1 3.5 %multiply_reduce_fusion.2 = (f32[512]{0:T(512)S(1)}, f32[512,960]{0,1:T(8,128)S(1)}) fusion(bf16[960,512]{1,0:T(8,128)(2,1)} %bitcast.123, bf16[960,960]{1,0:T(8,128)(2,1)} %bitcast.115, bf16[960,512]{1,0:T(8,128)(2,1)} %get-tuple-element.45), kind=kOutput, calls=%fused_computation.25 | convolution fusion | flops 945683968 | bytes 5777408 | tf_op jit(solution)/shard_map/dot_general | solution.py:23
  96.6 1.6 fusion.10
  98.5 1.6 fusion.9
  100.2 2.5 multiply_convert_fusion
  102.7 1.5 fusion.11
  104.2 1.5 add_convert_fusion.3
  105.7 1.6 collective-permute-start
  107.2 1.6 fusion.7
  108.8 2.0 fusion.6
  110.8 2.5 multiply_convert_fusion.1
  113.3 1.4 fusion.12
  116.2 2.9 add_convert_fusion.1
  120.6 2.9 add_convert_fusion
  123.5 2.9 add_convert_fusion.2
  126.4 1.5 fusion.8
  127.9 2.4 convolution_convert_fusion.1.feed_ref
  130.3 2.9 fusion.3.base_ref
  133.2 2.1 multiply_reduce_fusion
  136.0 2.2 convolution_convert_fusion.2
  138.1 2.5 convolution_convert_fusion
  141.6 178.2 %backward_sum.1 = (bf16[3,240,1280]{2,1,0:T(8,128)(2,1)}, bf16[2,960,256]{2,1,0:T(8,128)(2,1)}, bf16[2,960,256]{2,1,0:T(8,128)(2,1)}, bf16[256,960]{1,0:T(8,128)...) custom-call(bf16[15,64,512]{2,1,0:T(8,128)(2,1)} %get-tuple-element.34.query_ref, ...), custom_call_target="tpu_custom_call" | custom-call | flops 40265318400 | bytes 4915200 | tf_op jit(solution)/shard_map/backward_sum/pallas_call | solution.py:826
  319.9 2.7 convert_bitcast_fusion.1
  326.3 1.9 bitcast_convert_fusion
  (53 shorter events, 16.9 us)
Async XLA Ops:
  90.0 3.5 %copy-start.3 = (bf16[960,512]{1,0:T(8,128)(2,1)S(1)}, bf16[960,512]{1,0:T(8,128)(2,1)}, u32[]{:S(2)}) copy-start(bf16[960,512]{1,0:T(8,128)(2,1)} %get-tuple-element.38.tokens_ref) | copy-start | bytes 2949124
  90.1 3.5 %copy-start.13 = (bf16[4,240,960]{2,1,0:T(8,128)(2,1)S(1)}, bf16[4,240,960]{2,1,0:T(8,128)(2,1)}, u32[]{:S(2)}) copy-start(bf16[4,240,960]{2,1,0:T(8,128)(2,1)} %get-tuple-element.36) | copy-start | bytes 5529604
  90.1 3.5 %copy-start.14 = (bf16[15,64,512]{2,1,0:T(8,128)(2,1)S(1)}, bf16[15,64,512]{2,1,0:T(8,128)(2,1)}, u32[]{:S(2)}) copy-start(bf16[15,64,512]{2,1,0:T(8,128)(2,1)} %get-tuple-element.39.mixed_ref) | copy-start | bytes 2949124
  94.9 1.7 copy-start.1
  96.6 1.7 copy-start
  96.6 1.9 copy-start.4
  98.5 1.7 copy-start.5
  105.7 27.6 %collective-permute-start = (bf16[512,960]{0,1:T(8,128)(2,1)S(1)}, bf16[512,960]{0,1:T(8,128)(2,1)S(1)}, u32[]{:S(2)}, u32[]{:S(2)}) collective-permute-start(bf16[512,960]{0,1:T(8,128)(2,1)S(1)} %add_convert_fusion.3), channel_id=1, source_target_pairs={{0,1},{1,0},{2,3},{3,2},{4,5},{5,4},{6,7},{7,6},{8,9},{9,8},{10,11... | collective-permute-start | bytes 2949128 | tf_op jit(solution)/shard_map/ppermute | solution.py:1350
  107.2 1.6 copy-start.2
  136.0 2.2 copy-start.6
  319.8 2.7 copy-start.12
  319.9 3.5 %copy-start.10 = (bf16[256,960]{1,0:T(8,128)(2,1)S(1)}, bf16[256,960]{1,0:T(8,128)(2,1)}, u32[]{:S(2)}) copy-start(bf16[256,960]{1,0:T(8,128)(2,1)} %get-tuple-element.54) | copy-start | bytes 1474564
  319.9 4.5 %copy-start.11 = (bf16[256,640]{1,0:T(8,128)(2,1)S(1)}, bf16[256,640]{1,0:T(8,128)(2,1)}, u32[]{:S(2)}) copy-start(bf16[256,640]{1,0:T(8,128)(2,1)} %get-tuple-element.55) | copy-start | bytes 983044
  322.6 2.7 copy-start.9
  323.3 3.0 copy-start.7
  326.3 1.9 copy-start.8

commit v7 on v6

--- a/solution.py
+++ b/solution.py
@@ -329,7 +329,8 @@
     rows = share_ref.shape[1]
     per = rows // CHUNK_ROWS
     chunks = len(gradients) * per
-    early = 2 * per
+    iterations = KEYVAL_HEADS + 2
+    early = iterations * blocks // 2 - KEYVAL_HEADS * blocks // 2
 
     for m, gradient in enumerate(gradients):
         for half in range(2):
@@ -610,6 +611,12 @@
         to_mate(n)
 
     def tick(t):
+        h = t - last - 2 * (last - place)
+
+        @pl.when((h >= 0) & (h < KEYVAL_HEADS * blocks) & (lax.rem(h, blocks) == 0))
+        def _():
+            hand_on(h // blocks)
+
         @pl.when(t < chunks)
         def _():
             to_across(t)
@@ -624,16 +631,15 @@
         def _():
             to_next(b // 2)
 
-        c = t - 6 - 3 * last - 2 * (last - place)
-
-        @pl.when((c >= 0) & (c < 2 * early) & (lax.rem(c, 2) == 0))
+        c = t - KEYVAL_HEADS * blocks - 2 * (last - place)
+
+        @pl.when((c >= 0) & (c < 2 * chunks) & (lax.rem(c, 2) == 0))
         def _():
             give_back(c // 2)
 
         for at, stage, n in (
             (4, to_y, 0), (15, to_x, 0), (18, to_z, 0), (20, query_gradient, 1),
-            (20, to_all, 0), (21, to_y, 1), (23, to_back, 0), (25, to_x, 1), (27, to_z, 1),
-            (29, to_all, 1),
+            (20, to_all, 0), (21, to_y, 1), (22, to_back, 0), (24, to_x, 1), (26, to_z, 1),
         ):
             @pl.when(t == at)
             def _(stage=stage, n=n):
@@ -672,6 +678,10 @@
             back_value += dot(back, low(weights), 1, 1)
         parts[j, s, 0] = low(back_key)
         parts[j, s, 1] = low(back_value)
+        if not masked:
+            @pl.when(place == last)
+            def _():
+                part_copy(j, s).start()
 
     def hand_on(j):
         for s in range(blocks):
@@ -687,7 +697,9 @@
                         parts[j, s, kind] = low(total)
 
                 if s > 0:
-                    part_copy(j, s).start()
+                    @pl.when(place < last)
+                    def _():
+                        part_copy(j, s).start()
                 else:
                     leading = wide(parts[j, 0, 0, :HALF])
                     trailing = wide(parts[j, 0, 0, HALF:])
@@ -733,36 +745,30 @@
                     trailing * cosine - leading * sine
                 )
 
-        ready = j - (last - place)
-
-        @pl.when((ready >= 0) & (ready < KEYVAL_HEADS))
-        def _():
-            hand_on(ready)
-
         return carry
 
-    assert (KEYVAL_HEADS + last) * blocks >= 4 + 4 * last + 2 * (chunks - 1)
-    lax.fori_loop(0, KEYVAL_HEADS + last, head_loop, 0)
+    assert iterations * blocks > 4 + 2 * last + 2 * (chunks - 1)
+    lax.fori_loop(0, iterations, head_loop, 0)
 
     def keyval_gradient(n):
         weight_gradient(n, back_keyval_ref)
         to_mate(n)
 
     later = (
-        ((keyval_gradient, 2), (to_back, 1)), ((to_y, 2),), ((lambda n: input_gradient(), 3),),
-        ((to_x, 2),), ((to_y, 3),), ((to_z, 2), (to_x, 3)), ((to_all, 2), (to_z, 3)),
+        ((keyval_gradient, 2), (to_y, 2)), ((to_all, 1),), ((lambda n: input_gradient(), 3),),
+        ((to_x, 2), (to_back, 1)), ((to_y, 3),), ((to_z, 2), (to_x, 3)), ((to_all, 2), (to_z, 3)),
         ((to_back, 2), (to_all, 3)), ((to_back, 3),),
     )
     for slot, stages in enumerate(later):
         for stage, n in stages:
             stage(n)
         for index in range(blocks):
-            if early <= early + slot - last + index < chunks:
+            if early + slot - last + index < chunks:
                 @pl.when(place == index)
                 def _(k=early + slot - last + index):
                     give_back(k)
 
-    assert len(later) >= chunks - early + last
+    assert early >= last and len(later) >= chunks - early + last
     for n in range(chunks_in):
         finish_sum(n)
     token_copy.wait()

time: 334 us -> 311 us (0.931)
  Pallas kernels: 263 us -> 240 us
    pallas_call x1, Pallas kernels: 178 us -> 155 us  [backward_sum(): pl.pallas_call(backward_sum_kernel, in_specs=[vmem] * 16 + [anywhere] * 4...]
where the time goes in v7:
time: 311 us; the launch traced here: 306 us
  Pallas kernels  240 us (77%)
  matrix products  46 us (15%)
  other arithmetic  11.7 us (4%)
  local copies, waits for them, and re-layouts  5.74 us (2%)
    pallas_call x1, Pallas kernels, backward_sum(): pl.pallas_call(backward_sum_kernel, in_specs=[vmem] * 16 + [anywhere] * 4...  155 us
    pallas_call x1, Pallas kernels, front(): pl.pallas_call(front_kernel, in_specs=[vmem] * (4 + count), out_specs=[vm...  85.1 us
    dot_general x22, matrix products, dot(): lax.dot_general(left, right, (((left_dim,), (right_dim,)), ((), ())), pre...  46 us
  transfers between devices with their start and end apart: 1, of which 0 were waited for; matrix products, arithmetic and copies ran while one was open for 8% of the time, Pallas kernels for 0%

profile of v7, /device:TPU:0, one launch (start us, length us, event | category | flops | bytes accessed | tf_op | source)
XLA Modules:
  0.0 306.2 jit_solution(11097097962196761357)
XLA Ops:
  3.8 85.1 %front.1 = (bf16[960,512]{1,0:T(8,128)(2,1)}, bf16[960,512]{1,0:T(8,128)(2,1)}, bf16[960,512]{1,0:T(8,128)(2,1)}, bf16[960,512]{1,0:T(8,128)(2,1)}, bf16[15,64,5...) custom-call(bf16[2,960,256]{2,1,0:T(8,128)(2,1)} %bitcast.112, ...), custom_call_target="tpu_custom_call" | custom-call | flops 16106127360 | bytes 4915200 | tf_op jit(solution)/shard_map/front/pallas_call | solution.py:1155
  90.1 3.5 %multiply_reduce_fusion.2 = (f32[512]{0:T(512)S(1)}, f32[512,960]{0,1:T(8,128)S(1)}) fusion(bf16[960,512]{1,0:T(8,128)(2,1)} %bitcast.123, bf16[960,960]{1,0:T(8,128)(2,1)} %bitcast.115, bf16[960,512]{1,0:T(8,128)(2,1)} %get-tuple-element.45), kind=kOutput, calls=%fused_computation.25 | convolution fusion | flops 945683968 | bytes 5777408 | tf_op jit(solution)/shard_map/dot_general | solution.py:23
  96.6 1.6 fusion.10
  98.5 1.6 fusion.9
  100.2 2.5 multiply_convert_fusion
  102.7 1.5 fusion.11
  104.2 1.5 add_convert_fusion.3
  105.7 1.6 collective-permute-start
  107.2 1.6 fusion.7
  108.8 2.0 fusion.6
  110.8 2.5 multiply_convert_fusion.1
  113.3 1.4 fusion.12
  116.2 2.9 add_convert_fusion.1
  120.6 2.9 add_convert_fusion
  123.5 2.9 add_convert_fusion.2
  126.4 1.5 fusion.8
  127.9 2.4 convolution_convert_fusion.1.feed_ref
  130.3 2.9 fusion.3.base_ref
  133.2 2.1 multiply_reduce_fusion
  136.0 2.2 convolution_convert_fusion.2
  138.1 2.5 convolution_convert_fusion
  141.6 155.0 %backward_sum.1 = (bf16[3,240,1280]{2,1,0:T(8,128)(2,1)}, bf16[2,960,256]{2,1,0:T(8,128)(2,1)}, bf16[2,960,256]{2,1,0:T(8,128)(2,1)}, bf16[256,960]{1,0:T(8,128)...) custom-call(bf16[15,64,512]{2,1,0:T(8,128)(2,1)} %get-tuple-element.34.query_ref, ...), custom_call_target="tpu_custom_call" | custom-call | flops 40265318400 | bytes 4915200 | tf_op jit(solution)/shard_map/backward_sum/pallas_call | solution.py:832
  296.7 2.7 convert_bitcast_fusion.1
  303.2 1.9 bitcast_convert_fusion
  (53 shorter events, 16.9 us)
Async XLA Ops:
  90.0 3.5 %copy-start.3 = (bf16[960,512]{1,0:T(8,128)(2,1)S(1)}, bf16[960,512]{1,0:T(8,128)(2,1)}, u32[]{:S(2)}) copy-start(bf16[960,512]{1,0:T(8,128)(2,1)} %get-tuple-element.38.tokens_ref) | copy-start | bytes 2949124
  90.1 3.5 %copy-start.13 = (bf16[4,240,960]{2,1,0:T(8,128)(2,1)S(1)}, bf16[4,240,960]{2,1,0:T(8,128)(2,1)}, u32[]{:S(2)}) copy-start(bf16[4,240,960]{2,1,0:T(8,128)(2,1)} %get-tuple-element.36) | copy-start | bytes 5529604
  90.1 3.5 %copy-start.14 = (bf16[15,64,512]{2,1,0:T(8,128)(2,1)S(1)}, bf16[15,64,512]{2,1,0:T(8,128)(2,1)}, u32[]{:S(2)}) copy-start(bf16[15,64,512]{2,1,0:T(8,128)(2,1)} %get-tuple-element.39.mixed_ref) | copy-start | bytes 2949124
  94.9 1.7 copy-start.1
  96.6 1.7 copy-start
  96.6 1.9 copy-start.4
  98.5 1.7 copy-start.5
  105.7 27.6 %collective-permute-start = (bf16[512,960]{0,1:T(8,128)(2,1)S(1)}, bf16[512,960]{0,1:T(8,128)(2,1)S(1)}, u32[]{:S(2)}, u32[]{:S(2)}) collective-permute-start(bf16[512,960]{0,1:T(8,128)(2,1)S(1)} %add_convert_fusion.3), channel_id=1, source_target_pairs={{0,1},{1,0},{2,3},{3,2},{4,5},{5,4},{6,7},{7,6},{8,9},{9,8},{10,11... | collective-permute-start | bytes 2949128 | tf_op jit(solution)/shard_map/ppermute | solution.py:1356
  107.2 1.6 copy-start.2
  136.0 2.2 copy-start.6
  296.7 2.7 copy-start.12
  296.7 3.5 %copy-start.10 = (bf16[256,960]{1,0:T(8,128)(2,1)S(1)}, bf16[256,960]{1,0:T(8,128)(2,1)}, u32[]{:S(2)}) copy-start(bf16[256,960]{1,0:T(8,128)(2,1)} %get-tuple-element.54) | copy-start | bytes 1474564
  296.7 4.5 %copy-start.11 = (bf16[256,640]{1,0:T(8,128)(2,1)S(1)}, bf16[256,640]{1,0:T(8,128)(2,1)}, u32[]{:S(2)}) copy-start(bf16[256,640]{1,0:T(8,128)(2,1)} %get-tuple-element.55) | copy-start | bytes 983044
  299.4 2.7 copy-start.9
  300.2 3.0 copy-start.7
  303.2 1.9 copy-start.8

commit v8 on v7

--- a/solution.py
+++ b/solution.py
@@ -299,8 +299,8 @@
 
 def backward_sum_kernel(
     query_ref, keyval_ref, back_ref, mixed_ref, lse_ref, cosine_ref, sine_ref,
-    base_ref, feed_ref, tokens_ref, normed_ref, middle_ref, gains_ref, gain_two_ref,
-    full_query, full_keyval, down_ref, gate_ref, up_ref, out_ref,
+    base_ref, feed_ref, normed_ref, gains_ref, gain_two_ref,
+    down_ref, gate_ref, up_ref, out_ref, tokens_far, middle_far, query_far, keyval_far,
     share_ref, result_ref, back_tokens_ref, *refs,
 ):
     chunks_in = 4
@@ -313,6 +313,7 @@
     own_sem, mate_send, mate_recv, y_send, y_recv, up_send, up_recv, down_send, down_recv,
     part_send, part_recv, feed_in, traded, feed_send, feed_recv, trade_send, trade_recv,
     back_query_ref, back_keyval_ref, back_one, token_traded,
+    tokens_ref, middle_ref, full_query, full_keyval, far_sem,
     whole_sem, sum_mate_send, sum_mate_recv, sum_y_send, sum_y_recv, sum_x_send, sum_x_recv,
     sum_z_send, sum_z_recv, all_send, all_recv, back_send, back_recv, token_send, token_recv,
     ) = refs[5 * chunks_in :]
@@ -340,6 +341,13 @@
     greet(fsdp=mate)
     greet(fsdp=across)
     greet(tp=1 - side)
+    far = [
+        pltpu.make_async_copy(source, target, far_sem.at[i])
+        for i, (source, target) in enumerate((
+            (tokens_far, tokens_ref), (middle_far, middle_ref), (query_far, full_query),
+            (keyval_far, full_keyval),
+        ))
+    ]
     for d in range(1, blocks):
         greet(ctx=lax.rem(place + d, blocks))
     filled = out_ref.shape[1]
@@ -481,6 +489,8 @@
     )
 
     def input_gradient():
+        for copy in far:
+            copy.wait()
         tokens = wide(tokens_ref[...])
         inverse = lax.rsqrt(jnp.mean(tokens * tokens, 0, keepdims=True) + EPS)
 
@@ -515,7 +525,6 @@
             return carry
 
         lax.fori_loop(0, whole[0].shape[0], rows_back, 0)
-        token_copy.start()
 
     def chunk_at(ref, m, r, *front):
         return ref.at[(m,) + front + (pl.ds(r * CHUNK_ROWS, CHUNK_ROWS),)]
@@ -537,6 +546,8 @@
             out_ref.at[f], whole[0].at[f, pl.ds(0, filled)], whole_sem.at[f]
         ).wait()
     to_mate(0)
+    for copy in far:
+        copy.start()
     for m, gradient in enumerate(gradients):
         for half in range(2):
             pltpu.make_async_copy(
@@ -750,14 +761,17 @@
     assert iterations * blocks > 4 + 2 * last + 2 * (chunks - 1)
     lax.fori_loop(0, iterations, head_loop, 0)
 
+    def start_tokens(n):
+        token_copy.start()
+
     def keyval_gradient(n):
         weight_gradient(n, back_keyval_ref)
         to_mate(n)
 
     later = (
         ((keyval_gradient, 2), (to_y, 2)), ((to_all, 1),), ((lambda n: input_gradient(), 3),),
-        ((to_x, 2), (to_back, 1)), ((to_y, 3),), ((to_z, 2), (to_x, 3)), ((to_all, 2), (to_z, 3)),
-        ((to_back, 2), (to_all, 3)), ((to_back, 3),),
+        ((to_y, 3), (to_x, 2), (to_back, 1)), ((to_x, 3), (to_z, 2), (start_tokens, 3)),
+        ((to_all, 2), (to_z, 3)), ((to_back, 2), (to_all, 3)), ((to_back, 3),),
     )
     for slot, stages in enumerate(later):
         for stage, n in stages:
@@ -831,7 +845,7 @@
     pairs = jax.ShapeDtypeStruct((2, features, positions // 2), low_type)
     return pl.pallas_call(
         backward_sum_kernel,
-        in_specs=[vmem] * 16 + [anywhere] * 4,
+        in_specs=[vmem] * 12 + [anywhere] * 8,
         out_specs=[vmem] * (3 + each),
         out_shape=[jax.ShapeDtypeStruct(share, low_type), pairs, pairs] + [
             jax.ShapeDtypeStruct((padded, w), low_type) for w in widths
@@ -858,6 +872,11 @@
             pltpu.VMEM((2 * KEY_WIDTH, positions), low_type),
             pltpu.VMEM((features, positions), jnp.float32),
             pltpu.VMEM((features, positions // 2), low_type),
+            pltpu.VMEM(tokens.shape, low_type),
+            pltpu.VMEM(middle.shape, jnp.float32),
+            pltpu.VMEM(full_query.shape, low_type),
+            pltpu.VMEM(full_keyval.shape, low_type),
+            dma((4,)),
             dma((count,)),
             dma((each, 2)), dma((each, 2)),
             dma((each,)), dma((each,)),
@@ -875,8 +894,8 @@
         ),
         name="backward_sum",
     )(
-        query, keyval, back_mixed, mixed, lse, cosine, sine, base, feed, tokens, normed, middle,
-        gains, gain_two, full_query, full_keyval, *gradients, gradient_out,
+        query, keyval, back_mixed, mixed, lse, cosine, sine, base, feed, normed, gains, gain_two,
+        *gradients, gradient_out, tokens, middle, full_query, full_keyval,
     )
 
 
@@ -989,8 +1008,9 @@
         y_copy(w).start()
         mate_copy(w).start()
     token_copy.start()
-    y_copy(0).start()
-    mate_copy(0).start()
+    for w in (0, 2, 3, 4, 5):
+        y_copy(w).start()
+        mate_copy(w).start()
     y_copy(6).wait_recv()
     pass_copy(6).start()
     arrived(6)
@@ -1011,9 +1031,6 @@
     for w in (1, 0):
         y_copy(w).wait_recv()
         pass_copy(w).start()
-    for w in range(2, 6):
-        y_copy(w).start()
-        mate_copy(w).start()
     normed = normed_out[...]
     cosine, sine = cosine_ref[...], sine_ref[...]
 

time: 311 us -> 310 us (level)
  transfers between devices with their start and end apart: 1 -> 1, of which waited for: 0 -> 0; matrix products, arithmetic and copies ran while one was open for 8% -> 9% of each run, Pallas kernels for 0% -> 0%
where the time goes in v8:
time: 310 us; the launch traced here: 305 us
  Pallas kernels  239 us (77%)
  matrix products  46.1 us (15%)
  other arithmetic  11.7 us (4%)
  local copies, waits for them, and re-layouts  5.74 us (2%)
    pallas_call x1, Pallas kernels, backward_sum(): pl.pallas_call(backward_sum_kernel, in_specs=[vmem] * 12 + [anywhere] * 8...  154 us
    pallas_call x1, Pallas kernels, front(): pl.pallas_call(front_kernel, in_specs=[vmem] * (4 + count), out_specs=[vm...  84.8 us
    dot_general x22, matrix products, dot(): lax.dot_general(left, right, (((left_dim,), (right_dim,)), ((), ())), pre...  46.1 us
  transfers between devices with their start and end apart: 1, of which 0 were waited for; matrix products, arithmetic and copies ran while one was open for 9% of the time, Pallas kernels for 0%

profile of v8, /device:TPU:0, one launch (start us, length us, event | category | flops | bytes accessed | tf_op | source)
XLA Modules:
  0.0 305.2 jit_solution(4760117187293582471)
XLA Ops:
  3.8 84.8 %front.1 = (bf16[960,512]{1,0:T(8,128)(2,1)}, bf16[960,512]{1,0:T(8,128)(2,1)}, bf16[960,512]{1,0:T(8,128)(2,1)}, bf16[960,512]{1,0:T(8,128)(2,1)}, bf16[15,64,5...) custom-call(bf16[2,960,256]{2,1,0:T(8,128)(2,1)} %bitcast.112, ...), custom_call_target="tpu_custom_call" | custom-call | flops 16106127360 | bytes 4915200 | tf_op jit(solution)/shard_map/front/pallas_call | solution.py:1172
  89.8 3.5 %multiply_reduce_fusion.2 = (f32[512]{0:T(512)S(1)}, f32[512,960]{0,1:T(8,128)S(1)}) fusion(bf16[960,512]{1,0:T(8,128)(2,1)} %bitcast.123, bf16[960,960]{1,0:T(8,128)(2,1)} %bitcast.115, bf16[960,512]{1,0:T(8,128)(2,1)} %get-tuple-element.45), kind=kOutput, calls=%fused_computation.25 | convolution fusion | flops 945683968 | bytes 5777408 | tf_op jit(solution)/shard_map/dot_general | solution.py:23
  96.3 1.6 fusion.10
  98.2 1.6 fusion.9
  99.9 2.5 multiply_convert_fusion
  102.4 1.5 fusion.11
  103.9 1.5 add_convert_fusion.3
  105.4 1.5 collective-permute-start
  106.9 1.6 fusion.7
  108.5 2.0 fusion.6
  110.5 2.5 multiply_convert_fusion.1
  113.0 1.4 fusion.12
  115.9 2.9 add_convert_fusion.1
  120.3 2.9 add_convert_fusion
  123.2 2.9 add_convert_fusion.2
  126.1 1.5 fusion.8
  127.6 2.4 convolution_convert_fusion.1.feed_ref
  130.0 2.9 fusion.3.base_ref
  132.9 2.1 multiply_reduce_fusion
  135.7 2.2 convolution_convert_fusion.2
  137.8 2.6 convolution_convert_fusion
  141.4 154.2 %backward_sum.1 = (bf16[3,240,1280]{2,1,0:T(8,128)(2,1)}, bf16[2,960,256]{2,1,0:T(8,128)(2,1)}, bf16[2,960,256]{2,1,0:T(8,128)(2,1)}, bf16[256,960]{1,0:T(8,128)...) custom-call(bf16[15,64,512]{2,1,0:T(8,128)(2,1)} %get-tuple-element.34.query_ref, ...), custom_call_target="tpu_custom_call" | custom-call | flops 40265318400 | bytes 4915200 | tf_op jit(solution)/shard_map/backward_sum/pallas_call | solution.py:846
  295.7 2.7 convert_bitcast_fusion.1
  302.2 1.9 bitcast_convert_fusion
  (53 shorter events, 16.9 us)
Async XLA Ops:
  89.7 3.5 %copy-start.3 = (bf16[960,512]{1,0:T(8,128)(2,1)S(1)}, bf16[960,512]{1,0:T(8,128)(2,1)}, u32[]{:S(2)}) copy-start(bf16[960,512]{1,0:T(8,128)(2,1)} %get-tuple-element.38.tokens_far) | copy-start | bytes 2949124
  89.8 3.5 %copy-start.13 = (bf16[4,240,960]{2,1,0:T(8,128)(2,1)S(1)}, bf16[4,240,960]{2,1,0:T(8,128)(2,1)}, u32[]{:S(2)}) copy-start(bf16[4,240,960]{2,1,0:T(8,128)(2,1)} %get-tuple-element.36) | copy-start | bytes 5529604
  89.8 3.5 %copy-start.14 = (bf16[15,64,512]{2,1,0:T(8,128)(2,1)S(1)}, bf16[15,64,512]{2,1,0:T(8,128)(2,1)}, u32[]{:S(2)}) copy-start(bf16[15,64,512]{2,1,0:T(8,128)(2,1)} %get-tuple-element.39.mixed_ref) | copy-start | bytes 2949124
  94.6 1.7 copy-start.1
  96.3 1.7 copy-start
  96.3 1.9 copy-start.4
  98.2 1.7 copy-start.5
  105.4 27.6 %collective-permute-start = (bf16[512,960]{0,1:T(8,128)(2,1)S(1)}, bf16[512,960]{0,1:T(8,128)(2,1)S(1)}, u32[]{:S(2)}, u32[]{:S(2)}) collective-permute-start(bf16[512,960]{0,1:T(8,128)(2,1)S(1)} %add_convert_fusion.3), channel_id=1, source_target_pairs={{0,1},{1,0},{2,3},{3,2},{4,5},{5,4},{6,7},{7,6},{8,9},{9,8},{10,11... | collective-permute-start | bytes 2949128 | tf_op jit(solution)/shard_map/ppermute | solution.py:1373
  106.9 1.6 copy-start.2
  135.7 2.2 copy-start.6
  295.7 2.7 copy-start.12
  295.7 3.5 %copy-start.10 = (bf16[256,960]{1,0:T(8,128)(2,1)S(1)}, bf16[256,960]{1,0:T(8,128)(2,1)}, u32[]{:S(2)}) copy-start(bf16[256,960]{1,0:T(8,128)(2,1)} %get-tuple-element.54) | copy-start | bytes 1474564
  295.7 4.5 %copy-start.11 = (bf16[256,640]{1,0:T(8,128)(2,1)S(1)}, bf16[256,640]{1,0:T(8,128)(2,1)}, u32[]{:S(2)}) copy-start(bf16[256,640]{1,0:T(8,128)(2,1)} %get-tuple-element.55) | copy-start | bytes 983044
  298.4 2.7 copy-start.9
  299.2 3.0 copy-start.7
  302.2 1.9 copy-start.8

commit v9 on v8

--- a/solution.py
+++ b/solution.py
@@ -331,7 +331,7 @@
     per = rows // CHUNK_ROWS
     chunks = len(gradients) * per
     iterations = KEYVAL_HEADS + 2
-    early = iterations * blocks // 2 - KEYVAL_HEADS * blocks // 2
+    early = (iterations - KEYVAL_HEADS) * blocks
 
     for m, gradient in enumerate(gradients):
         for half in range(2):
@@ -644,9 +644,9 @@
 
         c = t - KEYVAL_HEADS * blocks - 2 * (last - place)
 
-        @pl.when((c >= 0) & (c < 2 * chunks) & (lax.rem(c, 2) == 0))
-        def _():
-            give_back(c // 2)
+        @pl.when((c >= 0) & (c < chunks))
+        def _():
+            give_back(c)
 
         for at, stage, n in (
             (4, to_y, 0), (15, to_x, 0), (18, to_z, 0), (20, query_gradient, 1),
@@ -769,20 +769,20 @@
         to_mate(n)
 
     later = (
-        ((keyval_gradient, 2), (to_y, 2)), ((to_all, 1),), ((lambda n: input_gradient(), 3),),
-        ((to_y, 3), (to_x, 2), (to_back, 1)), ((to_x, 3), (to_z, 2), (start_tokens, 3)),
-        ((to_all, 2), (to_z, 3)), ((to_back, 2), (to_all, 3)), ((to_back, 3),),
+        ((keyval_gradient, 2), (to_y, 2)), ((lambda n: input_gradient(), 3),),
+        ((to_y, 3), (to_x, 2), (to_all, 1)), ((to_x, 3), (to_z, 2), (start_tokens, 3)),
+        ((to_all, 2), (to_z, 3), (to_back, 1)), ((to_back, 2), (to_all, 3)), ((to_back, 3),),
     )
     for slot, stages in enumerate(later):
         for stage, n in stages:
             stage(n)
         for index in range(blocks):
-            if early + slot - last + index < chunks:
+            if early + slot - 2 * (last - index) < chunks:
                 @pl.when(place == index)
-                def _(k=early + slot - last + index):
+                def _(k=early + slot - 2 * (last - index)):
                     give_back(k)
 
-    assert early >= last and len(later) >= chunks - early + last
+    assert early >= 2 * last and len(later) >= chunks - early + 2 * last
     for n in range(chunks_in):
         finish_sum(n)
     token_copy.wait()

time: 310 us -> 313 us (level)
    pallas_call x1, Pallas kernels: 154 us -> 158 us  [backward_sum(): pl.pallas_call(backward_sum_kernel, in_specs=[vmem] * 12 + [anywhere] * 8...]
  transfers between devices with their start and end apart: 1 -> 1, of which waited for: 0 -> 0; matrix products, arithmetic and copies ran while one was open for 9% -> 8% of each run, Pallas kernels for 0% -> 0%
where the time goes in v9:
time: 313 us; the launch traced here: 309 us
  Pallas kernels  242 us (77%)
  matrix products  46.1 us (15%)
  other arithmetic  11.7 us (4%)
  local copies, waits for them, and re-layouts  5.74 us (2%)
    pallas_call x1, Pallas kernels, backward_sum(): pl.pallas_call(backward_sum_kernel, in_specs=[vmem] * 12 + [anywhere] * 8...  158 us
    pallas_call x1, Pallas kernels, front(): pl.pallas_call(front_kernel, in_specs=[vmem] * (4 + count), out_specs=[vm...  84.8 us
    dot_general x22, matrix products, dot(): lax.dot_general(left, right, (((left_dim,), (right_dim,)), ((), ())), pre...  46.1 us
  transfers between devices with their start and end apart: 1, of which 0 were waited for; matrix products, arithmetic and copies ran while one was open for 8% of the time, Pallas kernels for 0%

profile of v9, /device:TPU:0, one launch (start us, length us, event | category | flops | bytes accessed | tf_op | source)
XLA Modules:
  0.0 308.6 jit_solution(2226769333081362852)
XLA Ops:
  3.8 84.8 %front.1 = (bf16[960,512]{1,0:T(8,128)(2,1)}, bf16[960,512]{1,0:T(8,128)(2,1)}, bf16[960,512]{1,0:T(8,128)(2,1)}, bf16[960,512]{1,0:T(8,128)(2,1)}, bf16[15,64,5...) custom-call(bf16[2,960,256]{2,1,0:T(8,128)(2,1)} %bitcast.112, ...), custom_call_target="tpu_custom_call" | custom-call | flops 16106127360 | bytes 4915200 | tf_op jit(solution)/shard_map/front/pallas_call | solution.py:1172
  89.8 3.5 %multiply_reduce_fusion.2 = (f32[512]{0:T(512)S(1)}, f32[512,960]{0,1:T(8,128)S(1)}) fusion(bf16[960,512]{1,0:T(8,128)(2,1)} %bitcast.123, bf16[960,960]{1,0:T(8,128)(2,1)} %bitcast.115, bf16[960,512]{1,0:T(8,128)(2,1)} %get-tuple-element.45), kind=kOutput, calls=%fused_computation.25 | convolution fusion | flops 945683968 | bytes 5777408 | tf_op jit(solution)/shard_map/dot_general | solution.py:23
  96.3 1.6 fusion.10
  98.2 1.6 fusion.9
  99.9 2.5 multiply_convert_fusion
  102.4 1.5 fusion.11
  103.9 1.5 add_convert_fusion.3
  105.4 1.5 collective-permute-start
  106.9 1.6 fusion.7
  108.5 2.0 fusion.6
  110.5 2.5 multiply_convert_fusion.1
  113.0 1.4 fusion.12
  115.9 2.9 add_convert_fusion.1
  120.3 2.9 add_convert_fusion
  123.2 2.9 add_convert_fusion.2
  126.1 1.5 fusion.8
  127.6 2.4 convolution_convert_fusion.1.feed_ref
  130.0 2.9 fusion.3.base_ref
  132.9 2.1 multiply_reduce_fusion
  135.7 2.2 convolution_convert_fusion.2
  137.8 2.6 convolution_convert_fusion
  141.4 157.6 %backward_sum.1 = (bf16[3,240,1280]{2,1,0:T(8,128)(2,1)}, bf16[2,960,256]{2,1,0:T(8,128)(2,1)}, bf16[2,960,256]{2,1,0:T(8,128)(2,1)}, bf16[256,960]{1,0:T(8,128)...) custom-call(bf16[15,64,512]{2,1,0:T(8,128)(2,1)} %get-tuple-element.34.query_ref, ...), custom_call_target="tpu_custom_call" | custom-call | flops 40265318400 | bytes 4915200 | tf_op jit(solution)/shard_map/backward_sum/pallas_call | solution.py:846
  299.0 2.7 convert_bitcast_fusion.1
  305.5 1.9 bitcast_convert_fusion
  (53 shorter events, 16.9 us)
Async XLA Ops:
  89.7 3.5 %copy-start.3 = (bf16[960,512]{1,0:T(8,128)(2,1)S(1)}, bf16[960,512]{1,0:T(8,128)(2,1)}, u32[]{:S(2)}) copy-start(bf16[960,512]{1,0:T(8,128)(2,1)} %get-tuple-element.38.tokens_far) | copy-start | bytes 2949124
  89.8 3.5 %copy-start.13 = (bf16[4,240,960]{2,1,0:T(8,128)(2,1)S(1)}, bf16[4,240,960]{2,1,0:T(8,128)(2,1)}, u32[]{:S(2)}) copy-start(bf16[4,240,960]{2,1,0:T(8,128)(2,1)} %get-tuple-element.36) | copy-start | bytes 5529604
  89.8 3.5 %copy-start.14 = (bf16[15,64,512]{2,1,0:T(8,128)(2,1)S(1)}, bf16[15,64,512]{2,1,0:T(8,128)(2,1)}, u32[]{:S(2)}) copy-start(bf16[15,64,512]{2,1,0:T(8,128)(2,1)} %get-tuple-element.39.mixed_ref) | copy-start | bytes 2949124
  94.6 1.7 copy-start.1
  96.3 1.7 copy-start
  96.3 1.9 copy-start.4
  98.2 1.7 copy-start.5
  105.4 27.6 %collective-permute-start = (bf16[512,960]{0,1:T(8,128)(2,1)S(1)}, bf16[512,960]{0,1:T(8,128)(2,1)S(1)}, u32[]{:S(2)}, u32[]{:S(2)}) collective-permute-start(bf16[512,960]{0,1:T(8,128)(2,1)S(1)} %add_convert_fusion.3), channel_id=1, source_target_pairs={{0,1},{1,0},{2,3},{3,2},{4,5},{5,4},{6,7},{7,6},{8,9},{9,8},{10,11... | collective-permute-start | bytes 2949128 | tf_op jit(solution)/shard_map/ppermute | solution.py:1373
  106.9 1.6 copy-start.2
  135.7 2.2 copy-start.6
  299.0 2.7 copy-start.12
  299.0 3.5 %copy-start.10 = (bf16[256,960]{1,0:T(8,128)(2,1)S(1)}, bf16[256,960]{1,0:T(8,128)(2,1)}, u32[]{:S(2)}) copy-start(bf16[256,960]{1,0:T(8,128)(2,1)} %get-tuple-element.54) | copy-start | bytes 1474564
  299.0 4.5 %copy-start.11 = (bf16[256,640]{1,0:T(8,128)(2,1)S(1)}, bf16[256,640]{1,0:T(8,128)(2,1)}, u32[]{:S(2)}) copy-start(bf16[256,640]{1,0:T(8,128)(2,1)} %get-tuple-element.55) | copy-start | bytes 983044
  301.8 2.7 copy-start.9
  302.5 3.0 copy-start.7
  305.5 1.9 copy-start.8
